TPU v7x, 256 devices: a whole 4x4x8 slice. The times are simulated.
256 devices in a mesh: seq: 8 (over x, core), head: 32 (over y, z).
Axes of the slice: x: 4, y: 4, z: 8, core: 2. Of those that a mesh axis runs over, the one named last changes fastest.
Arguments:
- x_inner: bfloat16 [4096, 16384], P('seq', 'head'), may hold values from -6 to 6
- bc_proj: bfloat16 [4096, 4096], P('seq'), may hold values from -6 to 6
- z_gate: bfloat16 [4096, 16384], P('seq', 'head'), may hold values from -6 to 6
- dt_step: float32 [256, 4096], P('head', 'seq'), may hold values from 0.5 to 2
- decay_rate: float32 [256], P('head'), may hold values from 0 to 0.04, as said below
- conv_x_w: bfloat16 [4, 16384], P(None, 'head'), may hold values from -3 to 3
- conv_bc_w: bfloat16 [4, 4096], replicated, may hold values from -3 to 3
- norm_gain: float32 [16384], P('head'), may hold values from 0.5 to 1.5
- out_proj: bfloat16 [16384, 8192], P('head'), may hold values from -0.046875 to 0.046875
Outputs:
- layer_out: bfloat16 [8192, 4096], P('head', 'seq')
Inputs may be any that keep to these rules, and one draw needn't show every extreme that they name: `decay_rate`: every rate is positive.
All inputs are finite; a program needn't handle non-finite values.
Results may differ from a plain program's by a relative error of at most 0.025.
Values may be sent and summed in bfloat16 or wider, within the bound.
No kernel may reach another device: no remote copies, remote signals or barrier semaphores. Data moves between devices by JAX's collectives and lax.ppermute only.
A program may use at most 64 MiB of HBM per device.

v0:
```python
import jax
import jax.numpy as jnp
from jax import lax
from jax.sharding import PartitionSpec as P

HEADS = 256
GROUPS = 8
SPAN = 256


norm_eps = 1e-05


def shifted(block, axis, distance):
    devices = range(lax.axis_size(axis))
    route = [(i - distance, i) for i in devices if i - distance in devices]
    return lax.ppermute(block, axis, route)


def causal(extended, weight, tok_rows):
    running = jnp.zeros((tok_rows, extended.shape[1]), jnp.float32)
    for tap_idx in range(weight.shape[0]):
        running = running + weight[tap_idx].astype(jnp.float32)[None, :] * extended[
            tap_idx : tap_idx + tok_rows
        ].astype(jnp.float32)
    return jax.nn.silu(running).astype(jnp.bfloat16)


def normalize(gated, squares, picker, group_width, norm_gain):
    mean_sq = jnp.dot(squares, picker) / group_width
    return (gated * lax.rsqrt(mean_sq + norm_eps)[:, None] * norm_gain[None, :]).astype(
        jnp.bfloat16
    )


def project_term(out_proj, normed):
    return lax.dot_general(
        out_proj, normed, (((0,), (1,)), ((), ())), preferred_element_type=jnp.float32
    )


def on_device(
    x_inner, bc_proj, z_gate, dt_step, decay_rate, conv_x_w, conv_bc_w, norm_gain, out_proj
):
    tok_rows = x_inner.shape[0]
    head_count = decay_rate.shape[0]
    head_width = x_inner.shape[1] // head_count
    group_cols = bc_proj.shape[1] // GROUPS
    state_size = group_cols // 2
    group_heads = HEADS // GROUPS
    my_group = lax.axis_index("head") * head_count // group_heads
    bc_mine = lax.dynamic_slice_in_dim(bc_proj, my_group * group_cols, group_cols, 1)
    conv_mine = lax.dynamic_slice_in_dim(conv_bc_w, my_group * group_cols, group_cols, 1)
    rim_rows = conv_x_w.shape[0] - 1
    rim_x, rim_bc = shifted(
        (x_inner[tok_rows - rim_rows :], bc_mine[tok_rows - rim_rows :]), "seq", 1
    )
    x_conv = causal(jnp.concatenate([rim_x, x_inner], 0), conv_x_w, tok_rows)
    bc_conv = causal(jnp.concatenate([rim_bc, bc_mine], 0), conv_mine, tok_rows)
    n_spans = tok_rows // SPAN
    x_spans = x_conv.reshape(n_spans, SPAN, head_count, head_width)
    b_part = bc_conv[:, :state_size].reshape(n_spans, SPAN, state_size)
    c_part = bc_conv[:, state_size:].reshape(n_spans, SPAN, state_size)
    dt_spans = dt_step.reshape(head_count, n_spans, SPAN)
    cum_log = jnp.cumsum(-decay_rate[:, None, None] * dt_spans, axis=2)
    scores = jnp.einsum("cqn,ckn->cqk", c_part, b_part, preferred_element_type=jnp.float32)
    causal_mask = jnp.arange(SPAN)[:, None] >= jnp.arange(SPAN)[None, :]
    gap_log = cum_log[:, :, :, None] - cum_log[:, :, None, :]
    decay_mask = jnp.where(causal_mask, jnp.exp(jnp.where(causal_mask, gap_log, 0.0)), 0.0)
    weights = (scores[None] * decay_mask * dt_spans[:, :, None, :]).astype(jnp.bfloat16)
    y_diag = jnp.einsum("hcqk,ckhp->cqhp", weights, x_spans, preferred_element_type=jnp.float32)
    tail_decay = jnp.exp(cum_log[:, :, -1:] - cum_log) * dt_spans
    weighted_b = (tail_decay[..., None] * b_part[None].astype(jnp.float32)).astype(jnp.bfloat16)
    local_states = jnp.einsum(
        "hcqn,cqhp->hcpn", weighted_b, x_spans, preferred_element_type=jnp.float32
    )
    totals = cum_log[:, :, -1]

    def advance(running, span_in):
        span_state, log_total = span_in
        return (jnp.exp(log_total)[:, None, None] * running + span_state, running)

    zero_state = jnp.zeros((head_count, head_width, state_size), jnp.float32)
    end_state, start_local = lax.scan(
        advance, zero_state, (jnp.moveaxis(local_states, 1, 0), totals.T)
    )
    device_log = jnp.sum(totals, axis=1)
    prior_log = jnp.cumsum(totals, axis=1) - totals
    incoming = zero_state
    for relay_step in range(lax.axis_size("seq") - 1):
        incoming = shifted(
            (jnp.exp(device_log)[:, None, None] * incoming + end_state).astype(jnp.bfloat16),
            "seq",
            1,
        ).astype(jnp.float32)
    start_full = jnp.exp(prior_log).T[:, :, None, None] * incoming[None] + start_local
    carried = jnp.einsum(
        "cqn,chpn->cqhp", c_part.astype(jnp.float32), start_full, precision=lax.Precision.HIGHEST
    )
    y_off = jnp.transpose(jnp.exp(cum_log), (1, 2, 0))[..., None] * carried
    y_all = (y_diag + y_off).reshape(tok_rows, head_count * head_width)
    gated = y_all * jax.nn.silu(z_gate.astype(jnp.float32))
    picker = (jnp.arange(GROUPS) == my_group).astype(jnp.float32)
    group_width = group_heads * head_width
    row_squares = jnp.sum(gated * gated, axis=1)[:, None] * picker[None, :]
    squares = lax.psum(row_squares, "head")
    normed = normalize(gated, squares, picker, group_width, norm_gain)
    return lax.psum_scatter(
        project_term(out_proj, normed).astype(jnp.bfloat16), "head", scatter_dimension=0, tiled=True
    )


def solution(mesh):
    placed = (
        P("seq", "head"),
        P("seq", None),
        P("seq", "head"),
        P("head", "seq"),
        P("head"),
        P(None, "head"),
        P(),
        P("head"),
        P("head", None),
    )
    return jax.shard_map(
        on_device, mesh=mesh, in_specs=placed, out_specs=P("head", "seq"), check_vma=False
    )
```

profile of v0, /device:TPU:4, one launch (start us, length us, event | category | flops | bytes accessed | tf_op | source)
XLA Modules:
  0.0 477.3 jit_solution(7292520768222637486)
XLA Ops:
  7.4 1.9 collective-permute-start
  9.4 1.1 constant_dynamic-slice_fusion.1
  10.8 3.2 collective-permute-start.1
  14.7 0.8 slice_convert_fusion.3
  16.3 1.1 reduce-window.6
  18.8 0.9 dynamic-slice_convert_fusion.3
  19.7 1.3 copy.40
  21.0 1.2 multiply_convert_fusion.9
  22.4 0.8 convert_element_type.133
  23.2 1.2 multiply_convert_fusion.10
  24.4 0.9 reshape.93
  25.4 2.2 fusion.13
  28.1 2.1 collective-permute-start.2
  30.1 5.8 %collective-permute-done.2 = bf16[8,64,256]{2,1,0:T(8,128)(2,1)S(1)} collective-permute-done((bf16[8,64,256]{2,1,0:T(8,128)(2,1)S(1)}, bf16[8,64,256]{2,1,0:T(8,128)(2,1)S(1)}, u32[]{:S(2)}, u32[]{:S(2)}) %collective-permute-start.2) | collective-permute-done | bytes 262176 | tf_op jit(solution)/shard_map/ppermute | solution.py:17
  36.0 1.9 collective-permute-start.3
  38.0 5.8 %collective-permute-done.3 = bf16[8,64,256]{2,1,0:T(8,128)(2,1)S(1)} collective-permute-done((bf16[8,64,256]{2,1,0:T(8,128)(2,1)S(1)}, bf16[8,64,256]{2,1,0:T(8,128)(2,1)S(1)}, u32[]{:S(2)}, u32[]{:S(2)}) %collective-permute-start.3) | collective-permute-done | bytes 262176 | tf_op jit(solution)/shard_map/ppermute | solution.py:17
  43.9 1.9 collective-permute-start.4
  45.8 5.8 %collective-permute-done.4 = bf16[8,64,256]{2,1,0:T(8,128)(2,1)S(1)} collective-permute-done((bf16[8,64,256]{2,1,0:T(8,128)(2,1)S(1)}, bf16[8,64,256]{2,1,0:T(8,128)(2,1)S(1)}, u32[]{:S(2)}, u32[]{:S(2)}) %collective-permute-start.4) | collective-permute-done | bytes 262176 | tf_op jit(solution)/shard_map/ppermute | solution.py:17
  51.7 1.9 collective-permute-start.5
  53.6 5.8 %collective-permute-done.5 = bf16[8,64,256]{2,1,0:T(8,128)(2,1)S(1)} collective-permute-done((bf16[8,64,256]{2,1,0:T(8,128)(2,1)S(1)}, bf16[8,64,256]{2,1,0:T(8,128)(2,1)S(1)}, u32[]{:S(2)}, u32[]{:S(2)}) %collective-permute-start.5) | collective-permute-done | bytes 262176 | tf_op jit(solution)/shard_map/ppermute | solution.py:17
  59.5 1.9 collective-permute-start.6
  61.5 5.7 %collective-permute-done.6 = bf16[8,64,256]{2,1,0:T(8,128)(2,1)S(1)} collective-permute-done((bf16[8,64,256]{2,1,0:T(8,128)(2,1)S(1)}, bf16[8,64,256]{2,1,0:T(8,128)(2,1)S(1)}, u32[]{:S(2)}, u32[]{:S(2)}) %collective-permute-start.6) | collective-permute-done | bytes 262176 | tf_op jit(solution)/shard_map/ppermute | solution.py:17
  67.2 0.8 add_convert_fusion.1
  68.0 1.9 collective-permute-start.7
  70.6 5.3 %collective-permute-done.7 = bf16[8,64,256]{2,1,0:T(8,128)(2,1)S(1)} collective-permute-done((bf16[8,64,256]{2,1,0:T(8,128)(2,1)}, bf16[8,64,256]{2,1,0:T(8,128)(2,1)S(1)}, u32[]{:S(2)}, u32[]{:S(2)}) %collective-permute-start.7) | collective-permute-done | bytes 262176 | tf_op jit(solution)/shard_map/ppermute | solution.py:17
  76.1 1.9 collective-permute-start.8
  78.0 2.5 fusion.14
  80.5 3.3 collective-permute-done.8
  86.0 147.4 %psum.7 = bf16[512,8]{1,0:T(8,128)(2,1)S(1)} all-reduce(f32[512,8]{1,0:T(8,128)S(1)} %broadcast_multiply_fusion), channel_id=1, replica_groups=mesh['seq'=8,'head'=32] {'head'}, use_global_device_ids=true, to_apply=%region_7.8 | all-reduce | flops 4096 | bytes 24576 | tf_op jit(solution)/shard_map/psum | solution.py:106
  233.6 10.4 %fusion.2 = bf16[8192,512]{0,1:T(8,128)(2,1)} fusion(bf16[512,8192]{1,0:T(8,128)(2,1)} %param.19, f32[512]{0:T(512)S(1)} %copy-done.2, f32[512]{0:T(512)S(1)} %add_rsqrt_fusion, f32[512,512]{0,1:T(8,128)S(1)} %bitcast.69, bf16[512,512]{0,1:T(8,128)(2,1)S(1)} %copy.54), kind=kOutput, calls=%fused_computation.6 | convolution fusion | flops 4301520896 | bytes 18354176 | tf_op jit(solution)/shard_map/dot_general | solution.py:37
  244.0 224.7 %reduce-scatter.2.cloned.1.call-done = bf16[256,512]{0,1:T(8,128)(2,1)} async-done(((bf16[8192,512]{0,1:T(8,128)(2,1)}), bf16[256,512]{0,1:T(8,128)(2,1)}) %reduce-scatter.2.cloned.1.call-update) | async-done | bytes 262160 | tf_op jit(solution)/shard_map/reduce_scatter | solution.py:108
  468.7 1.8 copy.55
  (58 shorter events, 8.7 us)
Async XLA Ops:
  6.5 462.1 %reduce-scatter.2.cloned.1.call-start = ((), (), s32[]{:S(2)}) async-start(), calls=%async_computation.1 | async-start | bytes 8650752 | tf_op jit(solution)/shard_map/reduce_scatter | solution.py:108
  7.4 15.8 %collective-permute-start = (bf16[3,512]{0,1:T(8,128)(2,1)S(1)}, bf16[3,512]{0,1:T(8,128)(2,1)S(1)}, u32[]{:S(2)}, u32[]{:S(2)}) collective-permute-start(bf16[3,512]{0,1:T(8,128)(2,1)S(1)} %copy.39), channel_id=1, source_target_pairs={{0,32},{32,64},{64,96},{96,128},{128,160},{160,192},{192,224},{1,3... | collective-permute-start | bytes 9224 | tf_op jit(solution)/shard_map/ppermute | solution.py:17
  10.8 10.2 %collective-permute-start.1 = (bf16[3,512]{0,1:T(8,128)(2,1)S(1)}, bf16[3,512]{0,1:T(8,128)(2,1)S(1)}, u32[]{:S(2)}, u32[]{:S(2)}) collective-permute-start(bf16[3,512]{0,1:T(8,128)(2,1)S(1)} %slice.89), channel_id=1, source_target_pairs={{0,32},{32,64},{64,96},{96,128},{128,160},{160,192},{192,224},{1,3... | collective-permute-start | bytes 9224 | tf_op jit(solution)/shard_map/ppermute | solution.py:17
  28.0 42.0 %copy-start = (bf16[512,512]{1,0:T(8,128)(2,1)S(1)}, bf16[512,512]{1,0:T(8,128)(2,1)}, u32[]{:S(2)}) copy-start(bf16[512,512]{1,0:T(8,128)(2,1)} %param.13) | copy-start | bytes 1572868
  28.1 7.8 %collective-permute-start.2 = (bf16[8,64,256]{2,1,0:T(8,128)(2,1)S(1)}, bf16[8,64,256]{2,1,0:T(8,128)(2,1)S(1)}, u32[]{:S(2)}, u32[]{:S(2)}) collective-permute-start(bf16[8,64,256]{2,1,0:T(8,128)(2,1)S(1)} %add_convert_fusion.6), channel_id=1, source_target_pairs={{0,32},{32,64},{64,96},{96,128},{128,160},{160,192},{192,224},{1,3... | collective-permute-start | bytes 786440 | tf_op jit(solution)/shard_map/ppermute | solution.py:17
  36.0 42.0 %copy-start.1 = (f32[8,512]{1,0:T(8,128)S(1)}, f32[8,512]{1,0:T(8,128)}, u32[]{:S(2)}) copy-start(f32[8,512]{1,0:T(8,128)} %param.14) | copy-start | bytes 49156
  36.0 7.7 %collective-permute-start.3 = (bf16[8,64,256]{2,1,0:T(8,128)(2,1)S(1)}, bf16[8,64,256]{2,1,0:T(8,128)(2,1)S(1)}, u32[]{:S(2)}, u32[]{:S(2)}) collective-permute-start(bf16[8,64,256]{2,1,0:T(8,128)(2,1)S(1)} %add_convert_fusion.5), channel_id=1, source_target_pairs={{0,32},{32,64},{64,96},{96,128},{128,160},{160,192},{192,224},{1,3... | collective-permute-start | bytes 786440 | tf_op jit(solution)/shard_map/ppermute | solution.py:17
  43.9 7.7 %collective-permute-start.4 = (bf16[8,64,256]{2,1,0:T(8,128)(2,1)S(1)}, bf16[8,64,256]{2,1,0:T(8,128)(2,1)S(1)}, u32[]{:S(2)}, u32[]{:S(2)}) collective-permute-start(bf16[8,64,256]{2,1,0:T(8,128)(2,1)S(1)} %add_convert_fusion.4), channel_id=1, source_target_pairs={{0,32},{32,64},{64,96},{96,128},{128,160},{160,192},{192,224},{1,3... | collective-permute-start | bytes 786440 | tf_op jit(solution)/shard_map/ppermute | solution.py:17
  51.7 7.7 %collective-permute-start.5 = (bf16[8,64,256]{2,1,0:T(8,128)(2,1)S(1)}, bf16[8,64,256]{2,1,0:T(8,128)(2,1)S(1)}, u32[]{:S(2)}, u32[]{:S(2)}) collective-permute-start(bf16[8,64,256]{2,1,0:T(8,128)(2,1)S(1)} %add_convert_fusion.3), channel_id=1, source_target_pairs={{0,32},{32,64},{64,96},{96,128},{128,160},{160,192},{192,224},{1,3... | collective-permute-start | bytes 786440 | tf_op jit(solution)/shard_map/ppermute | solution.py:17
  59.5 7.7 %collective-permute-start.6 = (bf16[8,64,256]{2,1,0:T(8,128)(2,1)S(1)}, bf16[8,64,256]{2,1,0:T(8,128)(2,1)S(1)}, u32[]{:S(2)}, u32[]{:S(2)}) collective-permute-start(bf16[8,64,256]{2,1,0:T(8,128)(2,1)S(1)} %add_convert_fusion.2), channel_id=1, source_target_pairs={{0,32},{32,64},{64,96},{96,128},{128,160},{160,192},{192,224},{1,3... | collective-permute-start | bytes 786440 | tf_op jit(solution)/shard_map/ppermute | solution.py:17
  68.0 7.9 %collective-permute-start.7 = (bf16[8,64,256]{2,1,0:T(8,128)(2,1)}, bf16[8,64,256]{2,1,0:T(8,128)(2,1)S(1)}, u32[]{:S(2)}, u32[]{:S(2)}) collective-permute-start(bf16[8,64,256]{2,1,0:T(8,128)(2,1)} %add_convert_fusion.1), channel_id=1, source_target_pairs={{0,32},{32,64},{64,96},{96,128},{128,160},{160,192},{192,224},{1,3... | collective-permute-start | bytes 786440 | tf_op jit(solution)/shard_map/ppermute | solution.py:17
  76.1 7.7 %collective-permute-start.8 = (bf16[8,64,256]{2,1,0:T(8,128)(2,1)S(1)}, bf16[8,64,256]{2,1,0:T(8,128)(2,1)S(1)}, u32[]{:S(2)}, u32[]{:S(2)}) collective-permute-start(bf16[8,64,256]{2,1,0:T(8,128)(2,1)S(1)} %add_convert_fusion), channel_id=1, source_target_pairs={{0,32},{32,64},{64,96},{96,128},{128,160},{160,192},{192,224},{1,3... | collective-permute-start | bytes 786440 | tf_op jit(solution)/shard_map/ppermute | solution.py:17
  84.6 149.0 %copy-start.2 = (f32[512]{0:T(512)S(1)}, f32[512]{0:T(512)}, u32[]{:S(2)}) copy-start(f32[512]{0:T(512)} %param.18) | copy-start | bytes 6148
Sparse Core Ops, SparseCore 0:
  244.1 224.5 reduce-scatter.1
where the time goes:
time: 478 us; the launch traced here: 477 us
  waiting for transfers between devices  262 us (55%)
  blocking collectives  147 us (31%)
  starting transfers between devices  18.7 us (4%)
  matrix products  16.2 us (3%)
  between operations  13.8 us (3%)
  other arithmetic  11.3 us (2%)
  local copies, waits for them, and re-layouts  7.86 us (2%)
    reduce_scatter x1, waiting for transfers between devices, on_device(): lax.psum_scatter(project_term(out_proj, normed).astype(jnp.bfloat16), 'he...  225 us
    psum x1, blocking collectives, on_device(): squares = lax.psum(row_squares, 'head')  147 us
    ppermute x9, waiting for transfers between devices, shifted(): return lax.ppermute(block, axis, route)  37.4 us
    ppermute x9, starting transfers between devices, shifted(): return lax.ppermute(block, axis, route)  18.7 us
    dot_general x1, matrix products, project_term(): lax.dot_general(out_proj, normed, (((0,), (1,)), ((), ())), preferred_ele...  10.4 us
  transfers between devices with their start and end apart: 10, of which 8 were waited for; matrix products, arithmetic and copies ran while one was open for 3% of the time, Pallas kernels for 0%

commit v1 on v0

v1 whole, which is shorter than its diff:
```python
import functools

import jax
import jax.numpy as jnp
from jax import lax
from jax.experimental import pallas as pl
from jax.experimental.pallas import tpu as pltpu
from jax.sharding import PartitionSpec as P

GROUPS = 8
SPAN = 256
CORES = 2
NX = 4
NY = 4
NZ = 8
QUAD = 4
RIM = 16

norm_eps = 1e-05
F32 = jnp.float32
BF16 = jnp.bfloat16
EXACT = lax.Precision.HIGHEST


def y_route(dist):
    return [(y * NZ + z, (y + dist) % NY * NZ + z) for y in range(NY) for z in range(NZ)]


def z_route(dist):
    return [(y * NZ + z, y * NZ + (z + dist) % NZ) for y in range(NY) for z in range(NZ)]


def quad_route(dist):
    return [(h, h // QUAD * QUAD + (h + dist) % QUAD) for h in range(NY * NZ)]


def x_route(dist):
    return [(s, s + CORES * dist) for s in range(NX * CORES) if s + CORES * dist < NX * CORES]


CORE_SWAP = [(s, s ^ 1) for s in range(NX * CORES)]


def dot(a, b, dims=((1,), (0,)), precision=None):
    return lax.dot_general(a, b, (dims, ((), ())), precision=precision, preferred_element_type=F32)


def spread(heads_rows, width):
    heads = heads_rows.shape[0]
    pick = lax.broadcasted_iota(jnp.int32, (heads, width), 1) // (width // heads)
    own = lax.broadcasted_iota(jnp.int32, (heads, width), 0)
    return dot(heads_rows, (pick == own).astype(F32), ((0,), (0,)), EXACT)


def conv(buf, src_ref, rim, w_ref):
    rows = src_ref.shape[0]
    buf[0:8] = rim
    buf[8 : rows + 8] = src_ref[...].astype(F32)
    taps = w_ref[...].astype(F32)
    run = taps[0:1] * buf[5 : 5 + rows]
    for k in range(1, 4):
        run = run + taps[k : k + 1] * buf[5 + k : 5 + k + rows]
    return (run * jax.nn.sigmoid(run)).astype(BF16)


def state_kernel(
    at_ref, x_ref, bc_ref, rim_ref, wx_ref, wbc_ref, dt_ref, rate_ref,
    pay_ref, xs_ref, bc_out, s0_ref, ec_ref, e0_ref, xbuf, bbuf,
):
    width = x_ref.shape[1]
    rows = x_ref.shape[0]
    state = bc_ref.shape[1] // 2
    rim = rim_ref[...].astype(F32)[RIM - 8 :]
    x_conv = conv(xbuf, x_ref, rim[:, :width], wx_ref)
    bc = conv(bbuf, bc_ref, rim[:, width:], wbc_ref)
    bc_out[...] = bc
    dt = dt_ref[...]
    steps = -rate_ref[...] * dt
    before = (
        lax.broadcasted_iota(jnp.int32, (SPAN, SPAN), 0)
        <= lax.broadcasted_iota(jnp.int32, (SPAN, SPAN), 1)
    ).astype(F32)
    cum = jnp.concatenate(
        [dot(steps[:, s : s + SPAN], before, precision=EXACT) for s in range(0, rows, SPAN)], 1
    )
    grow = jnp.exp(cum)
    ec_ref[...] = grow
    scale = spread(dt * jnp.exp(-cum), width)
    xs = (x_conv.astype(F32) * scale).astype(BF16)
    xs_ref[...] = xs
    b_all = bc[:, :state]
    lasts = jnp.concatenate([grow[:, SPAN - 1 : SPAN], grow[:, rows - 1 : rows]], 1)
    last = spread(lasts, width)
    s0 = last[0:1] * dot(b_all[:SPAN], xs[:SPAN], ((0,), (0,)))
    s1 = last[1:2] * dot(b_all[SPAN:], xs[SPAN:], ((0,), (0,)))
    s0_ref[...] = s0.astype(BF16)
    e0_ref[...] = jnp.broadcast_to(last[0:1], e0_ref.shape)
    pay_ref[0:state] = (last[1:2] * s0 + s1).astype(BF16)
    whole = last[0:1] * last[1:2]
    pay_ref[state : state + 16] = decay_rows(whole)


def decay_rows(whole):
    top = whole.astype(BF16).astype(F32)
    mid = (whole - top).astype(BF16).astype(F32)
    low = whole - top - mid
    row = lax.broadcasted_iota(jnp.int32, (16, whole.shape[1]), 0)
    zero = jnp.zeros_like(row, F32)
    return jnp.where(
        row == 0, top, jnp.where(row == 1, mid, jnp.where(row == 2, low, zero))
    ).astype(BF16)


def decay_of(payload, state):
    rows = payload[state : state + 16].astype(F32)
    return rows[0:1] + rows[1:2] + rows[2:3]


def chip_kernel(at_ref, own_ref, other_ref, out_ref):
    core = at_ref[1]
    half = out_ref.shape[1]
    state = own_ref.shape[0] - 16
    cols = pl.ds(pl.multiple_of(core * half, half), half)
    own, other = own_ref[:, cols], other_ref[:, cols]
    own_decay, other_decay = decay_of(own, state), decay_of(other, state)
    own_s, other_s = own[:state].astype(F32), other[:state].astype(F32)
    late = jnp.where(core == 1, own_decay, other_decay)
    first = jnp.where(core == 1, other_s, own_s)
    second = jnp.where(core == 1, own_s, other_s)
    out_ref[0:state] = (late * first + second).astype(BF16)
    out_ref[state : state + 16] = decay_rows(own_decay * other_decay)


def prefix_kernel(one_ref, two_ref, three_ref, out_ref):
    state = out_ref.shape[0]
    one, two, three = one_ref[...], two_ref[...], three_ref[...]
    total = two[:state].astype(F32) + decay_of(two, state) * three[:state].astype(F32)
    total = one[:state].astype(F32) + decay_of(one, state) * total
    out_ref[...] = total.astype(BF16)


def diag_kernel(xs_ref, bc_ref, s0_ref, ec_ref, z_ref, y_ref, gate_ref):
    rows, width = xs_ref.shape
    state = bc_ref.shape[1] // 2
    seen = lax.broadcasted_iota(jnp.int32, (SPAN, SPAN), 0) >= lax.broadcasted_iota(
        jnp.int32, (SPAN, SPAN), 1
    )
    for s in range(0, rows, SPAN):
        b, c = bc_ref[s : s + SPAN, :state], bc_ref[s : s + SPAN, state:]
        scores = jnp.where(seen, dot(c, b, ((1,), (1,))), 0.0).astype(BF16)
        y = dot(scores, xs_ref[s : s + SPAN])
        if s:
            y = y + dot(c, s0_ref[...])
        y_ref[s : s + SPAN] = y
    z = z_ref[...].astype(F32)
    gate_ref[...] = z * jax.nn.sigmoid(z) * spread(ec_ref[...], width)


def gate_kernel(
    at_ref, mine_ref, theirs_ref, other_ref, bc_ref, y_ref, gate_ref, e0_ref, out_ref, ss_ref
):
    core = at_ref[1]
    state, half = mine_ref.shape
    rows = bc_ref.shape[0]
    mine, theirs = mine_ref[...].astype(F32), theirs_ref[...].astype(F32)
    left = jnp.where(core == 0, mine, theirs)
    right = jnp.where(core == 0, theirs, mine)
    prior = jnp.concatenate([left, right], 1)
    other = other_ref[...]
    after = decay_of(other, state) * prior + other[:state].astype(F32)
    incoming = jnp.where(core == 1, after, prior)
    ss = jnp.zeros(ss_ref.shape[:1] + (SPAN,), F32)
    ones = jnp.ones((8, out_ref.shape[1]), F32)
    for n, s in enumerate(range(0, rows, SPAN)):
        start = incoming if n == 0 else incoming * e0_ref[0:1]
        y = y_ref[s : s + SPAN] + dot(bc_ref[s : s + SPAN, state:], start.astype(BF16))
        gated = y * gate_ref[s : s + SPAN]
        out_ref[s : s + SPAN] = gated
        ss_ref[:, s : s + SPAN] = dot(ones, gated * gated, ((1,), (1,)), EXACT)


def norm_kernel(group_width, gated_ref, gain_ref, s0_ref, s1_ref, s2_ref, s3_ref, out_ref):
    mean_sq = (s0_ref[...] + s1_ref[...] + s2_ref[...] + s3_ref[...]) / group_width
    scale = spread(lax.rsqrt(mean_sq + norm_eps)[0:1], out_ref.shape[1])
    out_ref[...] = (gated_ref[...] * scale * gain_ref[...]).astype(BF16)


def project_kernel(
    at_ref, n0_ref, n1_ref, n2_ref, n3_ref, w0_ref, w1_ref, w2_ref, w3_ref, v1_ref, v2_ref, v3_ref, out_ref
):
    core = at_ref[1]
    half = w1_ref.shape[0]
    mine = pl.ds(pl.multiple_of(core * half, half), half)
    theirs = pl.ds(pl.multiple_of((1 - core) * half, half), half)
    total = dot(n0_ref[...], w0_ref[...])
    for n, w, v in ((n1_ref, w1_ref, v1_ref), (n2_ref, w2_ref, v2_ref), (n3_ref, w3_ref, v3_ref)):
        total = total + dot(n[:, mine], w[...])
        total = total + dot(n[:, theirs], v[...])
    out_ref[0] = total.astype(BF16)


def call(body, at, ins, outs, scratch=(), specs=None, grid=(1,), out_specs=None, flops=0):
    full = lambda s: pl.BlockSpec(s, lambda *_, n=len(s): (0,) * n)
    specs = specs or {}
    in_specs = [specs.get(k) or full(a.shape) for k, a in enumerate(ins)]
    kwargs = dict(
        out_shape=outs,
        compiler_params=pltpu.CompilerParams(vmem_limit_bytes=48 << 20),
        cost_estimate=pl.CostEstimate(
            flops=flops,
            bytes_accessed=sum(a.size * a.dtype.itemsize for a in (*ins, *outs)),
            transcendentals=0,
        ),
    )
    if out_specs is None:
        out_specs = [full(o.shape) for o in outs]
    if at is None:
        return pl.pallas_call(
            body, grid=grid, in_specs=in_specs, out_specs=out_specs, scratch_shapes=scratch, **kwargs
        )(*ins)
    return pl.pallas_call(
        body,
        grid_spec=pltpu.PrefetchScalarGridSpec(
            num_scalar_prefetch=1, grid=grid, in_specs=in_specs, out_specs=out_specs, scratch_shapes=scratch
        ),
        **kwargs,
    )(at, *ins)


def like(shape, dtype):
    return jax.ShapeDtypeStruct(shape, dtype)


def on_device(x, bc, z_gate, dt, rate, wx, wbc, gain, w_out):
    rows, width = x.shape
    heads = rate.shape[0]
    cols = bc.shape[1] // GROUPS
    state = cols // 2
    head_at, seq_at = lax.axis_index("head"), lax.axis_index("seq")
    group, core, y_at, z_at = head_at // QUAD, seq_at % CORES, head_at // NZ, head_at % NZ
    at = jnp.stack([group, core, y_at, z_at]).astype(jnp.int32)

    edge = lax.dynamic_slice(bc, (rows - RIM, group * cols), (RIM, cols))
    rim = lax.ppermute(
        jnp.concatenate([x[rows - RIM :], edge], 1), "seq", [(s, s + 1) for s in range(7)]
    )

    quarter = w_out.shape[1] // NY
    half_k = width // CORES
    w_mine = [
        lax.ppermute(
            lax.dynamic_slice(w_out, (core * half_k, (y_at + d) % NY * quarter), (half_k, quarter)),
            "head",
            y_route(d),
        )
        for d in range(1, NY)
    ]
    w_theirs = [lax.ppermute(w, "seq", CORE_SWAP) for w in w_mine]

    block = pl.BlockSpec((rows, cols), lambda i, s: (0, s[0]))
    wblock = pl.BlockSpec((4, cols), lambda i, s: (0, s[0]))
    payload, xs, bc_conv, s0, grow, e0 = call(
        state_kernel,
        at,
        [x, bc, rim, wx, wbc, dt, rate[:, None]],
        [
            like((state + 16, width), BF16),
            like((rows, width), BF16),
            like((rows, cols), BF16),
            like((state, width), BF16),
            like((heads, rows), F32),
            like((8, width), F32),
        ],
        scratch=[pltpu.VMEM((rows + 8, width), F32), pltpu.VMEM((rows + 8, cols), F32)],
        specs={1: block, 4: wblock},
    )
    other = lax.ppermute(payload, "seq", CORE_SWAP)
    [chip] = call(chip_kernel, at, [payload, other], [like((state + 16, width // 2), BF16)])
    befores = [lax.ppermute(chip, "seq", x_route(d)) for d in (1, 2, 3)]
    y_local, gate = call(
        diag_kernel,
        None,
        [xs, bc_conv, s0, grow, z_gate],
        [like((rows, width), F32), like((rows, width), F32)],
    )
    [mine] = call(prefix_kernel, None, befores, [like((state, width // 2), BF16)])
    theirs = lax.ppermute(mine, "seq", CORE_SWAP)
    gated, ss = call(
        gate_kernel,
        at,
        [mine, theirs, other, bc_conv, y_local, gate, e0],
        [like((rows, width), F32), like((8, rows), F32)],
    )
    more = [lax.ppermute(ss, "head", quad_route(d)) for d in range(1, QUAD)]
    [normed] = call(
        functools.partial(norm_kernel, width * QUAD),
        None,
        [gated, gain[None, :], ss, *more],
        [like((rows, width), BF16)],
    )
    peers = [lax.ppermute(normed, "head", y_route(d)) for d in range(1, NY)]
    feats = quarter // NZ
    in_quarter = pl.BlockSpec((half_k, feats), lambda i, s: (0, (s[3] + i) % NZ))
    in_whole = pl.BlockSpec((width, feats), lambda i, s: (0, s[2] * NZ + (s[3] + i) % NZ))
    [parts] = call(
        project_kernel,
        at,
        [normed, *peers, w_out, *w_mine, *w_theirs],
        [like((NZ, rows, feats), BF16)],
        specs={4: in_whole, **{k: in_quarter for k in range(5, 11)}},
        grid=(NZ,),
        out_specs=[pl.BlockSpec((1, rows, feats), lambda i, s: (i, 0, 0))],
        flops=2 * rows * width * quarter * NY,
    )
    send = lambda v, d: lax.ppermute(v, "head", z_route(d))
    mid = rows // 2
    up, down = send(parts[4, :mid], 1), send(parts[4, mid:], -1)
    add = lambda a, b: (a.astype(F32) + b.astype(F32)).astype(BF16)
    up = send(jnp.concatenate([add(parts[3, :mid], up), parts[3, mid:]], 0), 1)
    down = send(jnp.concatenate([parts[5, :mid], add(parts[5, mid:], down)], 0), -1)
    up, down = send(add(parts[2], up), 1), send(add(parts[6], down), -1)
    up, down = send(add(parts[1], up), 1), send(add(parts[7], down), -1)
    return (parts[0].astype(F32) + up.astype(F32) + down.astype(F32)).astype(BF16).T


def solution(mesh):
    placed = (
        P("seq", "head"),
        P("seq", None),
        P("seq", "head"),
        P("head", "seq"),
        P("head"),
        P(None, "head"),
        P(),
        P("head"),
        P("head", None),
    )
    return jax.shard_map(
        on_device, mesh=mesh, in_specs=placed, out_specs=P("head", "seq"), check_vma=False
    )
```

time: 478 us -> 145 us (0.30)
  waiting for transfers between devices: 262 us -> 64.8 us
  blocking collectives: 147 us -> 0 us
  starting transfers between devices: 18.7 us -> 46.8 us
  Pallas kernels: 0 us -> 19.9 us
  matrix products: 16.2 us -> 0 us
  between operations: 13.8 us -> 0.25 us
  other arithmetic: 11.3 us -> 1.54 us
    reduce_scatter x1 -> x0, waiting for transfers between devices: 225 us -> none  [on_device(): lax.psum_scatter(project_term(out_proj, normed).astype(jnp.bfloat16), 'he...]
    psum x1 -> x0, blocking collectives: 147 us -> none  [on_device(): squares = lax.psum(row_squares, 'head')]
    ppermute x9 -> x26, starting transfers between devices: 18.7 us -> 46.8 us  [the longest x3 14.9 us: on_device(): befores = [lax.ppermute(chip, 'seq', x_route(d)) for d in (1, 2, 3)]]
    ppermute x9 -> x26, waiting for transfers between devices: 37.4 us -> 64.8 us  [the longest x3 28.1 us: on_device(): peers = [lax.ppermute(normed, 'head', y_route(d)) for d in range(1, NY)]]
    pallas_call x0 -> x7, Pallas kernels: none -> 19.9 us  [the longest x4 17.4 us: call(): pl.pallas_call(body, grid_spec=pltpu.PrefetchScalarGridSpec(num_scalar_pr...]
    dot_general x6 -> x0, matrix products: 16.2 us -> none  [the longest x1 10.4 us: project_term(): lax.dot_general(out_proj, normed, (((0,), (1,)), ((), ())), preferred_ele...]
  transfers between devices with their start and end apart: 10 -> 26, of which waited for: 8 -> 14; matrix products, arithmetic and copies ran while one was open for 3% -> 1% of each run, Pallas kernels for 0% -> 7%
where the time goes in v1:
time: 145 us; the launch traced here: 143 us
  waiting for transfers between devices  64.8 us (45%)
  starting transfers between devices  46.8 us (32%)
  Pallas kernels  19.9 us (14%)
  local copies, waits for them, and re-layouts  9.9 us (7%)
  other arithmetic  1.54 us (1%)
    ppermute x3, waiting for transfers between devices, on_device(): peers = [lax.ppermute(normed, 'head', y_route(d)) for d in range(1, NY)]  28.1 us
    ppermute x8, waiting for transfers between devices, on_device(): send = lambda v, d: lax.ppermute(v, 'head', z_route(d))  22.2 us
    pallas_call x4, Pallas kernels, call(): pl.pallas_call(body, grid_spec=pltpu.PrefetchScalarGridSpec(num_scalar_pr...  17.4 us
    ppermute x3, starting transfers between devices, on_device(): befores = [lax.ppermute(chip, 'seq', x_route(d)) for d in (1, 2, 3)]  14.9 us
    ppermute x8, starting transfers between devices, on_device(): send = lambda v, d: lax.ppermute(v, 'head', z_route(d))  14.2 us
    ppermute x3, waiting for transfers between devices, on_device(): more = [lax.ppermute(ss, 'head', quad_route(d)) for d in range(1, QUAD)]  7.25 us
    ppermute x3, starting transfers between devices, on_device(): peers = [lax.ppermute(normed, 'head', y_route(d)) for d in range(1, NY)]  5.81 us
    ppermute x3, starting transfers between devices, on_device(): more = [lax.ppermute(ss, 'head', quad_route(d)) for d in range(1, QUAD)]  4.65 us
  transfers between devices with their start and end apart: 26, of which 14 were waited for; matrix products, arithmetic and copies ran while one was open for 1% of the time, Pallas kernels for 7%

profile of v1, /device:TPU:4, one launch (start us, length us, event | category | flops | bytes accessed | tf_op | source)
XLA Modules:
  0.0 143.3 jit_solution(9285787286765591365)
XLA Ops:
  0.0 3.6 %fusion.9 = (bf16[256,2048]{1,0:T(8,128)(2,1)}, bf16[256,2048]{1,0:T(8,128)(2,1)}, bf16[256,2048]{1,0:T(8,128)(2,1)}) fusion(bf16[512,8192]{1,0:T(8,128)(2,1)} %w0_ref.1, s32[]{:T(128)S(6)} %select_n.52, s32[]{:T(128)S(6)} %select_n.58, s32[]{:T(128)S(6)} %select_n.56, s32[]{:T(128)S(6)} %select_n.54), kind=kLoop, calls=%fused_computation.32 | loop fusion | bytes 6291472 | tf_op jit(solution)/shard_map/dynamic_slice | solution.py:252
  3.7 3.0 %collective-permute-start.14 = (bf16[256,2048]{1,0:T(8,128)(2,1)}, bf16[256,2048]{1,0:T(8,128)(2,1)S(1)}, u32[]{:S(2)}, u32[]{:S(2)}) collective-permute-start(bf16[256,2048]{1,0:T(8,128)(2,1)} %get-tuple-element.25), channel_id=1, source_target_pairs={{0,24},{1,25},{2,26},{3,27},{4,28},{5,29},{6,30},{7,31},{8,0},{9,1... | collective-permute-start | bytes 3145736 | tf_op jit(solution)/shard_map/ppermute | solution.py:251
  9.0 1.9 %collective-permute-start = (bf16[16,1024]{1,0:T(8,128)(2,1)S(1)}, bf16[16,1024]{1,0:T(8,128)(2,1)S(1)}, u32[]{:S(2)}, u32[]{:S(2)}) collective-permute-start(bf16[16,1024]{1,0:T(8,128)(2,1)S(1)} %pad_maximum_fusion.2), channel_id=1, source_target_pairs={{0,32},{32,64},{64,96},{96,128},{128,160},{160,192},{192,224},{1,3... | collective-permute-start | bytes 98312 | tf_op jit(solution)/shard_map/ppermute | solution.py:244
  11.1 3.1 %collective-permute-done.rim_ref = bf16[16,1024]{1,0:T(8,128)(2,1)S(1)} collective-permute-done((bf16[16,1024]{1,0:T(8,128)(2,1)S(1)}, bf16[16,1024]{1,0:T(8,128)(2,1)S(1)}, u32[]{:S(2)}, u32[]{:S(2)}) %collective-permute-start) | collective-permute-done | bytes 32800 | tf_op jit(solution)/shard_map/ppermute | solution.py:244
  15.3 5.1 %shard_map.91 = (bf16[272,512]{1,0:T(8,128)(2,1)S(1)}, bf16[512,512]{1,0:T(8,128)(2,1)S(1)}, bf16[512,512]{1,0:T(8,128)(2,1)S(1)}, bf16[256,512]{1,0:T(8,128)(2,...) custom-call(s32[4]{0:T(128)S(1)} %pad_add_fusion.at_ref, bf16[512,512]{1,0:T(8,128)(2,1)S(1)} %copy-done, ...), custom_call_target="tpu_custom_call" | custom-call | bytes 6426656 | tf_op jit(solution)/shard_map/pallas_call | solution.py:221
  20.5 1.5 %collective-permute-done.1.other_ref = bf16[272,512]{1,0:T(8,128)(2,1)S(1)} collective-permute-done((bf16[272,512]{1,0:T(8,128)(2,1)S(1)}, bf16[272,512]{1,0:T(8,128)(2,1)S(1)}, u32[]{:S(2)}, u32[]{:S(2)}) %collective-permute-start.1) | collective-permute-done | bytes 278560 | tf_op jit(solution)/shard_map/ppermute | solution.py:277
  23.4 1.3 collective-permute-start.3
  24.7 12.9 %collective-permute-start.2 = (bf16[272,256]{1,0:T(8,128)(2,1)S(1)}, bf16[272,256]{1,0:T(8,128)(2,1)S(1)}, u32[]{:S(2)}, u32[]{:S(2)}) collective-permute-start(bf16[272,256]{1,0:T(8,128)(2,1)S(1)} %shard_map.92), channel_id=1, source_target_pairs={{0,64},{32,96},{64,128},{96,160},{128,192},{160,224},{1,65},{33,97... | collective-permute-start | bytes 417800 | tf_op jit(solution)/shard_map/ppermute | solution.py:279
  37.6 2.6 %collective-permute-done.2.one_ref = bf16[272,256]{1,0:T(8,128)(2,1)S(1)} collective-permute-done((bf16[272,256]{1,0:T(8,128)(2,1)S(1)}, bf16[272,256]{1,0:T(8,128)(2,1)S(1)}, u32[]{:S(2)}, u32[]{:S(2)}) %collective-permute-start.2) | collective-permute-done | bytes 139296 | tf_op jit(solution)/shard_map/ppermute | solution.py:279
  40.4 1.4 shard_map.94
  41.8 1.8 %shard_map.95 = (f32[512,512]{1,0:T(8,128)S(1)}, f32[8,512]{1,0:T(8,128)S(1)}) custom-call(s32[4]{0:T(128)S(1)} %pad_add_fusion.at_ref, bf16[256,256]{1,0:T(8,128)(2,1)S(1)} %shard_map.93.mine_ref, bf16[256,256]{1,0:T(8,128)(2,1)S(1)} %collective-permute-done.5.theirs_ref, bf16[272,512]{1,0:T(8,128)(2,1)S(1)} %collective-permute-done.1.other_ref, ...), custom_call_target="tpu_custom_call" | custom-call | bytes 4243456 | tf_op jit(solution)/shard_map/pallas_call | solution.py:221
  43.6 4.6 %collective-permute-start.8 = (f32[8,512]{1,0:T(8,128)S(1)}, f32[8,512]{1,0:T(8,128)S(1)}, u32[]{:S(2)}, u32[]{:S(2)}) collective-permute-start(f32[8,512]{1,0:T(8,128)S(1)} %get-tuple-element.24.s0_ref), channel_id=1, source_target_pairs={{0,3},{1,0},{2,1},{3,2},{4,7},{5,4},{6,5},{7,6},{8,11},{9,8},{10,9... | collective-permute-start | bytes 49160 | tf_op jit(solution)/shard_map/ppermute | solution.py:294
  48.2 1.4 %collective-permute-done.8.s3_ref = f32[8,512]{1,0:T(8,128)S(1)} collective-permute-done((f32[8,512]{1,0:T(8,128)S(1)}, f32[8,512]{1,0:T(8,128)S(1)}, u32[]{:S(2)}, u32[]{:S(2)}) %collective-permute-start.8) | collective-permute-done | bytes 16416 | tf_op jit(solution)/shard_map/ppermute | solution.py:294
  49.7 3.2 %collective-permute-done.7.s2_ref = f32[8,512]{1,0:T(8,128)S(1)} collective-permute-done((f32[8,512]{1,0:T(8,128)S(1)}, f32[8,512]{1,0:T(8,128)S(1)}, u32[]{:S(2)}, u32[]{:S(2)}) %collective-permute-start.7) | collective-permute-done | bytes 16416 | tf_op jit(solution)/shard_map/ppermute | solution.py:294
  52.9 2.6 %collective-permute-done.6.s1_ref = f32[8,512]{1,0:T(8,128)S(1)} collective-permute-done((f32[8,512]{1,0:T(8,128)S(1)}, f32[8,512]{1,0:T(8,128)S(1)}, u32[]{:S(2)}, u32[]{:S(2)}) %collective-permute-start.6) | collective-permute-done | bytes 16416 | tf_op jit(solution)/shard_map/ppermute | solution.py:294
  56.5 2.3 %collective-permute-start.11 = (bf16[512,512]{1,0:T(8,128)(2,1)S(1)}, bf16[512,512]{1,0:T(8,128)(2,1)S(1)}, u32[]{:S(2)}, u32[]{:S(2)}) collective-permute-start(bf16[512,512]{1,0:T(8,128)(2,1)S(1)} %shard_map.96.n0_ref), channel_id=1, source_target_pairs={{0,24},{1,25},{2,26},{3,27},{4,28},{5,29},{6,30},{7,31},{8,0},{9,1... | collective-permute-start | bytes 1572872 | tf_op jit(solution)/shard_map/ppermute | solution.py:301
  59.5 1.7 %collective-permute-start.10 = (bf16[512,512]{1,0:T(8,128)(2,1)S(1)}, bf16[512,512]{1,0:T(8,128)(2,1)S(1)}, u32[]{:S(2)}, u32[]{:S(2)}) collective-permute-start(bf16[512,512]{1,0:T(8,128)(2,1)S(1)} %shard_map.96.n0_ref), channel_id=1, source_target_pairs={{0,16},{1,17},{2,18},{3,19},{4,20},{5,21},{6,22},{7,23},{8,24},{9,... | collective-permute-start | bytes 1572872 | tf_op jit(solution)/shard_map/ppermute | solution.py:301
  61.2 19.1 %collective-permute-done.11.n3_ref = bf16[512,512]{1,0:T(8,128)(2,1)S(1)} collective-permute-done((bf16[512,512]{1,0:T(8,128)(2,1)S(1)}, bf16[512,512]{1,0:T(8,128)(2,1)S(1)}, u32[]{:S(2)}, u32[]{:S(2)}) %collective-permute-start.11) | collective-permute-done | bytes 524320 | tf_op jit(solution)/shard_map/ppermute | solution.py:301
  80.3 1.8 %collective-permute-start.9 = (bf16[512,512]{1,0:T(8,128)(2,1)S(1)}, bf16[512,512]{1,0:T(8,128)(2,1)S(1)}, u32[]{:S(2)}, u32[]{:S(2)}) collective-permute-start(bf16[512,512]{1,0:T(8,128)(2,1)S(1)} %shard_map.96.n0_ref), channel_id=1, source_target_pairs={{0,8},{1,9},{2,10},{3,11},{4,12},{5,13},{6,14},{7,15},{8,16},{9,17... | collective-permute-start | bytes 1572872 | tf_op jit(solution)/shard_map/ppermute | solution.py:301
  82.0 9.0 %collective-permute-done.9.n1_ref = bf16[512,512]{1,0:T(8,128)(2,1)S(1)} collective-permute-done((bf16[512,512]{1,0:T(8,128)(2,1)S(1)}, bf16[512,512]{1,0:T(8,128)(2,1)S(1)}, u32[]{:S(2)}, u32[]{:S(2)}) %collective-permute-start.9) | collective-permute-done | bytes 524320 | tf_op jit(solution)/shard_map/ppermute | solution.py:301
  93.4 9.8 %shard_map.97 = bf16[8,512,256]{2,1,0:T(8,128)(2,1)} custom-call(s32[4]{0:T(128)S(1)} %pad_add_fusion.at_ref, bf16[512,512]{1,0:T(8,128)(2,1)S(1)} %shard_map.96.n0_ref, bf16[512,512]{1,0:T(8,128)(2,1)S(1)} %collective-permute-done.9.n1_ref, bf16[512,512]{1,0:T(8,128)(2,1)S(1)} %collective-permute-done.10.n2_ref, ...), custom_call_target="tpu_custom_call" | custom-call | flops 4294967296 | bytes 18874368 | tf_op jit(solution)/shard_map/pallas_call | solution.py:221
  103.2 1.3 slice_bitcast_fusion.9
  104.6 3.3 %collective-permute-start.22 = (bf16[256,256]{1,0:T(8,128)(2,1)S(1)}, bf16[256,256]{1,0:T(8,128)(2,1)S(1)}, u32[]{:S(2)}, u32[]{:S(2)}) collective-permute-start(bf16[256,256]{1,0:T(8,128)(2,1)S(1)} %get-tuple-element.33), channel_id=1, source_target_pairs={{0,7},{1,0},{2,1},{3,2},{4,3},{5,4},{6,5},{7,6},{8,15},{9,8},{10,9... | collective-permute-start | bytes 393224 | tf_op jit(solution)/shard_map/ppermute | solution.py:315
  107.9 2.9 %collective-permute-done.18 = bf16[256,256]{1,0:T(8,128)(2,1)S(1)} collective-permute-done((bf16[256,256]{1,0:T(8,128)(2,1)S(1)}, bf16[256,256]{1,0:T(8,128)(2,1)S(1)}, u32[]{:S(2)}, u32[]{:S(2)}) %collective-permute-start.18) | collective-permute-done | bytes 131104 | tf_op jit(solution)/shard_map/ppermute | solution.py:315
  112.4 2.9 %collective-permute-start.23 = (bf16[512,256]{1,0:T(8,128)(2,1)S(1)}, bf16[512,256]{1,0:T(8,128)(2,1)S(1)}, u32[]{:S(2)}, u32[]{:S(2)}) collective-permute-start(bf16[512,256]{1,0:T(8,128)(2,1)S(1)} %pad_maximum_fusion.1), channel_id=1, source_target_pairs={{0,7},{1,0},{2,1},{3,2},{4,3},{5,4},{6,5},{7,6},{8,15},{9,8},{10,9... | collective-permute-start | bytes 786440 | tf_op jit(solution)/shard_map/ppermute | solution.py:315
  115.4 4.6 %collective-permute-done.19 = bf16[512,256]{1,0:T(8,128)(2,1)S(1)} collective-permute-done((bf16[512,256]{1,0:T(8,128)(2,1)S(1)}, bf16[512,256]{1,0:T(8,128)(2,1)S(1)}, u32[]{:S(2)}, u32[]{:S(2)}) %collective-permute-start.19) | collective-permute-done | bytes 262176 | tf_op jit(solution)/shard_map/ppermute | solution.py:315
  120.1 1.9 %collective-permute-start.20 = (bf16[512,256]{1,0:T(8,128)(2,1)S(1)}, bf16[512,256]{1,0:T(8,128)(2,1)S(1)}, u32[]{:S(2)}, u32[]{:S(2)}) collective-permute-start(bf16[512,256]{1,0:T(8,128)(2,1)S(1)} %fusion.2), channel_id=1, source_target_pairs={{0,1},{1,2},{2,3},{3,4},{4,5},{5,6},{6,7},{7,0},{8,9},{9,10},{10,1... | collective-permute-start | bytes 786440 | tf_op jit(solution)/shard_map/ppermute | solution.py:315
  122.2 6.2 %collective-permute-done.20 = bf16[512,256]{1,0:T(8,128)(2,1)S(1)} collective-permute-done((bf16[512,256]{1,0:T(8,128)(2,1)S(1)}, bf16[512,256]{1,0:T(8,128)(2,1)S(1)}, u32[]{:S(2)}, u32[]{:S(2)}) %collective-permute-start.20) | collective-permute-done | bytes 262176 | tf_op jit(solution)/shard_map/ppermute | solution.py:315
  128.6 2.1 %collective-permute-start.24 = (bf16[512,256]{1,0:T(8,128)(2,1)S(1)}, bf16[512,256]{1,0:T(8,128)(2,1)S(1)}, u32[]{:S(2)}, u32[]{:S(2)}) collective-permute-start(bf16[512,256]{1,0:T(8,128)(2,1)S(1)} %get-tuple-element.29), channel_id=1, source_target_pairs={{0,7},{1,0},{2,1},{3,2},{4,3},{5,4},{6,5},{7,6},{8,15},{9,8},{10,9... | collective-permute-start | bytes 786440 | tf_op jit(solution)/shard_map/ppermute | solution.py:315
  130.7 4.3 %collective-permute-done.24 = bf16[512,256]{1,0:T(8,128)(2,1)S(1)} collective-permute-done((bf16[512,256]{1,0:T(8,128)(2,1)S(1)}, bf16[512,256]{1,0:T(8,128)(2,1)S(1)}, u32[]{:S(2)}, u32[]{:S(2)}) %collective-permute-start.24) | collective-permute-done | bytes 262176 | tf_op jit(solution)/shard_map/ppermute | solution.py:315
  135.1 3.3 %collective-permute-start.25 = (bf16[512,256]{1,0:T(8,128)(2,1)S(1)}, bf16[512,256]{1,0:T(8,128)(2,1)S(1)}, u32[]{:S(2)}, u32[]{:S(2)}) collective-permute-start(bf16[512,256]{1,0:T(8,128)(2,1)S(1)} %fusion.1), channel_id=1, source_target_pairs={{0,7},{1,0},{2,1},{3,2},{4,3},{5,4},{6,5},{7,6},{8,15},{9,8},{10,9... | collective-permute-start | bytes 786440 | tf_op jit(solution)/shard_map/ppermute | solution.py:315
  138.4 3.9 %collective-permute-done.25 = bf16[512,256]{1,0:T(8,128)(2,1)S(1)} collective-permute-done((bf16[512,256]{1,0:T(8,128)(2,1)S(1)}, bf16[512,256]{1,0:T(8,128)(2,1)S(1)}, u32[]{:S(2)}, u32[]{:S(2)}) %collective-permute-start.25) | collective-permute-done | bytes 262176 | tf_op jit(solution)/shard_map/ppermute | solution.py:315
  (65 shorter events, 12.3 us)
Async XLA Ops:
  0.0 14.2 %copy-start.2 = (bf16[4,4096]{1,0:T(4,128)(2,1)S(1)}, bf16[4,4096]{1,0:T(4,128)(2,1)}, u32[]{:S(2)}) copy-start(bf16[4,4096]{1,0:T(4,128)(2,1)} %wbc_ref.1) | copy-start | bytes 98308
  0.0 14.2 %copy-start.3 = (f32[8,512]{1,0:T(8,128)S(1)}, f32[8,512]{1,0:T(8,128)}, u32[]{:S(2)}) copy-start(f32[8,512]{1,0:T(8,128)} %dt_ref.1) | copy-start | bytes 49156
  0.0 14.2 %copy-start.4 = (bf16[4,512]{1,0:T(4,128)(2,1)S(1)}, bf16[4,512]{1,0:T(4,128)(2,1)}, u32[]{:S(2)}) copy-start(bf16[4,512]{1,0:T(4,128)(2,1)} %wx_ref.1) | copy-start | bytes 12292
  3.7 55.2 %collective-permute-start.14 = (bf16[256,2048]{1,0:T(8,128)(2,1)}, bf16[256,2048]{1,0:T(8,128)(2,1)S(1)}, u32[]{:S(2)}, u32[]{:S(2)}) collective-permute-start(bf16[256,2048]{1,0:T(8,128)(2,1)} %get-tuple-element.25), channel_id=1, source_target_pairs={{0,24},{1,25},{2,26},{3,27},{4,28},{5,29},{6,30},{7,31},{8,0},{9,1... | collective-permute-start | bytes 3145736 | tf_op jit(solution)/shard_map/ppermute | solution.py:251
  6.7 52.2 %collective-permute-start.13 = (bf16[256,2048]{1,0:T(8,128)(2,1)}, bf16[256,2048]{1,0:T(8,128)(2,1)S(1)}, u32[]{:S(2)}, u32[]{:S(2)}) collective-permute-start(bf16[256,2048]{1,0:T(8,128)(2,1)} %get-tuple-element.26), channel_id=1, source_target_pairs={{0,16},{1,17},{2,18},{3,19},{4,20},{5,21},{6,22},{7,23},{8,24},{9,... | collective-permute-start | bytes 3145736 | tf_op jit(solution)/shard_map/ppermute | solution.py:251
  7.3 52.1 %collective-permute-start.12 = (bf16[256,2048]{1,0:T(8,128)(2,1)}, bf16[256,2048]{1,0:T(8,128)(2,1)S(1)}, u32[]{:S(2)}, u32[]{:S(2)}) collective-permute-start(bf16[256,2048]{1,0:T(8,128)(2,1)} %get-tuple-element.27), channel_id=1, source_target_pairs={{0,8},{1,9},{2,10},{3,11},{4,12},{5,13},{6,14},{7,15},{8,16},{9,17... | collective-permute-start | bytes 3145736 | tf_op jit(solution)/shard_map/ppermute | solution.py:251
  9.0 5.2 %collective-permute-start = (bf16[16,1024]{1,0:T(8,128)(2,1)S(1)}, bf16[16,1024]{1,0:T(8,128)(2,1)S(1)}, u32[]{:S(2)}, u32[]{:S(2)}) collective-permute-start(bf16[16,1024]{1,0:T(8,128)(2,1)S(1)} %pad_maximum_fusion.2), channel_id=1, source_target_pairs={{0,32},{32,64},{64,96},{96,128},{128,160},{160,192},{192,224},{1,3... | collective-permute-start | bytes 98312 | tf_op jit(solution)/shard_map/ppermute | solution.py:244
  15.3 25.1 %copy-start.1 = (bf16[512,512]{1,0:T(8,128)(2,1)S(1)}, bf16[512,512]{1,0:T(8,128)(2,1)}, u32[]{:S(2)}) copy-start(bf16[512,512]{1,0:T(8,128)(2,1)} %z_ref.1) | copy-start | bytes 1572868
  20.4 1.6 %collective-permute-start.1 = (bf16[272,512]{1,0:T(8,128)(2,1)S(1)}, bf16[272,512]{1,0:T(8,128)(2,1)S(1)}, u32[]{:S(2)}, u32[]{:S(2)}) collective-permute-start(bf16[272,512]{1,0:T(8,128)(2,1)S(1)} %get-tuple-element.15.own_ref), channel_id=1, source_target_pairs={{0,32},{32,0},{64,96},{96,64},{128,160},{160,128},{192,224},{224,1... | collective-permute-start | bytes 835592 | tf_op jit(solution)/shard_map/ppermute | solution.py:277
  22.7 2.0 %collective-permute-start.4 = (bf16[272,256]{1,0:T(8,128)(2,1)S(1)}, bf16[272,256]{1,0:T(8,128)(2,1)S(1)}, u32[]{:S(2)}, u32[]{:S(2)}) collective-permute-start(bf16[272,256]{1,0:T(8,128)(2,1)S(1)} %shard_map.92), channel_id=1, source_target_pairs={{0,192},{32,224},{1,193},{33,225},{2,194},{34,226},{3,195},{35,227... | collective-permute-start | bytes 417800 | tf_op jit(solution)/shard_map/ppermute | solution.py:279
  23.4 14.2 %collective-permute-start.3 = (bf16[272,256]{1,0:T(8,128)(2,1)S(1)}, bf16[272,256]{1,0:T(8,128)(2,1)S(1)}, u32[]{:S(2)}, u32[]{:S(2)}) collective-permute-start(bf16[272,256]{1,0:T(8,128)(2,1)S(1)} %shard_map.92), channel_id=1, source_target_pairs={{0,128},{32,160},{64,192},{96,224},{1,129},{33,161},{65,193},{97,2... | collective-permute-start | bytes 417800 | tf_op jit(solution)/shard_map/ppermute | solution.py:279
  24.7 15.5 %collective-permute-start.2 = (bf16[272,256]{1,0:T(8,128)(2,1)S(1)}, bf16[272,256]{1,0:T(8,128)(2,1)S(1)}, u32[]{:S(2)}, u32[]{:S(2)}) collective-permute-start(bf16[272,256]{1,0:T(8,128)(2,1)S(1)} %shard_map.92), channel_id=1, source_target_pairs={{0,64},{32,96},{64,128},{96,160},{128,192},{160,224},{1,65},{33,97... | collective-permute-start | bytes 417800 | tf_op jit(solution)/shard_map/ppermute | solution.py:279
  40.3 1.5 %collective-permute-start.5 = (bf16[256,256]{1,0:T(8,128)(2,1)S(1)}, bf16[256,256]{1,0:T(8,128)(2,1)S(1)}, u32[]{:S(2)}, u32[]{:S(2)}) collective-permute-start(bf16[256,256]{1,0:T(8,128)(2,1)S(1)} %shard_map.93.mine_ref), channel_id=1, source_target_pairs={{0,32},{32,0},{64,96},{96,64},{128,160},{160,128},{192,224},{224,1... | collective-permute-start | bytes 393224 | tf_op jit(solution)/shard_map/ppermute | solution.py:287
  40.4 15.1 %copy-start.5 = (f32[512]{0:T(512)S(1)}, f32[512]{0:T(512)}, u32[]{:S(2)}) copy-start(f32[512]{0:T(512)} %param.16) | copy-start | bytes 6148
  43.6 6.1 %collective-permute-start.8 = (f32[8,512]{1,0:T(8,128)S(1)}, f32[8,512]{1,0:T(8,128)S(1)}, u32[]{:S(2)}, u32[]{:S(2)}) collective-permute-start(f32[8,512]{1,0:T(8,128)S(1)} %get-tuple-element.24.s0_ref), channel_id=1, source_target_pairs={{0,3},{1,0},{2,1},{3,2},{4,7},{5,4},{6,5},{7,6},{8,11},{9,8},{10,9... | collective-permute-start | bytes 49160 | tf_op jit(solution)/shard_map/ppermute | solution.py:294
  48.2 4.6 %collective-permute-start.7 = (f32[8,512]{1,0:T(8,128)S(1)}, f32[8,512]{1,0:T(8,128)S(1)}, u32[]{:S(2)}, u32[]{:S(2)}) collective-permute-start(f32[8,512]{1,0:T(8,128)S(1)} %get-tuple-element.24.s0_ref), channel_id=1, source_target_pairs={{0,2},{1,3},{2,0},{3,1},{4,6},{5,7},{6,4},{7,5},{8,10},{9,11},{10,... | collective-permute-start | bytes 49160 | tf_op jit(solution)/shard_map/ppermute | solution.py:294
  49.7 5.8 %collective-permute-start.6 = (f32[8,512]{1,0:T(8,128)S(1)}, f32[8,512]{1,0:T(8,128)S(1)}, u32[]{:S(2)}, u32[]{:S(2)}) collective-permute-start(f32[8,512]{1,0:T(8,128)S(1)} %get-tuple-element.24.s0_ref), channel_id=1, source_target_pairs={{0,1},{1,2},{2,3},{3,0},{4,5},{5,6},{6,7},{7,4},{8,9},{9,10},{10,1... | collective-permute-start | bytes 49160 | tf_op jit(solution)/shard_map/ppermute | solution.py:294
  56.5 23.7 %collective-permute-start.11 = (bf16[512,512]{1,0:T(8,128)(2,1)S(1)}, bf16[512,512]{1,0:T(8,128)(2,1)S(1)}, u32[]{:S(2)}, u32[]{:S(2)}) collective-permute-start(bf16[512,512]{1,0:T(8,128)(2,1)S(1)} %shard_map.96.n0_ref), channel_id=1, source_target_pairs={{0,24},{1,25},{2,26},{3,27},{4,28},{5,29},{6,30},{7,31},{8,0},{9,1... | collective-permute-start | bytes 1572872 | tf_op jit(solution)/shard_map/ppermute | solution.py:301
  58.9 32.2 %collective-permute-start.17 = (bf16[256,2048]{1,0:T(8,128)(2,1)S(1)}, bf16[256,2048]{1,0:T(8,128)(2,1)S(1)}, u32[]{:S(2)}, u32[]{:S(2)}) collective-permute-start(bf16[256,2048]{1,0:T(8,128)(2,1)S(1)} %collective-permute-done.14.w3_ref), channel_id=1, source_target_pairs={{0,32},{32,0},{64,96},{96,64},{128,160},{160,128},{192,224},{224,1... | collective-permute-start | bytes 3145736 | tf_op jit(solution)/shard_map/ppermute | solution.py:258
  58.9 32.2 %collective-permute-start.16 = (bf16[256,2048]{1,0:T(8,128)(2,1)S(1)}, bf16[256,2048]{1,0:T(8,128)(2,1)S(1)}, u32[]{:S(2)}, u32[]{:S(2)}) collective-permute-start(bf16[256,2048]{1,0:T(8,128)(2,1)S(1)} %collective-permute-done.13.w2_ref), channel_id=1, source_target_pairs={{0,32},{32,0},{64,96},{96,64},{128,160},{160,128},{192,224},{224,1... | collective-permute-start | bytes 3145736 | tf_op jit(solution)/shard_map/ppermute | solution.py:258
  59.4 31.7 %collective-permute-start.15 = (bf16[256,2048]{1,0:T(8,128)(2,1)S(1)}, bf16[256,2048]{1,0:T(8,128)(2,1)S(1)}, u32[]{:S(2)}, u32[]{:S(2)}) collective-permute-start(bf16[256,2048]{1,0:T(8,128)(2,1)S(1)} %collective-permute-done.12.w1_ref), channel_id=1, source_target_pairs={{0,32},{32,0},{64,96},{96,64},{128,160},{160,128},{192,224},{224,1... | collective-permute-start | bytes 3145736 | tf_op jit(solution)/shard_map/ppermute | solution.py:258
  59.5 22.5 %collective-permute-start.10 = (bf16[512,512]{1,0:T(8,128)(2,1)S(1)}, bf16[512,512]{1,0:T(8,128)(2,1)S(1)}, u32[]{:S(2)}, u32[]{:S(2)}) collective-permute-start(bf16[512,512]{1,0:T(8,128)(2,1)S(1)} %shard_map.96.n0_ref), channel_id=1, source_target_pairs={{0,16},{1,17},{2,18},{3,19},{4,20},{5,21},{6,22},{7,23},{8,24},{9,... | collective-permute-start | bytes 1572872 | tf_op jit(solution)/shard_map/ppermute | solution.py:301
  80.3 10.8 %collective-permute-start.9 = (bf16[512,512]{1,0:T(8,128)(2,1)S(1)}, bf16[512,512]{1,0:T(8,128)(2,1)S(1)}, u32[]{:S(2)}, u32[]{:S(2)}) collective-permute-start(bf16[512,512]{1,0:T(8,128)(2,1)S(1)} %shard_map.96.n0_ref), channel_id=1, source_target_pairs={{0,8},{1,9},{2,10},{3,11},{4,12},{5,13},{6,14},{7,15},{8,16},{9,17... | collective-permute-start | bytes 1572872 | tf_op jit(solution)/shard_map/ppermute | solution.py:301
  103.2 16.8 %copy-start.6 = (bf16[8,512,256]{2,1,0:T(8,128)(2,1)S(1)}, bf16[8,512,256]{2,1,0:T(8,128)(2,1)}, u32[]{:S(2)}) copy-start(bf16[8,512,256]{2,1,0:T(8,128)(2,1)} %shard_map.97) | copy-start | bytes 6291460
  104.5 6.3 %collective-permute-start.18 = (bf16[256,256]{1,0:T(8,128)(2,1)S(1)}, bf16[256,256]{1,0:T(8,128)(2,1)S(1)}, u32[]{:S(2)}, u32[]{:S(2)}) collective-permute-start(bf16[256,256]{1,0:T(8,128)(2,1)S(1)} %get-tuple-element.32), channel_id=1, source_target_pairs={{0,1},{1,2},{2,3},{3,4},{4,5},{5,6},{6,7},{7,0},{8,9},{9,10},{10,1... | collective-permute-start | bytes 393224 | tf_op jit(solution)/shard_map/ppermute | solution.py:315
  104.6 6.2 %collective-permute-start.22 = (bf16[256,256]{1,0:T(8,128)(2,1)S(1)}, bf16[256,256]{1,0:T(8,128)(2,1)S(1)}, u32[]{:S(2)}, u32[]{:S(2)}) collective-permute-start(bf16[256,256]{1,0:T(8,128)(2,1)S(1)} %get-tuple-element.33), channel_id=1, source_target_pairs={{0,7},{1,0},{2,1},{3,2},{4,3},{5,4},{6,5},{7,6},{8,15},{9,8},{10,9... | collective-permute-start | bytes 393224 | tf_op jit(solution)/shard_map/ppermute | solution.py:315
  111.9 8.1 %collective-permute-start.19 = (bf16[512,256]{1,0:T(8,128)(2,1)S(1)}, bf16[512,256]{1,0:T(8,128)(2,1)S(1)}, u32[]{:S(2)}, u32[]{:S(2)}) collective-permute-start(bf16[512,256]{1,0:T(8,128)(2,1)S(1)} %pad_maximum_fusion), channel_id=1, source_target_pairs={{0,1},{1,2},{2,3},{3,4},{4,5},{5,6},{6,7},{7,0},{8,9},{9,10},{10,1... | collective-permute-start | bytes 786440 | tf_op jit(solution)/shard_map/ppermute | solution.py:315
  112.4 9.8 %collective-permute-start.23 = (bf16[512,256]{1,0:T(8,128)(2,1)S(1)}, bf16[512,256]{1,0:T(8,128)(2,1)S(1)}, u32[]{:S(2)}, u32[]{:S(2)}) collective-permute-start(bf16[512,256]{1,0:T(8,128)(2,1)S(1)} %pad_maximum_fusion.1), channel_id=1, source_target_pairs={{0,7},{1,0},{2,1},{3,2},{4,3},{5,4},{6,5},{7,6},{8,15},{9,8},{10,9... | collective-permute-start | bytes 786440 | tf_op jit(solution)/shard_map/ppermute | solution.py:315
  120.1 8.4 %collective-permute-start.20 = (bf16[512,256]{1,0:T(8,128)(2,1)S(1)}, bf16[512,256]{1,0:T(8,128)(2,1)S(1)}, u32[]{:S(2)}, u32[]{:S(2)}) collective-permute-start(bf16[512,256]{1,0:T(8,128)(2,1)S(1)} %fusion.2), channel_id=1, source_target_pairs={{0,1},{1,2},{2,3},{3,4},{4,5},{5,6},{6,7},{7,0},{8,9},{9,10},{10,1... | collective-permute-start | bytes 786440 | tf_op jit(solution)/shard_map/ppermute | solution.py:315
  128.6 6.5 %collective-permute-start.24 = (bf16[512,256]{1,0:T(8,128)(2,1)S(1)}, bf16[512,256]{1,0:T(8,128)(2,1)S(1)}, u32[]{:S(2)}, u32[]{:S(2)}) collective-permute-start(bf16[512,256]{1,0:T(8,128)(2,1)S(1)} %get-tuple-element.29), channel_id=1, source_target_pairs={{0,7},{1,0},{2,1},{3,2},{4,3},{5,4},{6,5},{7,6},{8,15},{9,8},{10,9... | collective-permute-start | bytes 786440 | tf_op jit(solution)/shard_map/ppermute | solution.py:315
  130.7 7.7 %collective-permute-start.21 = (bf16[512,256]{1,0:T(8,128)(2,1)S(1)}, bf16[512,256]{1,0:T(8,128)(2,1)S(1)}, u32[]{:S(2)}, u32[]{:S(2)}) collective-permute-start(bf16[512,256]{1,0:T(8,128)(2,1)S(1)} %get-tuple-element.28), channel_id=1, source_target_pairs={{0,1},{1,2},{2,3},{3,4},{4,5},{5,6},{6,7},{7,0},{8,9},{9,10},{10,1... | collective-permute-start | bytes 786440 | tf_op jit(solution)/shard_map/ppermute | solution.py:315
  135.1 7.2 %collective-permute-start.25 = (bf16[512,256]{1,0:T(8,128)(2,1)S(1)}, bf16[512,256]{1,0:T(8,128)(2,1)S(1)}, u32[]{:S(2)}, u32[]{:S(2)}) collective-permute-start(bf16[512,256]{1,0:T(8,128)(2,1)S(1)} %fusion.1), channel_id=1, source_target_pairs={{0,7},{1,0},{2,1},{3,2},{4,3},{5,4},{6,5},{7,6},{8,15},{9,8},{10,9... | collective-permute-start | bytes 786440 | tf_op jit(solution)/shard_map/ppermute | solution.py:315
  (6 other events, 24.4 us)

commit v2 on v1

--- a/solution.py
+++ b/solution.py
@@ -75,7 +75,10 @@
     bc = conv(bbuf, bc_ref, rim[:, width:], wbc_ref)
     bc_out[...] = bc
     dt = dt_ref[...]
-    steps = -rate_ref[...] * dt
+    own_row = lax.broadcasted_iota(jnp.int32, (dt.shape[0],) * 2, 0)
+    own_row = own_row == lax.broadcasted_iota(jnp.int32, own_row.shape, 1)
+    rate = jnp.sum(jnp.where(own_row, rate_ref[...], 0.0), 1, keepdims=True)
+    steps = -rate * dt
     before = (
         lax.broadcasted_iota(jnp.int32, (SPAN, SPAN), 0)
         <= lax.broadcasted_iota(jnp.int32, (SPAN, SPAN), 1)
@@ -161,7 +164,6 @@
 ):
     core = at_ref[1]
     state, half = mine_ref.shape
-    rows = bc_ref.shape[0]
     mine, theirs = mine_ref[...].astype(F32), theirs_ref[...].astype(F32)
     left = jnp.where(core == 0, mine, theirs)
     right = jnp.where(core == 0, theirs, mine)
@@ -169,9 +171,8 @@
     other = other_ref[...]
     after = decay_of(other, state) * prior + other[:state].astype(F32)
     incoming = jnp.where(core == 1, after, prior)
-    ss = jnp.zeros(ss_ref.shape[:1] + (SPAN,), F32)
     ones = jnp.ones((8, out_ref.shape[1]), F32)
-    for n, s in enumerate(range(0, rows, SPAN)):
+    for n, s in enumerate(range(0, bc_ref.shape[0], SPAN)):
         start = incoming if n == 0 else incoming * e0_ref[0:1]
         y = y_ref[s : s + SPAN] + dot(bc_ref[s : s + SPAN, state:], start.astype(BF16))
         gated = y * gate_ref[s : s + SPAN]
@@ -179,33 +180,60 @@
         ss_ref[:, s : s + SPAN] = dot(ones, gated * gated, ((1,), (1,)), EXACT)
 
 
+def part_order(px, core):
+    return [2 * px + core, 2 * px + 1 - core, 2 * (1 - px) + core, 2 * (1 - px) + 1 - core]
+
+
+def ahead_kernel(at_ref, *refs):
+    out_ref = refs[-1]
+    feats = out_ref.shape[3]
+    for y, w_ref in enumerate(refs[:-1]):
+        for j in range(out_ref.shape[1]):
+            out_ref[y, j] = w_ref[:, j * feats : (j + 1) * feats]
+
+
+def sort_kernel(at_ref, one_ref, two_ref, three_ref, all_ref, low_ref, high_ref):
+    half = low_ref.shape[2]
+    for d, ref in enumerate((one_ref, two_ref, three_ref)):
+        piece = ref[0]
+        all_ref[d] = piece
+        low_ref[d] = piece[:, :half]
+        high_ref[d] = piece[:, half:]
+
+
 def norm_kernel(group_width, gated_ref, gain_ref, s0_ref, s1_ref, s2_ref, s3_ref, out_ref):
     mean_sq = (s0_ref[...] + s1_ref[...] + s2_ref[...] + s3_ref[...]) / group_width
-    scale = spread(lax.rsqrt(mean_sq + norm_eps)[0:1], out_ref.shape[1])
-    out_ref[...] = (gated_ref[...] * scale * gain_ref[...]).astype(BF16)
-
-
-def project_kernel(
-    at_ref, n0_ref, n1_ref, n2_ref, n3_ref, w0_ref, w1_ref, w2_ref, w3_ref, v1_ref, v2_ref, v3_ref, out_ref
-):
-    core = at_ref[1]
-    half = w1_ref.shape[0]
-    mine = pl.ds(pl.multiple_of(core * half, half), half)
-    theirs = pl.ds(pl.multiple_of((1 - core) * half, half), half)
-    total = dot(n0_ref[...], w0_ref[...])
-    for n, w, v in ((n1_ref, w1_ref, v1_ref), (n2_ref, w2_ref, v2_ref), (n3_ref, w3_ref, v3_ref)):
-        total = total + dot(n[:, mine], w[...])
-        total = total + dot(n[:, theirs], v[...])
-    out_ref[0] = total.astype(BF16)
-
-
-def call(body, at, ins, outs, scratch=(), specs=None, grid=(1,), out_specs=None, flops=0):
+    scale = spread(lax.rsqrt(mean_sq + norm_eps)[0:1], 128)
+    for k in range(0, out_ref.shape[1], 128):
+        piece = gated_ref[:, k : k + 128] * scale * gain_ref[:, k : k + 128]
+        out_ref[:, k : k + 128] = piece.astype(BF16)
+
+
+def project_kernel(at_ref, n0_ref, n1_ref, low_ref, high_ref, n3_ref, w0_ref, *refs):
+    pieces, out_refs = refs[:6], refs[6:]
+    part = n0_ref.shape[1] // 4
+    rows, weights = [n0_ref[...]], [w0_ref[...]]
+    for d, n_refs in enumerate(((n1_ref,), (low_ref, high_ref), (n3_ref,))):
+        for p in part_order(at_ref[4], at_ref[1]):
+            cols = pl.ds(pl.multiple_of(p * part, part), part)
+            rows.append(jnp.concatenate([n[:, cols] for n in n_refs], 0))
+        weights += [p[d, 0] for p in pieces]
+    total = dot(jnp.concatenate(rows, 1), jnp.concatenate(weights, 0))
+    if len(out_refs) == 1:
+        out_refs[0][0] = total.astype(BF16)
+    else:
+        mid = out_refs[0].shape[0]
+        out_refs[0][...] = total[:mid].astype(BF16)
+        out_refs[1][...] = total[mid:].astype(BF16)
+
+
+def call(body, at, ins, outs, scratch=(), specs=None, grid=(1,), out_specs=None, flops=0, vmem=48):
     full = lambda s: pl.BlockSpec(s, lambda *_, n=len(s): (0,) * n)
     specs = specs or {}
     in_specs = [specs.get(k) or full(a.shape) for k, a in enumerate(ins)]
     kwargs = dict(
         out_shape=outs,
-        compiler_params=pltpu.CompilerParams(vmem_limit_bytes=48 << 20),
+        compiler_params=pltpu.CompilerParams(vmem_limit_bytes=vmem << 20),
         cost_estimate=pl.CostEstimate(
             flops=flops,
             bytes_accessed=sum(a.size * a.dtype.itemsize for a in (*ins, *outs)),
@@ -238,31 +266,36 @@
     state = cols // 2
     head_at, seq_at = lax.axis_index("head"), lax.axis_index("seq")
     group, core, y_at, z_at = head_at // QUAD, seq_at % CORES, head_at // NZ, head_at % NZ
-    at = jnp.stack([group, core, y_at, z_at]).astype(jnp.int32)
+    at = jnp.stack([group, core, y_at, z_at, seq_at // CORES % 2]).astype(jnp.int32)
 
     edge = lax.dynamic_slice(bc, (rows - RIM, group * cols), (RIM, cols))
-    rim = lax.ppermute(
-        jnp.concatenate([x[rows - RIM :], edge], 1), "seq", [(s, s + 1) for s in range(7)]
-    )
+    edges = jnp.concatenate([x[rows - RIM :], edge], 1)
+    rim = lax.ppermute(edges, "seq", [(s, s + 1) for s in range(7)])
 
     quarter = w_out.shape[1] // NY
-    half_k = width // CORES
-    w_mine = [
-        lax.ppermute(
-            lax.dynamic_slice(w_out, (core * half_k, (y_at + d) % NY * quarter), (half_k, quarter)),
-            "head",
-            y_route(d),
-        )
-        for d in range(1, NY)
-    ]
-    w_theirs = [lax.ppermute(w, "seq", CORE_SWAP) for w in w_mine]
+    feats = quarter // NZ
+    part_k = width // 4
+    at_late, _ = lax.optimization_barrier((at, edges))
+    [ahead] = call(
+        ahead_kernel,
+        at_late,
+        [w_out] * NY,
+        [like((NY, NZ, part_k, feats), BF16)],
+        specs={
+            y: pl.BlockSpec((part_k, quarter), lambda i, s, y=y: (2 * s[4] + s[1], y))
+            for y in range(NY)
+        },
+    )
+    rim, ahead = lax.optimization_barrier((rim, ahead))
+    columns = [[y * NZ + z for y in range(NY)] for z in range(NZ)]
+    arrived = lax.all_to_all(ahead, "head", 0, 0, tiled=True, axis_index_groups=columns)
 
     block = pl.BlockSpec((rows, cols), lambda i, s: (0, s[0]))
     wblock = pl.BlockSpec((4, cols), lambda i, s: (0, s[0]))
     payload, xs, bc_conv, s0, grow, e0 = call(
         state_kernel,
         at,
-        [x, bc, rim, wx, wbc, dt, rate[:, None]],
+        [x, bc, rim, wx, wbc, dt, rate[None, :]],
         [
             like((state + 16, width), BF16),
             like((rows, width), BF16),
@@ -272,7 +305,7 @@
             like((8, width), F32),
         ],
         scratch=[pltpu.VMEM((rows + 8, width), F32), pltpu.VMEM((rows + 8, cols), F32)],
-        specs={1: block, 4: wblock},
+        specs={1: block, 4: wblock}
     )
     other = lax.ppermute(payload, "seq", CORE_SWAP)
     [chip] = call(chip_kernel, at, [payload, other], [like((state + 16, width // 2), BF16)])
@@ -285,6 +318,7 @@
     )
     [mine] = call(prefix_kernel, None, befores, [like((state, width // 2), BF16)])
     theirs = lax.ppermute(mine, "seq", CORE_SWAP)
+
     gated, ss = call(
         gate_kernel,
         at,
@@ -298,29 +332,70 @@
         [gated, gain[None, :], ss, *more],
         [like((rows, width), BF16)],
     )
-    peers = [lax.ppermute(normed, "head", y_route(d)) for d in range(1, NY)]
-    feats = quarter // NZ
-    in_quarter = pl.BlockSpec((half_k, feats), lambda i, s: (0, (s[3] + i) % NZ))
-    in_whole = pl.BlockSpec((width, feats), lambda i, s: (0, s[2] * NZ + (s[3] + i) % NZ))
-    [parts] = call(
-        project_kernel,
-        at,
-        [normed, *peers, w_out, *w_mine, *w_theirs],
-        [like((NZ, rows, feats), BF16)],
-        specs={4: in_whole, **{k: in_quarter for k in range(5, 11)}},
-        grid=(NZ,),
-        out_specs=[pl.BlockSpec((1, rows, feats), lambda i, s: (i, 0, 0))],
-        flops=2 * rows * width * quarter * NY,
-    )
+    mid = rows // 2
+    near_up, near_down = (lax.ppermute(normed, "head", y_route(d)) for d in (1, -1))
+    far_low = lax.ppermute(near_up[:mid], "head", y_route(1))
+    far_high = lax.ppermute(near_down[mid:], "head", y_route(-1))
+    peers = [near_up, far_low, far_high, near_down]
+
+    at_then, _ = lax.optimization_barrier((at, ss))
+    arrived_from = lambda d: pl.BlockSpec(
+        (1, NZ, part_k, feats), lambda i, s: ((s[2] + NY - d) % NY, 0, 0, 0)
+    )
+    pair = (NY - 1, NZ, part_k // 2, feats)
+    own, low, high = call(
+        sort_kernel,
+        at_then,
+        [arrived] * (NY - 1),
+        [like((NY - 1, NZ, part_k, feats), BF16), like(pair, BF16), like(pair, BF16)],
+        specs={d - 1: arrived_from(d) for d in range(1, NY)},
+    )
+    ring = NX * CORES
+    x_low = lax.ppermute(low, "seq", [(s, (s + CORES) % ring) for s in range(ring)])
+    x_high = lax.ppermute(high, "seq", [(s, (s - CORES) % ring) for s in range(ring)])
+    own_late, _ = lax.optimization_barrier((own, normed))
+    swap = lambda v: lax.ppermute(v, "seq", CORE_SWAP)
+    pieces = [own, swap(own_late), x_low, x_high, swap(x_low), swap(x_high)]
+
+    def project(order, after):
+        at_then, _ = lax.optimization_barrier((at, after))
+        turn = lambda i: order[0] + sum(
+            (b - a) * (i >= k + 1).astype(jnp.int32) for k, (a, b) in enumerate(zip(order, order[1:]))
+        )
+        piece = lambda v: pl.BlockSpec(
+            (NY - 1, 1, v.shape[2], feats), lambda i, s: (0, (s[3] + turn(i)) % NZ, 0, 0)
+        )
+        own = pl.BlockSpec((width, feats), lambda i, s: (0, s[2] * NZ + (s[3] + turn(i)) % NZ))
+        if len(order) == 1:
+            outs, out_specs = [like((rows // 2, feats), BF16)] * 2, None
+        else:
+            outs = [like((len(order), rows, feats), BF16)]
+            out_specs = [pl.BlockSpec((1, rows, feats), lambda i, s: (i, 0, 0))]
+        return call(
+            project_kernel,
+            at_then,
+            [normed, *peers, w_out, *pieces],
+            outs,
+            specs={5: own, **{6 + k: piece(v) for k, v in enumerate(pieces)}},
+            grid=(len(order),),
+            out_specs=out_specs,
+            flops=2 * rows * width * NY * feats * len(order),
+        )
+
     send = lambda v, d: lax.ppermute(v, "head", z_route(d))
-    mid = rows // 2
-    up, down = send(parts[4, :mid], 1), send(parts[4, mid:], -1)
     add = lambda a, b: (a.astype(F32) + b.astype(F32)).astype(BF16)
-    up = send(jnp.concatenate([add(parts[3, :mid], up), parts[3, mid:]], 0), 1)
-    down = send(jnp.concatenate([parts[5, :mid], add(parts[5, mid:], down)], 0), -1)
-    up, down = send(add(parts[2], up), 1), send(add(parts[6], down), -1)
-    up, down = send(add(parts[1], up), 1), send(add(parts[7], down), -1)
-    return (parts[0].astype(F32) + up.astype(F32) + down.astype(F32)).astype(BF16).T
+    far_up, far_down = project((4,), normed)
+    up, down = send(far_up, 1), send(far_down, -1)
+    [third] = project((3, 5), far_up)
+    [second] = project((2, 6), (up, down))
+    up = send(jnp.concatenate([add(third[0, :mid], up), third[0, mid:]], 0), 1)
+    down = send(jnp.concatenate([third[1, :mid], add(third[1, mid:], down)], 0), -1)
+    [first] = project((1, 7), (up, down))
+    up, down = send(add(second[0], up), 1), send(add(second[1], down), -1)
+    own_halves = project((0,), (up, down))
+    up, down = send(add(first[0], up), 1), send(add(first[1], down), -1)
+    own = jnp.concatenate(own_halves, 0)
+    return (own.astype(F32) + up.astype(F32) + down.astype(F32)).astype(BF16).T
 
 
 def solution(mesh):

time: 145 us -> 119 us (0.82)
  waiting for transfers between devices: 64.8 us -> 41.7 us
  Pallas kernels: 19.9 us -> 26.9 us
  local copies, waits for them, and re-layouts: 9.9 us -> 4.93 us
  starting transfers between devices: 46.8 us -> 43.1 us
    ppermute x8, waiting for transfers between devices: 22.2 us -> 7.57 us  [on_device(): send = lambda v, d: lax.ppermute(v, 'head', z_route(d))]
    ppermute x3, starting transfers between devices: 14.9 us -> 4.42 us  [on_device(): befores = [lax.ppermute(chip, 'seq', x_route(d)) for d in (1, 2, 3)]]
    ppermute x10, waiting for transfers between devices: 31.3 us -> 23.3 us  [the longest x1 14.2 us: on_device(): lax.ppermute(low, 'seq', [(s, (s + CORES) % ring) for s in range(ring)])]
    pallas_call x4 -> x10, Pallas kernels: 17.4 us -> 24.9 us  [call(): pl.pallas_call(body, grid_spec=pltpu.PrefetchScalarGridSpec(num_scalar_pr...]
    all_to_all x0 -> x1, starting transfers between devices: none -> 4.61 us  [on_device(): lax.all_to_all(ahead, 'head', 0, 0, tiled=True, axis_index_groups=columns)]
    ppermute x3, waiting for transfers between devices: 7.25 us -> 2.73 us  [on_device(): more = [lax.ppermute(ss, 'head', quad_route(d)) for d in range(1, QUAD)]]
    ppermute x3, waiting for transfers between devices: 2.57 us -> 6.86 us  [on_device(): befores = [lax.ppermute(chip, 'seq', x_route(d)) for d in (1, 2, 3)]]
    dynamic_slice x1 -> x0, local copies, waits for them, and re-layouts: 3.64 us -> none  [on_device(): lax.dynamic_slice(w_out, (core * half_k, (y_at + d) % NY * quarter), (hal...]
  transfers between devices with their start and end apart: 26 -> 27, of which waited for: 14 -> 14; matrix products, arithmetic and copies ran while one was open for 1% -> 0% of each run, Pallas kernels for 7% -> 20%
where the time goes in v2:
time: 119 us; the launch traced here: 118 us
  starting transfers between devices  43.1 us (36%)
  waiting for transfers between devices  41.7 us (35%)
  Pallas kernels  26.9 us (23%)
  local copies, waits for them, and re-layouts  4.93 us (4%)
    pallas_call x10, Pallas kernels, call(): pl.pallas_call(body, grid_spec=pltpu.PrefetchScalarGridSpec(num_scalar_pr...  24.9 us
    ppermute x8, starting transfers between devices, on_device(): send = lambda v, d: lax.ppermute(v, 'head', z_route(d))  15 us
    ppermute x1, waiting for transfers between devices, on_device(): lax.ppermute(low, 'seq', [(s, (s + CORES) % ring) for s in range(ring)])  14.2 us
    ppermute x8, waiting for transfers between devices, on_device(): send = lambda v, d: lax.ppermute(v, 'head', z_route(d))  7.57 us
    ppermute x3, waiting for transfers between devices, on_device(): befores = [lax.ppermute(chip, 'seq', x_route(d)) for d in (1, 2, 3)]  6.86 us
    ppermute x1, waiting for transfers between devices, on_device(): far_low = lax.ppermute(near_up[:mid], 'head', y_route(1))  6.62 us
    ppermute x3, starting transfers between devices, on_device(): more = [lax.ppermute(ss, 'head', quad_route(d)) for d in range(1, QUAD)]  6.21 us
    all_to_all x1, starting transfers between devices, on_device(): lax.all_to_all(ahead, 'head', 0, 0, tiled=True, axis_index_groups=columns)  4.61 us
  transfers between devices with their start and end apart: 27, of which 14 were waited for; matrix products, arithmetic and copies ran while one was open for 0% of the time, Pallas kernels for 20%

profile of v2, /device:TPU:4, one launch (start us, length us, event | category | flops | bytes accessed | tf_op | source)
XLA Modules:
  0.0 117.5 jit_solution(6474694706549765301)
XLA Ops:
  1.4 1.9 %collective-permute-start = (bf16[16,1024]{1,0:T(8,128)(2,1)S(1)}, bf16[16,1024]{1,0:T(8,128)(2,1)S(1)}, u32[]{:S(2)}, u32[]{:S(2)}) collective-permute-start(bf16[16,1024]{1,0:T(8,128)(2,1)S(1)} %pad_maximum_fusion.2), channel_id=1, source_target_pairs={{0,32},{32,64},{64,96},{96,128},{128,160},{160,192},{192,224},{1,3... | collective-permute-start | bytes 98312 | tf_op jit(solution)/shard_map/ppermute | solution.py:273
  3.5 2.2 %shard_map.91 = bf16[4,8,128,256]{3,2,1,0:T(8,128)(2,1)S(1)} custom-call(s32[5]{0:T(128)S(1)} %stack.23.at_ref, bf16[512,8192]{1,0:T(8,128)(2,1)} %w0_ref.9, bf16[512,8192]{1,0:T(8,128)(2,1)} %w0_ref.9, bf16[512,8192]{1,0:T(8,128)(2,1)} %w0_ref.9, bf16[512,8192]{1,0:T(8,128)(2,1)} %w0_ref.9), custom_call_target="tpu_custom_call" | custom-call | bytes 35651584 | tf_op jit(solution)/shard_map/pallas_call | solution.py:249
  7.1 4.6 %all-to-all-start = ((bf16[4,8,128,256]{3,2,1,0:T(8,128)(2,1)}), bf16[4,8,128,256]{3,2,1,0:T(8,128)(2,1)S(1)}, u32[]{:S(2)}, u32[]{:S(2)}) async-start(bf16[4,8,128,256]{3,2,1,0:T(8,128)(2,1)} %copy-done.1), calls=%async_computation | async-start | bytes 4194304 | tf_op jit(solution)/shard_map/all_to_all | solution.py:291
  11.7 5.1 %shard_map.92 = (bf16[272,512]{1,0:T(8,128)(2,1)S(1)}, bf16[512,512]{1,0:T(8,128)(2,1)S(1)}, bf16[512,512]{1,0:T(8,128)(2,1)S(1)}, bf16[256,512]{1,0:T(8,128)(2,...) custom-call(s32[5]{0:T(128)S(1)} %stack.23.at_ref, bf16[512,512]{1,0:T(8,128)(2,1)S(1)} %copy-done.2, ...), custom_call_target="tpu_custom_call" | custom-call | bytes 6426656 | tf_op jit(solution)/shard_map/pallas_call | solution.py:249
  19.8 2.5 %collective-permute-start.2 = (bf16[272,256]{1,0:T(8,128)(2,1)S(1)}, bf16[272,256]{1,0:T(8,128)(2,1)S(1)}, u32[]{:S(2)}, u32[]{:S(2)}) collective-permute-start(bf16[272,256]{1,0:T(8,128)(2,1)S(1)} %shard_map.93), channel_id=1, source_target_pairs={{0,64},{32,96},{64,128},{96,160},{128,192},{160,224},{1,65},{33,97... | collective-permute-start | bytes 417800 | tf_op jit(solution)/shard_map/ppermute | solution.py:312
  24.2 3.4 %collective-permute-done.2.one_ref = bf16[272,256]{1,0:T(8,128)(2,1)S(1)} collective-permute-done((bf16[272,256]{1,0:T(8,128)(2,1)S(1)}, bf16[272,256]{1,0:T(8,128)(2,1)S(1)}, u32[]{:S(2)}, u32[]{:S(2)}) %collective-permute-start.2) | collective-permute-done | bytes 139296 | tf_op jit(solution)/shard_map/ppermute | solution.py:312
  27.6 3.5 %collective-permute-done.3.two_ref = bf16[272,256]{1,0:T(8,128)(2,1)S(1)} collective-permute-done((bf16[272,256]{1,0:T(8,128)(2,1)S(1)}, bf16[272,256]{1,0:T(8,128)(2,1)S(1)}, u32[]{:S(2)}, u32[]{:S(2)}) %collective-permute-start.3) | collective-permute-done | bytes 139296 | tf_op jit(solution)/shard_map/ppermute | solution.py:312
  31.3 1.4 %shard_map.95 = (f32[512,512]{1,0:T(8,128)S(1)}, f32[512,512]{1,0:T(8,128)S(1)}) custom-call(bf16[512,512]{1,0:T(8,128)(2,1)S(1)} %get-tuple-element.36.xs_ref, bf16[512,512]{1,0:T(8,128)(2,1)S(1)} %get-tuple-element.35.bc_ref, bf16[256,512]{1,0:T(8,128)(2,1)S(1)} %get-tuple-element.37.s0_ref, f32[8,512]{1,0:T(8,128)S(1)} %get-tuple-element.38.ec_ref, ...), custom_call_target="tpu_custom_call" | custom-call | bytes 3948544 | tf_op jit(solution)/shard_map/pallas_call | solution.py:246
  32.7 1.8 %shard_map.96 = (f32[512,512]{1,0:T(8,128)S(1)}, f32[8,512]{1,0:T(8,128)S(1)}) custom-call(s32[5]{0:T(128)S(1)} %stack.23.at_ref, bf16[256,256]{1,0:T(8,128)(2,1)S(1)} %shard_map.94.mine_ref, bf16[256,256]{1,0:T(8,128)(2,1)S(1)} %collective-permute-done.5.theirs_ref, bf16[272,512]{1,0:T(8,128)(2,1)S(1)} %collective-permute-done.1.other_ref, ...), custom_call_target="tpu_custom_call" | custom-call | bytes 4243456 | tf_op jit(solution)/shard_map/pallas_call | solution.py:249
  34.5 1.9 %collective-permute-start.6 = (f32[8,512]{1,0:T(8,128)S(1)}, f32[8,512]{1,0:T(8,128)S(1)}, u32[]{:S(2)}, u32[]{:S(2)}) collective-permute-start(f32[8,512]{1,0:T(8,128)S(1)} %get-tuple-element.43.s0_ref), channel_id=1, source_target_pairs={{0,1},{1,2},{2,3},{3,0},{4,5},{5,6},{6,7},{7,4},{8,9},{9,10},{10,1... | collective-permute-start | bytes 49160 | tf_op jit(solution)/shard_map/ppermute | solution.py:328
  36.5 3.3 %collective-permute-start.7 = (f32[8,512]{1,0:T(8,128)S(1)}, f32[8,512]{1,0:T(8,128)S(1)}, u32[]{:S(2)}, u32[]{:S(2)}) collective-permute-start(f32[8,512]{1,0:T(8,128)S(1)} %get-tuple-element.43.s0_ref), channel_id=1, source_target_pairs={{0,2},{1,3},{2,0},{3,1},{4,6},{5,7},{6,4},{7,5},{8,10},{9,11},{10,... | collective-permute-start | bytes 49160 | tf_op jit(solution)/shard_map/ppermute | solution.py:328
  41.5 2.0 %collective-permute-done.8.s3_ref = f32[8,512]{1,0:T(8,128)S(1)} collective-permute-done((f32[8,512]{1,0:T(8,128)S(1)}, f32[8,512]{1,0:T(8,128)S(1)}, u32[]{:S(2)}, u32[]{:S(2)}) %collective-permute-start.8) | collective-permute-done | bytes 16416 | tf_op jit(solution)/shard_map/ppermute | solution.py:328
  44.9 3.0 %collective-permute-start.14 = (bf16[3,8,64,256]{3,2,1,0:T(8,128)(2,1)S(1)}, bf16[3,8,64,256]{3,2,1,0:T(8,128)(2,1)S(1)}, u32[]{:S(2)}, u32[]{:S(2)}) collective-permute-start(bf16[3,8,64,256]{3,2,1,0:T(8,128)(2,1)S(1)} %get-tuple-element.49), channel_id=1, source_target_pairs={{0,64},{32,96},{64,128},{96,160},{128,192},{160,224},{192,0},{224,... | collective-permute-start | bytes 2359304 | tf_op jit(solution)/shard_map/ppermute | solution.py:354
  47.8 1.8 %collective-permute-start.9 = (bf16[512,512]{1,0:T(8,128)(2,1)S(1)}, bf16[512,512]{1,0:T(8,128)(2,1)S(1)}, u32[]{:S(2)}, u32[]{:S(2)}) collective-permute-start(bf16[512,512]{1,0:T(8,128)(2,1)S(1)} %shard_map.97.n0_ref), channel_id=1, source_target_pairs={{0,8},{1,9},{2,10},{3,11},{4,12},{5,13},{6,14},{7,15},{8,16},{9,17... | collective-permute-start | bytes 1572872 | tf_op jit(solution)/shard_map/ppermute | solution.py:336
  49.6 1.5 %collective-permute-start.11 = (bf16[512,512]{1,0:T(8,128)(2,1)S(1)}, bf16[512,512]{1,0:T(8,128)(2,1)S(1)}, u32[]{:S(2)}, u32[]{:S(2)}) collective-permute-start(bf16[512,512]{1,0:T(8,128)(2,1)S(1)} %shard_map.97.n0_ref), channel_id=1, source_target_pairs={{0,24},{1,25},{2,26},{3,27},{4,28},{5,29},{6,30},{7,31},{8,0},{9,1... | collective-permute-start | bytes 1572872 | tf_op jit(solution)/shard_map/ppermute | solution.py:336
  51.1 14.2 %collective-permute-done.14.refs_2_ = bf16[3,8,64,256]{3,2,1,0:T(8,128)(2,1)S(1)} collective-permute-done((bf16[3,8,64,256]{3,2,1,0:T(8,128)(2,1)S(1)}, bf16[3,8,64,256]{3,2,1,0:T(8,128)(2,1)S(1)}, u32[]{:S(2)}, u32[]{:S(2)}) %collective-permute-start.14) | collective-permute-done | bytes 786464 | tf_op jit(solution)/shard_map/ppermute | solution.py:354
  65.2 2.2 %collective-permute-done.15.refs_3_ = bf16[3,8,64,256]{3,2,1,0:T(8,128)(2,1)S(1)} collective-permute-done((bf16[3,8,64,256]{3,2,1,0:T(8,128)(2,1)S(1)}, bf16[3,8,64,256]{3,2,1,0:T(8,128)(2,1)S(1)}, u32[]{:S(2)}, u32[]{:S(2)}) %collective-permute-start.15) | collective-permute-done | bytes 786464 | tf_op jit(solution)/shard_map/ppermute | solution.py:355
  67.5 1.8 %collective-permute-start.10 = (bf16[256,512]{1,0:T(8,128)(2,1)S(1)}, bf16[256,512]{1,0:T(8,128)(2,1)S(1)}, u32[]{:S(2)}, u32[]{:S(2)}) collective-permute-start(bf16[256,512]{1,0:T(8,128)(2,1)S(1)} %slice.44), channel_id=1, source_target_pairs={{0,8},{1,9},{2,10},{3,11},{4,12},{5,13},{6,14},{7,15},{8,16},{9,17... | collective-permute-start | bytes 786440 | tf_op jit(solution)/shard_map/ppermute | solution.py:337
  69.3 1.5 %collective-permute-start.12 = (bf16[256,512]{1,0:T(8,128)(2,1)S(1)}, bf16[256,512]{1,0:T(8,128)(2,1)S(1)}, u32[]{:S(2)}, u32[]{:S(2)}) collective-permute-start(bf16[256,512]{1,0:T(8,128)(2,1)S(1)} %slice.45), channel_id=1, source_target_pairs={{0,24},{1,25},{2,26},{3,27},{4,28},{5,29},{6,30},{7,31},{8,0},{9,1... | collective-permute-start | bytes 786440 | tf_op jit(solution)/shard_map/ppermute | solution.py:338
  70.9 6.6 %collective-permute-done.10.low_ref = bf16[256,512]{1,0:T(8,128)(2,1)S(1)} collective-permute-done((bf16[256,512]{1,0:T(8,128)(2,1)S(1)}, bf16[256,512]{1,0:T(8,128)(2,1)S(1)}, u32[]{:S(2)}, u32[]{:S(2)}) %collective-permute-start.10) | collective-permute-done | bytes 262176 | tf_op jit(solution)/shard_map/ppermute | solution.py:337
  79.0 2.4 %shard_map.99 = (bf16[256,256]{1,0:T(8,128)(2,1)S(1)}, bf16[256,256]{1,0:T(8,128)(2,1)S(1)}) custom-call(s32[5]{0:T(128)S(1)} %stack.23.at_ref, bf16[512,512]{1,0:T(8,128)(2,1)S(1)} %shard_map.97.n0_ref, bf16[512,512]{1,0:T(8,128)(2,1)S(1)} %collective-permute-done.9.n1_ref, bf16[256,512]{1,0:T(8,128)(2,1)S(1)} %collective-permute-done.10.low_ref, ...), custom_call_target="tpu_custom_call" | custom-call | flops 536870912 | bytes 17039360 | tf_op jit(solution)/shard_map/pallas_call | solution.py:249
  81.5 5.0 %collective-permute-start.19 = (bf16[256,256]{1,0:T(8,128)(2,1)S(1)}, bf16[256,256]{1,0:T(8,128)(2,1)S(1)}, u32[]{:S(2)}, u32[]{:S(2)}) collective-permute-start(bf16[256,256]{1,0:T(8,128)(2,1)S(1)} %get-tuple-element.52), channel_id=1, source_target_pairs={{0,7},{1,0},{2,1},{3,2},{4,3},{5,4},{6,5},{7,6},{8,15},{9,8},{10,9... | collective-permute-start | bytes 393224 | tf_op jit(solution)/shard_map/ppermute | solution.py:385
  86.5 3.2 %shard_map.101 = bf16[2,512,256]{2,1,0:T(8,128)(2,1)S(1)} custom-call(s32[5]{0:T(128)S(1)} %stack.23.at_ref, bf16[512,512]{1,0:T(8,128)(2,1)S(1)} %shard_map.97.n0_ref, bf16[512,512]{1,0:T(8,128)(2,1)S(1)} %collective-permute-done.9.n1_ref, bf16[256,512]{1,0:T(8,128)(2,1)S(1)} %collective-permute-done.10.low_ref, ...), custom_call_target="tpu_custom_call" | custom-call | flops 1073741824 | bytes 17301504 | tf_op jit(solution)/shard_map/pallas_call | solution.py:249
  89.9 3.0 %collective-permute-start.22 = (bf16[512,256]{1,0:T(8,128)(2,1)S(1)}, bf16[512,256]{1,0:T(8,128)(2,1)S(1)}, u32[]{:S(2)}, u32[]{:S(2)}) collective-permute-start(bf16[512,256]{1,0:T(8,128)(2,1)S(1)} %pad_maximum_fusion.1), channel_id=1, source_target_pairs={{0,7},{1,0},{2,1},{3,2},{4,3},{5,4},{6,5},{7,6},{8,15},{9,8},{10,9... | collective-permute-start | bytes 786440 | tf_op jit(solution)/shard_map/ppermute | solution.py:385
  93.0 3.2 %shard_map.100 = bf16[2,512,256]{2,1,0:T(8,128)(2,1)S(1)} custom-call(s32[5]{0:T(128)S(1)} %stack.23.at_ref, bf16[512,512]{1,0:T(8,128)(2,1)S(1)} %shard_map.97.n0_ref, bf16[512,512]{1,0:T(8,128)(2,1)S(1)} %collective-permute-done.9.n1_ref, bf16[256,512]{1,0:T(8,128)(2,1)S(1)} %collective-permute-done.10.low_ref, ...), custom_call_target="tpu_custom_call" | custom-call | flops 1073741824 | bytes 17301504 | tf_op jit(solution)/shard_map/pallas_call | solution.py:249
  97.3 3.2 %collective-permute-done.20 = bf16[512,256]{1,0:T(8,128)(2,1)S(1)} collective-permute-done((bf16[512,256]{1,0:T(8,128)(2,1)S(1)}, bf16[512,256]{1,0:T(8,128)(2,1)S(1)}, u32[]{:S(2)}, u32[]{:S(2)}) %collective-permute-start.20) | collective-permute-done | bytes 262176 | tf_op jit(solution)/shard_map/ppermute | solution.py:385
  100.8 3.2 %collective-permute-start.23 = (bf16[512,256]{1,0:T(8,128)(2,1)S(1)}, bf16[512,256]{1,0:T(8,128)(2,1)S(1)}, u32[]{:S(2)}, u32[]{:S(2)}) collective-permute-start(bf16[512,256]{1,0:T(8,128)(2,1)S(1)} %get-tuple-element.62), channel_id=1, source_target_pairs={{0,7},{1,0},{2,1},{3,2},{4,3},{5,4},{6,5},{7,6},{8,15},{9,8},{10,9... | collective-permute-start | bytes 786440 | tf_op jit(solution)/shard_map/ppermute | solution.py:385
  104.0 3.2 %shard_map.103 = bf16[2,512,256]{2,1,0:T(8,128)(2,1)S(1)} custom-call(s32[5]{0:T(128)S(1)} %stack.23.at_ref, bf16[512,512]{1,0:T(8,128)(2,1)S(1)} %shard_map.97.n0_ref, bf16[512,512]{1,0:T(8,128)(2,1)S(1)} %collective-permute-done.9.n1_ref, bf16[256,512]{1,0:T(8,128)(2,1)S(1)} %collective-permute-done.10.low_ref, ...), custom_call_target="tpu_custom_call" | custom-call | flops 1073741824 | bytes 17301504 | tf_op jit(solution)/shard_map/pallas_call | solution.py:249
  107.2 1.4 %collective-permute-done.21 = bf16[512,256]{1,0:T(8,128)(2,1)S(1)} collective-permute-done((bf16[512,256]{1,0:T(8,128)(2,1)S(1)}, bf16[512,256]{1,0:T(8,128)(2,1)S(1)}, u32[]{:S(2)}, u32[]{:S(2)}) %collective-permute-start.21) | collective-permute-done | bytes 262176 | tf_op jit(solution)/shard_map/ppermute | solution.py:385
  108.8 3.5 %collective-permute-start.25 = (bf16[512,256]{1,0:T(8,128)(2,1)S(1)}, bf16[512,256]{1,0:T(8,128)(2,1)S(1)}, u32[]{:S(2)}, u32[]{:S(2)}) collective-permute-start(bf16[512,256]{1,0:T(8,128)(2,1)S(1)} %get-tuple-element.60), channel_id=1, source_target_pairs={{0,7},{1,0},{2,1},{3,2},{4,3},{5,4},{6,5},{7,6},{8,15},{9,8},{10,9... | collective-permute-start | bytes 786440 | tf_op jit(solution)/shard_map/ppermute | solution.py:385
  112.3 2.4 %shard_map.102 = (bf16[256,256]{1,0:T(8,128)(2,1)S(1)}, bf16[256,256]{1,0:T(8,128)(2,1)S(1)}) custom-call(s32[5]{0:T(128)S(1)} %stack.23.at_ref, bf16[512,512]{1,0:T(8,128)(2,1)S(1)} %shard_map.97.n0_ref, bf16[512,512]{1,0:T(8,128)(2,1)S(1)} %collective-permute-done.9.n1_ref, bf16[256,512]{1,0:T(8,128)(2,1)S(1)} %collective-permute-done.10.low_ref, ...), custom_call_target="tpu_custom_call" | custom-call | flops 536870912 | bytes 17039360 | tf_op jit(solution)/shard_map/pallas_call | solution.py:249
  114.7 1.9 %collective-permute-done.24 = bf16[512,256]{1,0:T(8,128)(2,1)S(1)} collective-permute-done((bf16[512,256]{1,0:T(8,128)(2,1)S(1)}, bf16[512,256]{1,0:T(8,128)(2,1)S(1)}, u32[]{:S(2)}, u32[]{:S(2)}) %collective-permute-start.24) | collective-permute-done | bytes 262176 | tf_op jit(solution)/shard_map/ppermute | solution.py:385
  (69 shorter events, 15.3 us)
Async XLA Ops:
  1.4 5.6 %collective-permute-start = (bf16[16,1024]{1,0:T(8,128)(2,1)S(1)}, bf16[16,1024]{1,0:T(8,128)(2,1)S(1)}, u32[]{:S(2)}, u32[]{:S(2)}) collective-permute-start(bf16[16,1024]{1,0:T(8,128)(2,1)S(1)} %pad_maximum_fusion.2), channel_id=1, source_target_pairs={{0,32},{32,64},{64,96},{96,128},{128,160},{160,192},{192,224},{1,3... | collective-permute-start | bytes 98312 | tf_op jit(solution)/shard_map/ppermute | solution.py:273
  7.1 4.6 %copy-start.6 = (bf16[4,512]{1,0:T(4,128)(2,1)S(1)}, bf16[4,512]{1,0:T(4,128)(2,1)}, u32[]{:S(2)}) copy-start(bf16[4,512]{1,0:T(4,128)(2,1)} %wx_ref.1) | copy-start | bytes 12292
  7.1 4.7 %copy-start.8 = (f32[8]{0:T(128)S(1)}, f32[8]{0:T(128)}, u32[]{:S(2)}) copy-start(f32[8]{0:T(128)} %param.13) | copy-start | bytes 100
  7.1 36.9 %all-to-all-start = ((bf16[4,8,128,256]{3,2,1,0:T(8,128)(2,1)}), bf16[4,8,128,256]{3,2,1,0:T(8,128)(2,1)S(1)}, u32[]{:S(2)}, u32[]{:S(2)}) async-start(bf16[4,8,128,256]{3,2,1,0:T(8,128)(2,1)} %copy-done.1), calls=%async_computation | async-start | bytes 4194304 | tf_op jit(solution)/shard_map/all_to_all | solution.py:291
  11.7 19.6 %copy-start.3 = (bf16[512,512]{1,0:T(8,128)(2,1)S(1)}, bf16[512,512]{1,0:T(8,128)(2,1)}, u32[]{:S(2)}) copy-start(bf16[512,512]{1,0:T(8,128)(2,1)} %z_ref.1) | copy-start | bytes 1572868
  16.9 2.3 %collective-permute-start.1 = (bf16[272,512]{1,0:T(8,128)(2,1)S(1)}, bf16[272,512]{1,0:T(8,128)(2,1)S(1)}, u32[]{:S(2)}, u32[]{:S(2)}) collective-permute-start(bf16[272,512]{1,0:T(8,128)(2,1)S(1)} %get-tuple-element.34.own_ref), channel_id=1, source_target_pairs={{0,32},{32,0},{64,96},{96,64},{128,160},{160,128},{192,224},{224,1... | collective-permute-start | bytes 835592 | tf_op jit(solution)/shard_map/ppermute | solution.py:310
  19.8 7.8 %collective-permute-start.2 = (bf16[272,256]{1,0:T(8,128)(2,1)S(1)}, bf16[272,256]{1,0:T(8,128)(2,1)S(1)}, u32[]{:S(2)}, u32[]{:S(2)}) collective-permute-start(bf16[272,256]{1,0:T(8,128)(2,1)S(1)} %shard_map.93), channel_id=1, source_target_pairs={{0,64},{32,96},{64,128},{96,160},{128,192},{160,224},{1,65},{33,97... | collective-permute-start | bytes 417800 | tf_op jit(solution)/shard_map/ppermute | solution.py:312
  22.3 8.8 %collective-permute-start.3 = (bf16[272,256]{1,0:T(8,128)(2,1)S(1)}, bf16[272,256]{1,0:T(8,128)(2,1)S(1)}, u32[]{:S(2)}, u32[]{:S(2)}) collective-permute-start(bf16[272,256]{1,0:T(8,128)(2,1)S(1)} %shard_map.93), channel_id=1, source_target_pairs={{0,128},{32,160},{64,192},{96,224},{1,129},{33,161},{65,193},{97,2... | collective-permute-start | bytes 417800 | tf_op jit(solution)/shard_map/ppermute | solution.py:312
  23.6 7.5 %collective-permute-start.4 = (bf16[272,256]{1,0:T(8,128)(2,1)S(1)}, bf16[272,256]{1,0:T(8,128)(2,1)S(1)}, u32[]{:S(2)}, u32[]{:S(2)}) collective-permute-start(bf16[272,256]{1,0:T(8,128)(2,1)S(1)} %shard_map.93), channel_id=1, source_target_pairs={{0,192},{32,224},{1,193},{33,225},{2,194},{34,226},{3,195},{35,227... | collective-permute-start | bytes 417800 | tf_op jit(solution)/shard_map/ppermute | solution.py:312
  31.2 1.5 %collective-permute-start.5 = (bf16[256,256]{1,0:T(8,128)(2,1)S(1)}, bf16[256,256]{1,0:T(8,128)(2,1)S(1)}, u32[]{:S(2)}, u32[]{:S(2)}) collective-permute-start(bf16[256,256]{1,0:T(8,128)(2,1)S(1)} %shard_map.94.mine_ref), channel_id=1, source_target_pairs={{0,32},{32,0},{64,96},{96,64},{128,160},{160,128},{192,224},{224,1... | collective-permute-start | bytes 393224 | tf_op jit(solution)/shard_map/ppermute | solution.py:320
  31.3 12.2 %copy-start.7 = (f32[512]{0:T(512)S(1)}, f32[512]{0:T(512)}, u32[]{:S(2)}) copy-start(f32[512]{0:T(512)} %param.16) | copy-start | bytes 6148
  34.5 6.4 %collective-permute-start.6 = (f32[8,512]{1,0:T(8,128)S(1)}, f32[8,512]{1,0:T(8,128)S(1)}, u32[]{:S(2)}, u32[]{:S(2)}) collective-permute-start(f32[8,512]{1,0:T(8,128)S(1)} %get-tuple-element.43.s0_ref), channel_id=1, source_target_pairs={{0,1},{1,2},{2,3},{3,0},{4,5},{5,6},{6,7},{7,4},{8,9},{9,10},{10,1... | collective-permute-start | bytes 49160 | tf_op jit(solution)/shard_map/ppermute | solution.py:328
  36.5 5.0 %collective-permute-start.7 = (f32[8,512]{1,0:T(8,128)S(1)}, f32[8,512]{1,0:T(8,128)S(1)}, u32[]{:S(2)}, u32[]{:S(2)}) collective-permute-start(f32[8,512]{1,0:T(8,128)S(1)} %get-tuple-element.43.s0_ref), channel_id=1, source_target_pairs={{0,2},{1,3},{2,0},{3,1},{4,6},{5,7},{6,4},{7,5},{8,10},{9,11},{10,... | collective-permute-start | bytes 49160 | tf_op jit(solution)/shard_map/ppermute | solution.py:328
  39.7 3.7 %collective-permute-start.8 = (f32[8,512]{1,0:T(8,128)S(1)}, f32[8,512]{1,0:T(8,128)S(1)}, u32[]{:S(2)}, u32[]{:S(2)}) collective-permute-start(f32[8,512]{1,0:T(8,128)S(1)} %get-tuple-element.43.s0_ref), channel_id=1, source_target_pairs={{0,3},{1,0},{2,1},{3,2},{4,7},{5,4},{6,5},{7,6},{8,11},{9,8},{10,9... | collective-permute-start | bytes 49160 | tf_op jit(solution)/shard_map/ppermute | solution.py:328
  44.8 33.1 %copy-start = (bf16[3,8,128,256]{3,2,1,0:T(8,128)(2,1)}, bf16[3,8,128,256]{3,2,1,0:T(8,128)(2,1)S(1)}, u32[]{:S(2)}) copy-start(bf16[3,8,128,256]{3,2,1,0:T(8,128)(2,1)S(1)} %get-tuple-element.48.refs_0_) | copy-start | bytes 4718596
  44.8 33.1 %collective-permute-start.13 = (bf16[3,8,128,256]{3,2,1,0:T(8,128)(2,1)S(1)}, bf16[3,8,128,256]{3,2,1,0:T(8,128)(2,1)S(1)}, u32[]{:S(2)}, u32[]{:S(2)}) collective-permute-start(bf16[3,8,128,256]{3,2,1,0:T(8,128)(2,1)S(1)} %get-tuple-element.48.refs_0_), channel_id=1, source_target_pairs={{0,32},{32,0},{64,96},{96,64},{128,160},{160,128},{192,224},{224,1... | collective-permute-start | bytes 4718600 | tf_op jit(solution)/shard_map/ppermute | solution.py:357
  44.9 20.4 %collective-permute-start.14 = (bf16[3,8,64,256]{3,2,1,0:T(8,128)(2,1)S(1)}, bf16[3,8,64,256]{3,2,1,0:T(8,128)(2,1)S(1)}, u32[]{:S(2)}, u32[]{:S(2)}) collective-permute-start(bf16[3,8,64,256]{3,2,1,0:T(8,128)(2,1)S(1)} %get-tuple-element.49), channel_id=1, source_target_pairs={{0,64},{32,96},{64,128},{96,160},{128,192},{160,224},{192,0},{224,... | collective-permute-start | bytes 2359304 | tf_op jit(solution)/shard_map/ppermute | solution.py:354
  47.8 19.6 %collective-permute-start.15 = (bf16[3,8,64,256]{3,2,1,0:T(8,128)(2,1)S(1)}, bf16[3,8,64,256]{3,2,1,0:T(8,128)(2,1)S(1)}, u32[]{:S(2)}, u32[]{:S(2)}) collective-permute-start(bf16[3,8,64,256]{3,2,1,0:T(8,128)(2,1)S(1)} %get-tuple-element.50), channel_id=1, source_target_pairs={{0,192},{32,224},{64,0},{96,32},{128,64},{160,96},{192,128},{224,1... | collective-permute-start | bytes 2359304 | tf_op jit(solution)/shard_map/ppermute | solution.py:355
  47.8 19.6 %collective-permute-start.9 = (bf16[512,512]{1,0:T(8,128)(2,1)S(1)}, bf16[512,512]{1,0:T(8,128)(2,1)S(1)}, u32[]{:S(2)}, u32[]{:S(2)}) collective-permute-start(bf16[512,512]{1,0:T(8,128)(2,1)S(1)} %shard_map.97.n0_ref), channel_id=1, source_target_pairs={{0,8},{1,9},{2,10},{3,11},{4,12},{5,13},{6,14},{7,15},{8,16},{9,17... | collective-permute-start | bytes 1572872 | tf_op jit(solution)/shard_map/ppermute | solution.py:336
  49.6 19.7 %collective-permute-start.11 = (bf16[512,512]{1,0:T(8,128)(2,1)S(1)}, bf16[512,512]{1,0:T(8,128)(2,1)S(1)}, u32[]{:S(2)}, u32[]{:S(2)}) collective-permute-start(bf16[512,512]{1,0:T(8,128)(2,1)S(1)} %shard_map.97.n0_ref), channel_id=1, source_target_pairs={{0,24},{1,25},{2,26},{3,27},{4,28},{5,29},{6,30},{7,31},{8,0},{9,1... | collective-permute-start | bytes 1572872 | tf_op jit(solution)/shard_map/ppermute | solution.py:336
  65.2 12.6 %collective-permute-start.16 = (bf16[3,8,64,256]{3,2,1,0:T(8,128)(2,1)S(1)}, bf16[3,8,64,256]{3,2,1,0:T(8,128)(2,1)S(1)}, u32[]{:S(2)}, u32[]{:S(2)}) collective-permute-start(bf16[3,8,64,256]{3,2,1,0:T(8,128)(2,1)S(1)} %collective-permute-done.14.refs_2_), channel_id=1, source_target_pairs={{0,32},{32,0},{64,96},{96,64},{128,160},{160,128},{192,224},{224,1... | collective-permute-start | bytes 2359304 | tf_op jit(solution)/shard_map/ppermute | solution.py:357
  67.4 10.4 %collective-permute-start.17 = (bf16[3,8,64,256]{3,2,1,0:T(8,128)(2,1)S(1)}, bf16[3,8,64,256]{3,2,1,0:T(8,128)(2,1)S(1)}, u32[]{:S(2)}, u32[]{:S(2)}) collective-permute-start(bf16[3,8,64,256]{3,2,1,0:T(8,128)(2,1)S(1)} %collective-permute-done.15.refs_3_), channel_id=1, source_target_pairs={{0,32},{32,0},{64,96},{96,64},{128,160},{160,128},{192,224},{224,1... | collective-permute-start | bytes 2359304 | tf_op jit(solution)/shard_map/ppermute | solution.py:357
  67.5 10.0 %collective-permute-start.10 = (bf16[256,512]{1,0:T(8,128)(2,1)S(1)}, bf16[256,512]{1,0:T(8,128)(2,1)S(1)}, u32[]{:S(2)}, u32[]{:S(2)}) collective-permute-start(bf16[256,512]{1,0:T(8,128)(2,1)S(1)} %slice.44), channel_id=1, source_target_pairs={{0,8},{1,9},{2,10},{3,11},{4,12},{5,13},{6,14},{7,15},{8,16},{9,17... | collective-permute-start | bytes 786440 | tf_op jit(solution)/shard_map/ppermute | solution.py:337
  69.3 8.5 %collective-permute-start.12 = (bf16[256,512]{1,0:T(8,128)(2,1)S(1)}, bf16[256,512]{1,0:T(8,128)(2,1)S(1)}, u32[]{:S(2)}, u32[]{:S(2)}) collective-permute-start(bf16[256,512]{1,0:T(8,128)(2,1)S(1)} %slice.45), channel_id=1, source_target_pairs={{0,24},{1,25},{2,26},{3,27},{4,28},{5,29},{6,30},{7,31},{8,0},{9,1... | collective-permute-start | bytes 786440 | tf_op jit(solution)/shard_map/ppermute | solution.py:338
  81.4 8.4 %collective-permute-start.18 = (bf16[256,256]{1,0:T(8,128)(2,1)S(1)}, bf16[256,256]{1,0:T(8,128)(2,1)S(1)}, u32[]{:S(2)}, u32[]{:S(2)}) collective-permute-start(bf16[256,256]{1,0:T(8,128)(2,1)S(1)} %get-tuple-element.51), channel_id=1, source_target_pairs={{0,1},{1,2},{2,3},{3,4},{4,5},{5,6},{6,7},{7,0},{8,9},{9,10},{10,1... | collective-permute-start | bytes 393224 | tf_op jit(solution)/shard_map/ppermute | solution.py:385
  81.5 8.2 %collective-permute-start.19 = (bf16[256,256]{1,0:T(8,128)(2,1)S(1)}, bf16[256,256]{1,0:T(8,128)(2,1)S(1)}, u32[]{:S(2)}, u32[]{:S(2)}) collective-permute-start(bf16[256,256]{1,0:T(8,128)(2,1)S(1)} %get-tuple-element.52), channel_id=1, source_target_pairs={{0,7},{1,0},{2,1},{3,2},{4,3},{5,4},{6,5},{7,6},{8,15},{9,8},{10,9... | collective-permute-start | bytes 393224 | tf_op jit(solution)/shard_map/ppermute | solution.py:385
  89.9 7.4 %collective-permute-start.22 = (bf16[512,256]{1,0:T(8,128)(2,1)S(1)}, bf16[512,256]{1,0:T(8,128)(2,1)S(1)}, u32[]{:S(2)}, u32[]{:S(2)}) collective-permute-start(bf16[512,256]{1,0:T(8,128)(2,1)S(1)} %pad_maximum_fusion.1), channel_id=1, source_target_pairs={{0,7},{1,0},{2,1},{3,2},{4,3},{5,4},{6,5},{7,6},{8,15},{9,8},{10,9... | collective-permute-start | bytes 786440 | tf_op jit(solution)/shard_map/ppermute | solution.py:385
  92.9 7.7 %collective-permute-start.20 = (bf16[512,256]{1,0:T(8,128)(2,1)S(1)}, bf16[512,256]{1,0:T(8,128)(2,1)S(1)}, u32[]{:S(2)}, u32[]{:S(2)}) collective-permute-start(bf16[512,256]{1,0:T(8,128)(2,1)S(1)} %pad_maximum_fusion), channel_id=1, source_target_pairs={{0,1},{1,2},{2,3},{3,4},{4,5},{5,6},{6,7},{7,0},{8,9},{9,10},{10,1... | collective-permute-start | bytes 786440 | tf_op jit(solution)/shard_map/ppermute | solution.py:385
  100.7 7.9 %collective-permute-start.21 = (bf16[512,256]{1,0:T(8,128)(2,1)S(1)}, bf16[512,256]{1,0:T(8,128)(2,1)S(1)}, u32[]{:S(2)}, u32[]{:S(2)}) collective-permute-start(bf16[512,256]{1,0:T(8,128)(2,1)S(1)} %get-tuple-element.61), channel_id=1, source_target_pairs={{0,1},{1,2},{2,3},{3,4},{4,5},{5,6},{6,7},{7,0},{8,9},{9,10},{10,1... | collective-permute-start | bytes 786440 | tf_op jit(solution)/shard_map/ppermute | solution.py:385
  100.8 7.8 %collective-permute-start.23 = (bf16[512,256]{1,0:T(8,128)(2,1)S(1)}, bf16[512,256]{1,0:T(8,128)(2,1)S(1)}, u32[]{:S(2)}, u32[]{:S(2)}) collective-permute-start(bf16[512,256]{1,0:T(8,128)(2,1)S(1)} %get-tuple-element.62), channel_id=1, source_target_pairs={{0,7},{1,0},{2,1},{3,2},{4,3},{5,4},{6,5},{7,6},{8,15},{9,8},{10,9... | collective-permute-start | bytes 786440 | tf_op jit(solution)/shard_map/ppermute | solution.py:385
  108.7 7.9 %collective-permute-start.24 = (bf16[512,256]{1,0:T(8,128)(2,1)S(1)}, bf16[512,256]{1,0:T(8,128)(2,1)S(1)}, u32[]{:S(2)}, u32[]{:S(2)}) collective-permute-start(bf16[512,256]{1,0:T(8,128)(2,1)S(1)} %get-tuple-element.59), channel_id=1, source_target_pairs={{0,1},{1,2},{2,3},{3,4},{4,5},{5,6},{6,7},{7,0},{8,9},{9,10},{10,1... | collective-permute-start | bytes 786440 | tf_op jit(solution)/shard_map/ppermute | solution.py:385
  108.8 7.8 %collective-permute-start.25 = (bf16[512,256]{1,0:T(8,128)(2,1)S(1)}, bf16[512,256]{1,0:T(8,128)(2,1)S(1)}, u32[]{:S(2)}, u32[]{:S(2)}) collective-permute-start(bf16[512,256]{1,0:T(8,128)(2,1)S(1)} %get-tuple-element.60), channel_id=1, source_target_pairs={{0,7},{1,0},{2,1},{3,2},{4,3},{5,4},{6,5},{7,6},{8,15},{9,8},{10,9... | collective-permute-start | bytes 786440 | tf_op jit(solution)/shard_map/ppermute | solution.py:385
  (5 other events, 16.4 us)

commit v3 on v2

--- a/solution.py
+++ b/solution.py
@@ -45,11 +45,21 @@
     return lax.dot_general(a, b, (dims, ((), ())), precision=precision, preferred_element_type=F32)
 
 
+def thirds(v):
+    top = v.astype(BF16)
+    rest = v - top.astype(F32)
+    mid = rest.astype(BF16)
+    return top, mid, (rest - mid.astype(F32)).astype(BF16)
+
+
 def spread(heads_rows, width):
     heads = heads_rows.shape[0]
     pick = lax.broadcasted_iota(jnp.int32, (heads, width), 1) // (width // heads)
     own = lax.broadcasted_iota(jnp.int32, (heads, width), 0)
-    return dot(heads_rows, (pick == own).astype(F32), ((0,), (0,)), EXACT)
+    pick = (pick == own).astype(F32)
+    pick = jnp.concatenate([pick] * 3, 0).astype(BF16)
+    parts = jnp.concatenate([p.astype(F32) for p in thirds(heads_rows)], 0).astype(BF16)
+    return dot(parts, pick, ((0,), (0,)))
 
 
 def conv(buf, src_ref, rim, w_ref):
@@ -171,13 +181,14 @@
     other = other_ref[...]
     after = decay_of(other, state) * prior + other[:state].astype(F32)
     incoming = jnp.where(core == 1, after, prior)
-    ones = jnp.ones((8, out_ref.shape[1]), F32)
+    ones = jnp.ones((8, out_ref.shape[1]), BF16)
     for n, s in enumerate(range(0, bc_ref.shape[0], SPAN)):
         start = incoming if n == 0 else incoming * e0_ref[0:1]
         y = y_ref[s : s + SPAN] + dot(bc_ref[s : s + SPAN, state:], start.astype(BF16))
         gated = y * gate_ref[s : s + SPAN]
         out_ref[s : s + SPAN] = gated
-        ss_ref[:, s : s + SPAN] = dot(ones, gated * gated, ((1,), (1,)), EXACT)
+        top, mid, _ = thirds(gated * gated)
+        ss_ref[:, s : s + SPAN] = dot(ones, top, ((1,), (1,))) + dot(ones, mid, ((1,), (1,)))
 
 
 def part_order(px, core):
@@ -190,6 +201,12 @@
     for y, w_ref in enumerate(refs[:-1]):
         for j in range(out_ref.shape[1]):
             out_ref[y, j] = w_ref[:, j * feats : (j + 1) * feats]
+
+
+def own_kernel(at_ref, w_ref, out_ref):
+    feats = out_ref.shape[2]
+    for j in range(out_ref.shape[0]):
+        out_ref[j] = w_ref[:, j * feats : (j + 1) * feats]
 
 
 def sort_kernel(at_ref, one_ref, two_ref, three_ref, all_ref, low_ref, high_ref):
@@ -212,7 +229,7 @@
 def project_kernel(at_ref, n0_ref, n1_ref, low_ref, high_ref, n3_ref, w0_ref, *refs):
     pieces, out_refs = refs[:6], refs[6:]
     part = n0_ref.shape[1] // 4
-    rows, weights = [n0_ref[...]], [w0_ref[...]]
+    rows, weights = [n0_ref[...]], [w0_ref[0]]
     for d, n_refs in enumerate(((n1_ref,), (low_ref, high_ref), (n3_ref,))):
         for p in part_order(at_ref[4], at_ref[1]):
             cols = pl.ds(pl.multiple_of(p * part, part), part)
@@ -227,10 +244,11 @@
         out_refs[1][...] = total[mid:].astype(BF16)
 
 
-def call(body, at, ins, outs, scratch=(), specs=None, grid=(1,), out_specs=None, flops=0, vmem=48):
-    full = lambda s: pl.BlockSpec(s, lambda *_, n=len(s): (0,) * n)
+def call(body, at, ins, outs, scratch=(), specs=None, grid=(1,), out_specs=None, flops=0, vmem=48, pin=False):
+    block = lambda v: pl.BlockSpec(v.shape, lambda *_, n=len(v.shape): (0,) * n)
+    full = (lambda _: pl.BlockSpec(memory_space=pltpu.VMEM)) if pin else block
     specs = specs or {}
-    in_specs = [specs.get(k) or full(a.shape) for k, a in enumerate(ins)]
+    in_specs = [specs.get(k) or full(a) for k, a in enumerate(ins)]
     kwargs = dict(
         out_shape=outs,
         compiler_params=pltpu.CompilerParams(vmem_limit_bytes=vmem << 20),
@@ -241,7 +259,7 @@
         ),
     )
     if out_specs is None:
-        out_specs = [full(o.shape) for o in outs]
+        out_specs = [block(o) for o in outs]
     if at is None:
         return pl.pallas_call(
             body, grid=grid, in_specs=in_specs, out_specs=out_specs, scratch_shapes=scratch, **kwargs
@@ -316,6 +334,8 @@
         [xs, bc_conv, s0, grow, z_gate],
         [like((rows, width), F32), like((rows, width), F32)],
     )
+    before, y_local = lax.optimization_barrier((befores[0], y_local))
+    befores[0] = before
     [mine] = call(prefix_kernel, None, befores, [like((state, width // 2), BF16)])
     theirs = lax.ppermute(mine, "seq", CORE_SWAP)
 
@@ -326,18 +346,6 @@
         [like((rows, width), F32), like((8, rows), F32)],
     )
     more = [lax.ppermute(ss, "head", quad_route(d)) for d in range(1, QUAD)]
-    [normed] = call(
-        functools.partial(norm_kernel, width * QUAD),
-        None,
-        [gated, gain[None, :], ss, *more],
-        [like((rows, width), BF16)],
-    )
-    mid = rows // 2
-    near_up, near_down = (lax.ppermute(normed, "head", y_route(d)) for d in (1, -1))
-    far_low = lax.ppermute(near_up[:mid], "head", y_route(1))
-    far_high = lax.ppermute(near_down[mid:], "head", y_route(-1))
-    peers = [near_up, far_low, far_high, near_down]
-
     at_then, _ = lax.optimization_barrier((at, ss))
     arrived_from = lambda d: pl.BlockSpec(
         (1, NZ, part_k, feats), lambda i, s: ((s[2] + NY - d) % NY, 0, 0, 0)
@@ -353,7 +361,29 @@
     ring = NX * CORES
     x_low = lax.ppermute(low, "seq", [(s, (s + CORES) % ring) for s in range(ring)])
     x_high = lax.ppermute(high, "seq", [(s, (s - CORES) % ring) for s in range(ring)])
+    ss, _ = lax.optimization_barrier((ss, low))
+    [normed] = call(
+        functools.partial(norm_kernel, width * QUAD),
+        None,
+        [gated, gain[None, :], ss, *more],
+        [like((rows, width), BF16)],
+    )
+    mid = rows // 2
+    near_up, near_down = (lax.ppermute(normed, "head", y_route(d)) for d in (1, -1))
+    far_low = lax.ppermute(near_up[:mid], "head", y_route(1))
+    far_high = lax.ppermute(near_down[mid:], "head", y_route(-1))
+    peers = [near_up, far_low, far_high, near_down]
+
     own_late, _ = lax.optimization_barrier((own, normed))
+    at_own, _ = lax.optimization_barrier((at, normed))
+    [w_own] = call(
+        own_kernel,
+        at_own,
+        [w_out],
+        [like((NZ, width, feats), BF16)],
+        specs={0: pl.BlockSpec((width, quarter), lambda i, s: (0, s[2]))},
+    )
+    x_low, x_high, _, w_own = lax.optimization_barrier((x_low, x_high, near_up, w_own))
     swap = lambda v: lax.ppermute(v, "seq", CORE_SWAP)
     pieces = [own, swap(own_late), x_low, x_high, swap(x_low), swap(x_high)]
 
@@ -365,7 +395,7 @@
         piece = lambda v: pl.BlockSpec(
             (NY - 1, 1, v.shape[2], feats), lambda i, s: (0, (s[3] + turn(i)) % NZ, 0, 0)
         )
-        own = pl.BlockSpec((width, feats), lambda i, s: (0, s[2] * NZ + (s[3] + turn(i)) % NZ))
+        own = pl.BlockSpec((1, width, feats), lambda i, s: ((s[3] + turn(i)) % NZ, 0, 0))
         if len(order) == 1:
             outs, out_specs = [like((rows // 2, feats), BF16)] * 2, None
         else:
@@ -374,12 +404,14 @@
         return call(
             project_kernel,
             at_then,
-            [normed, *peers, w_out, *pieces],
+            [normed, *peers, w_own, *pieces],
             outs,
             specs={5: own, **{6 + k: piece(v) for k, v in enumerate(pieces)}},
             grid=(len(order),),
             out_specs=out_specs,
             flops=2 * rows * width * NY * feats * len(order),
+            vmem=24,
+            pin=True,
         )
 
     send = lambda v, d: lax.ppermute(v, "head", z_route(d))

time: 119 us -> 112 us (0.941)
  the two profiles are of different devices: /device:TPU:4 before, /device:TPU:90 now
where the time goes in v3:
time: 112 us; the launch traced here: 111 us
  waiting for transfers between devices  47.3 us (42%)
  starting transfers between devices  37.3 us (33%)
  Pallas kernels  22.2 us (20%)
  local copies, waits for them, and re-layouts  3.8 us (3%)
    pallas_call x11, Pallas kernels, call(): pl.pallas_call(body, grid_spec=pltpu.PrefetchScalarGridSpec(num_scalar_pr...  21.1 us
    ppermute x8, waiting for transfers between devices, on_device(): send = lambda v, d: lax.ppermute(v, 'head', z_route(d))  15.9 us
    ppermute x8, starting transfers between devices, on_device(): send = lambda v, d: lax.ppermute(v, 'head', z_route(d))  13.4 us
    ppermute x2, waiting for transfers between devices, on_device(): lax.ppermute(normed, 'head', y_route(d))  9.9 us
    ppermute x1, waiting for transfers between devices, on_device(): far_low = lax.ppermute(near_up[:mid], 'head', y_route(1))  6.03 us
    ppermute x3, starting transfers between devices, on_device(): befores = [lax.ppermute(chip, 'seq', x_route(d)) for d in (1, 2, 3)]  5.34 us
    all_to_all x1, starting transfers between devices, on_device(): lax.all_to_all(ahead, 'head', 0, 0, tiled=True, axis_index_groups=columns)  4.83 us
    all_to_all x1, waiting for transfers between devices, on_device(): lax.all_to_all(ahead, 'head', 0, 0, tiled=True, axis_index_groups=columns)  3.78 us
  transfers between devices with their start and end apart: 27, of which 17 were waited for; matrix products, arithmetic and copies ran while one was open for 0% of the time, Pallas kernels for 19%

profile of v3, /device:TPU:90, one launch (start us, length us, event | category | flops | bytes accessed | tf_op | source)
XLA Modules:
  0.0 111.4 jit_solution(14982061053612179008)
XLA Ops:
  1.4 1.9 %collective-permute-start = (bf16[16,1024]{1,0:T(8,128)(2,1)S(1)}, bf16[16,1024]{1,0:T(8,128)(2,1)S(1)}, u32[]{:S(2)}, u32[]{:S(2)}) collective-permute-start(bf16[16,1024]{1,0:T(8,128)(2,1)S(1)} %pad_maximum_fusion.2), channel_id=1, source_target_pairs={{0,32},{32,64},{64,96},{96,128},{128,160},{160,192},{192,224},{1,3... | collective-permute-start | bytes 98312 | tf_op jit(solution)/shard_map/ppermute | solution.py:291
  3.5 2.2 %shard_map.91 = bf16[4,8,128,256]{3,2,1,0:T(8,128)(2,1)S(1)} custom-call(s32[5]{0:T(128)S(1)} %stack.23.at_ref, bf16[512,8192]{1,0:T(8,128)(2,1)} %w_ref.1, bf16[512,8192]{1,0:T(8,128)(2,1)} %w_ref.1, bf16[512,8192]{1,0:T(8,128)(2,1)} %w_ref.1, bf16[512,8192]{1,0:T(8,128)(2,1)} %w_ref.1), custom_call_target="tpu_custom_call" | custom-call | bytes 35651584 | tf_op jit(solution)/shard_map/pallas_call | solution.py:267
  7.1 4.8 %all-to-all-start = ((bf16[4,8,128,256]{3,2,1,0:T(8,128)(2,1)}), bf16[4,8,128,256]{3,2,1,0:T(8,128)(2,1)S(1)}, u32[]{:S(2)}, u32[]{:S(2)}) async-start(bf16[4,8,128,256]{3,2,1,0:T(8,128)(2,1)} %copy-done), calls=%async_computation | async-start | bytes 4194304 | tf_op jit(solution)/shard_map/all_to_all | solution.py:309
  12.0 4.4 %shard_map.92 = (bf16[272,512]{1,0:T(8,128)(2,1)S(1)}, bf16[512,512]{1,0:T(8,128)(2,1)S(1)}, bf16[512,512]{1,0:T(8,128)(2,1)S(1)}, bf16[256,512]{1,0:T(8,128)(2,...) custom-call(s32[5]{0:T(128)S(1)} %stack.23.at_ref, bf16[512,512]{1,0:T(8,128)(2,1)S(1)} %copy-done.1, ...), custom_call_target="tpu_custom_call" | custom-call | bytes 6426656 | tf_op jit(solution)/shard_map/pallas_call | solution.py:267
  19.3 3.1 %collective-permute-start.2 = (bf16[272,256]{1,0:T(8,128)(2,1)S(1)}, bf16[272,256]{1,0:T(8,128)(2,1)S(1)}, u32[]{:S(2)}, u32[]{:S(2)}) collective-permute-start(bf16[272,256]{1,0:T(8,128)(2,1)S(1)} %shard_map.93), channel_id=1, source_target_pairs={{0,64},{32,96},{64,128},{96,160},{128,192},{160,224},{1,65},{33,97... | collective-permute-start | bytes 417800 | tf_op jit(solution)/shard_map/ppermute | solution.py:330
  22.5 1.5 %collective-permute-start.3 = (bf16[272,256]{1,0:T(8,128)(2,1)S(1)}, bf16[272,256]{1,0:T(8,128)(2,1)S(1)}, u32[]{:S(2)}, u32[]{:S(2)}) collective-permute-start(bf16[272,256]{1,0:T(8,128)(2,1)S(1)} %shard_map.93), channel_id=1, source_target_pairs={{0,128},{32,160},{64,192},{96,224},{1,129},{33,161},{65,193},{97,2... | collective-permute-start | bytes 417800 | tf_op jit(solution)/shard_map/ppermute | solution.py:330
  25.5 1.7 %collective-permute-done.2.one_ref = bf16[272,256]{1,0:T(8,128)(2,1)S(1)} collective-permute-done((bf16[272,256]{1,0:T(8,128)(2,1)S(1)}, bf16[272,256]{1,0:T(8,128)(2,1)S(1)}, u32[]{:S(2)}, u32[]{:S(2)}) %collective-permute-start.2) | collective-permute-done | bytes 139296 | tf_op jit(solution)/shard_map/ppermute | solution.py:330
  30.0 1.9 %collective-permute-start.6 = (f32[8,512]{1,0:T(8,128)S(1)}, f32[8,512]{1,0:T(8,128)S(1)}, u32[]{:S(2)}, u32[]{:S(2)}) collective-permute-start(f32[8,512]{1,0:T(8,128)S(1)} %get-tuple-element.55.s0_ref), channel_id=1, source_target_pairs={{0,1},{1,2},{2,3},{3,0},{4,5},{5,6},{6,7},{7,4},{8,9},{9,10},{10,1... | collective-permute-start | bytes 49160 | tf_op jit(solution)/shard_map/ppermute | solution.py:348
  31.9 1.5 %collective-permute-start.8 = (f32[8,512]{1,0:T(8,128)S(1)}, f32[8,512]{1,0:T(8,128)S(1)}, u32[]{:S(2)}, u32[]{:S(2)}) collective-permute-start(f32[8,512]{1,0:T(8,128)S(1)} %get-tuple-element.55.s0_ref), channel_id=1, source_target_pairs={{0,3},{1,0},{2,1},{3,2},{4,7},{5,4},{6,5},{7,6},{8,11},{9,8},{10,9... | collective-permute-start | bytes 49160 | tf_op jit(solution)/shard_map/ppermute | solution.py:348
  33.5 3.8 %all-to-all-done.one_ref.two_ref.three_ref = bf16[4,8,128,256]{3,2,1,0:T(8,128)(2,1)S(1)} async-done(((bf16[4,8,128,256]{3,2,1,0:T(8,128)(2,1)}), bf16[4,8,128,256]{3,2,1,0:T(8,128)(2,1)S(1)}, u32[]{:S(2)}, u32[]{:S(2)}) %all-to-all-start) | async-done | bytes 2097184 | tf_op jit(solution)/shard_map/all_to_all | solution.py:309
  38.0 1.9 %collective-permute-start.13 = (bf16[3,8,64,256]{3,2,1,0:T(8,128)(2,1)S(1)}, bf16[3,8,64,256]{3,2,1,0:T(8,128)(2,1)S(1)}, u32[]{:S(2)}, u32[]{:S(2)}) collective-permute-start(bf16[3,8,64,256]{3,2,1,0:T(8,128)(2,1)S(1)} %get-tuple-element.54), channel_id=1, source_target_pairs={{0,64},{32,96},{64,128},{96,160},{128,192},{160,224},{192,0},{224,... | collective-permute-start | bytes 2359304 | tf_op jit(solution)/shard_map/ppermute | solution.py:362
  40.6 2.1 %collective-permute-start.9 = (bf16[512,512]{1,0:T(8,128)(2,1)S(1)}, bf16[512,512]{1,0:T(8,128)(2,1)S(1)}, u32[]{:S(2)}, u32[]{:S(2)}) collective-permute-start(bf16[512,512]{1,0:T(8,128)(2,1)S(1)} %shard_map.98.n0_ref), channel_id=1, source_target_pairs={{0,8},{1,9},{2,10},{3,11},{4,12},{5,13},{6,14},{7,15},{8,16},{9,17... | collective-permute-start | bytes 1572872 | tf_op jit(solution)/shard_map/ppermute | solution.py:372
  42.7 2.3 %shard_map.99.w0_ref = bf16[8,512,256]{2,1,0:T(8,128)(2,1)S(1)} custom-call(s32[5]{0:T(128)S(1)} %stack.23.at_ref, bf16[512,8192]{1,0:T(8,128)(2,1)} %w_ref.1), custom_call_target="tpu_custom_call" | custom-call | bytes 10485760 | tf_op jit(solution)/shard_map/pallas_call | solution.py:267
  45.0 9.9 %collective-permute-done.9.n1_ref = bf16[512,512]{1,0:T(8,128)(2,1)S(1)} collective-permute-done((bf16[512,512]{1,0:T(8,128)(2,1)S(1)}, bf16[512,512]{1,0:T(8,128)(2,1)S(1)}, u32[]{:S(2)}, u32[]{:S(2)}) %collective-permute-start.9) | collective-permute-done | bytes 524320 | tf_op jit(solution)/shard_map/ppermute | solution.py:372
  54.9 2.8 %collective-permute-done.13.refs_2_ = bf16[3,8,64,256]{3,2,1,0:T(8,128)(2,1)S(1)} collective-permute-done((bf16[3,8,64,256]{3,2,1,0:T(8,128)(2,1)S(1)}, bf16[3,8,64,256]{3,2,1,0:T(8,128)(2,1)S(1)}, u32[]{:S(2)}, u32[]{:S(2)}) %collective-permute-start.13) | collective-permute-done | bytes 786464 | tf_op jit(solution)/shard_map/ppermute | solution.py:362
  57.7 1.5 %collective-permute-done.14.refs_3_ = bf16[3,8,64,256]{3,2,1,0:T(8,128)(2,1)S(1)} collective-permute-done((bf16[3,8,64,256]{3,2,1,0:T(8,128)(2,1)S(1)}, bf16[3,8,64,256]{3,2,1,0:T(8,128)(2,1)S(1)}, u32[]{:S(2)}, u32[]{:S(2)}) %collective-permute-start.14) | collective-permute-done | bytes 786464 | tf_op jit(solution)/shard_map/ppermute | solution.py:363
  59.7 2.1 %collective-permute-start.10 = (bf16[256,512]{1,0:T(8,128)(2,1)S(1)}, bf16[256,512]{1,0:T(8,128)(2,1)S(1)}, u32[]{:S(2)}, u32[]{:S(2)}) collective-permute-start(bf16[256,512]{1,0:T(8,128)(2,1)S(1)} %slice.44), channel_id=1, source_target_pairs={{0,8},{1,9},{2,10},{3,11},{4,12},{5,13},{6,14},{7,15},{8,16},{9,17... | collective-permute-start | bytes 786440 | tf_op jit(solution)/shard_map/ppermute | solution.py:373
  61.9 6.0 %collective-permute-done.10.low_ref = bf16[256,512]{1,0:T(8,128)(2,1)S(1)} collective-permute-done((bf16[256,512]{1,0:T(8,128)(2,1)S(1)}, bf16[256,512]{1,0:T(8,128)(2,1)S(1)}, u32[]{:S(2)}, u32[]{:S(2)}) %collective-permute-start.10) | collective-permute-done | bytes 262176 | tf_op jit(solution)/shard_map/ppermute | solution.py:373
  68.0 3.1 %collective-permute-done.12.high_ref = bf16[256,512]{1,0:T(8,128)(2,1)S(1)} collective-permute-done((bf16[256,512]{1,0:T(8,128)(2,1)S(1)}, bf16[256,512]{1,0:T(8,128)(2,1)S(1)}, u32[]{:S(2)}, u32[]{:S(2)}) %collective-permute-start.12) | collective-permute-done | bytes 262176 | tf_op jit(solution)/shard_map/ppermute | solution.py:374
  72.4 2.0 %collective-permute-start.18 = (bf16[256,256]{1,0:T(8,128)(2,1)S(1)}, bf16[256,256]{1,0:T(8,128)(2,1)S(1)}, u32[]{:S(2)}, u32[]{:S(2)}) collective-permute-start(bf16[256,256]{1,0:T(8,128)(2,1)S(1)} %get-tuple-element.63), channel_id=1, source_target_pairs={{0,1},{1,2},{2,3},{3,4},{4,5},{5,6},{6,7},{7,0},{8,9},{9,10},{10,1... | collective-permute-start | bytes 393224 | tf_op jit(solution)/shard_map/ppermute | solution.py:417
  74.5 2.3 %shard_map.102 = bf16[2,512,256]{2,1,0:T(8,128)(2,1)S(1)} custom-call(s32[5]{0:T(128)S(1)} %stack.23.at_ref, bf16[512,512]{1,0:T(8,128)(2,1)S(1)} %shard_map.98.n0_ref, bf16[512,512]{1,0:T(8,128)(2,1)S(1)} %collective-permute-done.9.n1_ref, bf16[256,512]{1,0:T(8,128)(2,1)S(1)} %collective-permute-done.10.low_ref, ...), custom_call_target="tpu_custom_call" | custom-call | flops 1073741824 | bytes 11010048 | tf_op jit(solution)/shard_map/pallas_call | solution.py:267
  77.4 3.0 %collective-permute-done.19 = bf16[256,256]{1,0:T(8,128)(2,1)S(1)} collective-permute-done((bf16[256,256]{1,0:T(8,128)(2,1)S(1)}, bf16[256,256]{1,0:T(8,128)(2,1)S(1)}, u32[]{:S(2)}, u32[]{:S(2)}) %collective-permute-start.19) | collective-permute-done | bytes 131104 | tf_op jit(solution)/shard_map/ppermute | solution.py:417
  80.6 3.3 %collective-permute-start.20 = (bf16[512,256]{1,0:T(8,128)(2,1)S(1)}, bf16[512,256]{1,0:T(8,128)(2,1)S(1)}, u32[]{:S(2)}, u32[]{:S(2)}) collective-permute-start(bf16[512,256]{1,0:T(8,128)(2,1)S(1)} %pad_maximum_fusion), channel_id=1, source_target_pairs={{0,1},{1,2},{2,3},{3,4},{4,5},{5,6},{6,7},{7,0},{8,9},{9,10},{10,1... | collective-permute-start | bytes 786440 | tf_op jit(solution)/shard_map/ppermute | solution.py:417
  84.0 2.3 %shard_map.101 = bf16[2,512,256]{2,1,0:T(8,128)(2,1)S(1)} custom-call(s32[5]{0:T(128)S(1)} %stack.23.at_ref, bf16[512,512]{1,0:T(8,128)(2,1)S(1)} %shard_map.98.n0_ref, bf16[512,512]{1,0:T(8,128)(2,1)S(1)} %collective-permute-done.9.n1_ref, bf16[256,512]{1,0:T(8,128)(2,1)S(1)} %collective-permute-done.10.low_ref, ...), custom_call_target="tpu_custom_call" | custom-call | flops 1073741824 | bytes 11010048 | tf_op jit(solution)/shard_map/pallas_call | solution.py:267
  86.3 1.9 %collective-permute-done.22 = bf16[512,256]{1,0:T(8,128)(2,1)S(1)} collective-permute-done((bf16[512,256]{1,0:T(8,128)(2,1)S(1)}, bf16[512,256]{1,0:T(8,128)(2,1)S(1)}, u32[]{:S(2)}, u32[]{:S(2)}) %collective-permute-start.22) | collective-permute-done | bytes 262176 | tf_op jit(solution)/shard_map/ppermute | solution.py:417
  88.3 3.3 %collective-permute-start.21 = (bf16[512,256]{1,0:T(8,128)(2,1)S(1)}, bf16[512,256]{1,0:T(8,128)(2,1)S(1)}, u32[]{:S(2)}, u32[]{:S(2)}) collective-permute-start(bf16[512,256]{1,0:T(8,128)(2,1)S(1)} %get-tuple-element.73), channel_id=1, source_target_pairs={{0,1},{1,2},{2,3},{3,4},{4,5},{5,6},{6,7},{7,0},{8,9},{9,10},{10,1... | collective-permute-start | bytes 786440 | tf_op jit(solution)/shard_map/ppermute | solution.py:417
  91.6 2.3 %shard_map.104 = bf16[2,512,256]{2,1,0:T(8,128)(2,1)S(1)} custom-call(s32[5]{0:T(128)S(1)} %stack.23.at_ref, bf16[512,512]{1,0:T(8,128)(2,1)S(1)} %shard_map.98.n0_ref, bf16[512,512]{1,0:T(8,128)(2,1)S(1)} %collective-permute-done.9.n1_ref, bf16[256,512]{1,0:T(8,128)(2,1)S(1)} %collective-permute-done.10.low_ref, ...), custom_call_target="tpu_custom_call" | custom-call | flops 1073741824 | bytes 11010048 | tf_op jit(solution)/shard_map/pallas_call | solution.py:267
  94.0 1.5 %collective-permute-done.21 = bf16[512,256]{1,0:T(8,128)(2,1)S(1)} collective-permute-done((bf16[512,256]{1,0:T(8,128)(2,1)S(1)}, bf16[512,256]{1,0:T(8,128)(2,1)S(1)}, u32[]{:S(2)}, u32[]{:S(2)}) %collective-permute-start.21) | collective-permute-done | bytes 262176 | tf_op jit(solution)/shard_map/ppermute | solution.py:417
  95.5 3.8 %collective-permute-done.23 = bf16[512,256]{1,0:T(8,128)(2,1)S(1)} collective-permute-done((bf16[512,256]{1,0:T(8,128)(2,1)S(1)}, bf16[512,256]{1,0:T(8,128)(2,1)S(1)}, u32[]{:S(2)}, u32[]{:S(2)}) %collective-permute-start.23) | collective-permute-done | bytes 262176 | tf_op jit(solution)/shard_map/ppermute | solution.py:417
  99.4 4.6 %collective-permute-start.24 = (bf16[512,256]{1,0:T(8,128)(2,1)S(1)}, bf16[512,256]{1,0:T(8,128)(2,1)S(1)}, u32[]{:S(2)}, u32[]{:S(2)}) collective-permute-start(bf16[512,256]{1,0:T(8,128)(2,1)S(1)} %get-tuple-element.71), channel_id=1, source_target_pairs={{0,1},{1,2},{2,3},{3,4},{4,5},{5,6},{6,7},{7,0},{8,9},{9,10},{10,1... | collective-permute-start | bytes 786440 | tf_op jit(solution)/shard_map/ppermute | solution.py:417
  105.3 2.6 %collective-permute-done.24 = bf16[512,256]{1,0:T(8,128)(2,1)S(1)} collective-permute-done((bf16[512,256]{1,0:T(8,128)(2,1)S(1)}, bf16[512,256]{1,0:T(8,128)(2,1)S(1)}, u32[]{:S(2)}, u32[]{:S(2)}) %collective-permute-start.24) | collective-permute-done | bytes 262176 | tf_op jit(solution)/shard_map/ppermute | solution.py:417
  107.9 2.5 %collective-permute-done.25 = bf16[512,256]{1,0:T(8,128)(2,1)S(1)} collective-permute-done((bf16[512,256]{1,0:T(8,128)(2,1)S(1)}, bf16[512,256]{1,0:T(8,128)(2,1)S(1)}, u32[]{:S(2)}, u32[]{:S(2)}) %collective-permute-start.25) | collective-permute-done | bytes 262176 | tf_op jit(solution)/shard_map/ppermute | solution.py:417
  (66 shorter events, 16.7 us)
Async XLA Ops:
  1.4 5.6 %collective-permute-start = (bf16[16,1024]{1,0:T(8,128)(2,1)S(1)}, bf16[16,1024]{1,0:T(8,128)(2,1)S(1)}, u32[]{:S(2)}, u32[]{:S(2)}) collective-permute-start(bf16[16,1024]{1,0:T(8,128)(2,1)S(1)} %pad_maximum_fusion.2), channel_id=1, source_target_pairs={{0,32},{32,64},{64,96},{96,128},{128,160},{160,192},{192,224},{1,3... | collective-permute-start | bytes 98312 | tf_op jit(solution)/shard_map/ppermute | solution.py:291
  7.1 4.9 %copy-start.4 = (f32[8,512]{1,0:T(8,128)S(1)}, f32[8,512]{1,0:T(8,128)}, u32[]{:S(2)}) copy-start(f32[8,512]{1,0:T(8,128)} %dt_ref.1) | copy-start | bytes 49156
  7.1 4.9 %copy-start.5 = (bf16[4,512]{1,0:T(4,128)(2,1)S(1)}, bf16[4,512]{1,0:T(4,128)(2,1)}, u32[]{:S(2)}) copy-start(bf16[4,512]{1,0:T(4,128)(2,1)} %wx_ref.1) | copy-start | bytes 12292
  7.1 4.9 %copy-start.7 = (f32[8]{0:T(128)S(1)}, f32[8]{0:T(128)}, u32[]{:S(2)}) copy-start(f32[8]{0:T(128)} %param.13) | copy-start | bytes 100
  7.1 30.2 %all-to-all-start = ((bf16[4,8,128,256]{3,2,1,0:T(8,128)(2,1)}), bf16[4,8,128,256]{3,2,1,0:T(8,128)(2,1)S(1)}, u32[]{:S(2)}, u32[]{:S(2)}) async-start(bf16[4,8,128,256]{3,2,1,0:T(8,128)(2,1)} %copy-done), calls=%async_computation | async-start | bytes 4194304 | tf_op jit(solution)/shard_map/all_to_all | solution.py:309
  12.0 12.8 %copy-start.2 = (bf16[512,512]{1,0:T(8,128)(2,1)S(1)}, bf16[512,512]{1,0:T(8,128)(2,1)}, u32[]{:S(2)}) copy-start(bf16[512,512]{1,0:T(8,128)(2,1)} %z_ref.1) | copy-start | bytes 1572868
  16.4 2.3 %collective-permute-start.1 = (bf16[272,512]{1,0:T(8,128)(2,1)S(1)}, bf16[272,512]{1,0:T(8,128)(2,1)S(1)}, u32[]{:S(2)}, u32[]{:S(2)}) collective-permute-start(bf16[272,512]{1,0:T(8,128)(2,1)S(1)} %get-tuple-element.40.own_ref), channel_id=1, source_target_pairs={{0,32},{32,0},{64,96},{96,64},{128,160},{160,128},{192,224},{224,1... | collective-permute-start | bytes 835592 | tf_op jit(solution)/shard_map/ppermute | solution.py:328
  19.3 7.8 %collective-permute-start.2 = (bf16[272,256]{1,0:T(8,128)(2,1)S(1)}, bf16[272,256]{1,0:T(8,128)(2,1)S(1)}, u32[]{:S(2)}, u32[]{:S(2)}) collective-permute-start(bf16[272,256]{1,0:T(8,128)(2,1)S(1)} %shard_map.93), channel_id=1, source_target_pairs={{0,64},{32,96},{64,128},{96,160},{128,192},{160,224},{1,65},{33,97... | collective-permute-start | bytes 417800 | tf_op jit(solution)/shard_map/ppermute | solution.py:330
  22.5 4.8 %collective-permute-start.3 = (bf16[272,256]{1,0:T(8,128)(2,1)S(1)}, bf16[272,256]{1,0:T(8,128)(2,1)S(1)}, u32[]{:S(2)}, u32[]{:S(2)}) collective-permute-start(bf16[272,256]{1,0:T(8,128)(2,1)S(1)} %shard_map.93), channel_id=1, source_target_pairs={{0,128},{32,160},{64,192},{96,224},{1,129},{33,161},{65,193},{97,2... | collective-permute-start | bytes 417800 | tf_op jit(solution)/shard_map/ppermute | solution.py:330
  24.0 3.2 %collective-permute-start.4 = (bf16[272,256]{1,0:T(8,128)(2,1)S(1)}, bf16[272,256]{1,0:T(8,128)(2,1)S(1)}, u32[]{:S(2)}, u32[]{:S(2)}) collective-permute-start(bf16[272,256]{1,0:T(8,128)(2,1)S(1)} %shard_map.93), channel_id=1, source_target_pairs={{0,192},{32,224},{1,193},{33,225},{2,194},{34,226},{3,195},{35,227... | collective-permute-start | bytes 417800 | tf_op jit(solution)/shard_map/ppermute | solution.py:330
  27.3 1.4 %collective-permute-start.5 = (bf16[256,256]{1,0:T(8,128)(2,1)S(1)}, bf16[256,256]{1,0:T(8,128)(2,1)S(1)}, u32[]{:S(2)}, u32[]{:S(2)}) collective-permute-start(bf16[256,256]{1,0:T(8,128)(2,1)S(1)} %shard_map.95.mine_ref), channel_id=1, source_target_pairs={{0,32},{32,0},{64,96},{96,64},{128,160},{160,128},{192,224},{224,1... | collective-permute-start | bytes 393224 | tf_op jit(solution)/shard_map/ppermute | solution.py:340
  30.0 10.1 %copy-start.6 = (f32[512]{0:T(512)S(1)}, f32[512]{0:T(512)}, u32[]{:S(2)}) copy-start(f32[512]{0:T(512)} %param.16) | copy-start | bytes 6148
  30.0 10.1 %collective-permute-start.6 = (f32[8,512]{1,0:T(8,128)S(1)}, f32[8,512]{1,0:T(8,128)S(1)}, u32[]{:S(2)}, u32[]{:S(2)}) collective-permute-start(f32[8,512]{1,0:T(8,128)S(1)} %get-tuple-element.55.s0_ref), channel_id=1, source_target_pairs={{0,1},{1,2},{2,3},{3,0},{4,5},{5,6},{6,7},{7,4},{8,9},{9,10},{10,1... | collective-permute-start | bytes 49160 | tf_op jit(solution)/shard_map/ppermute | solution.py:348
  31.9 8.2 %collective-permute-start.7 = (f32[8,512]{1,0:T(8,128)S(1)}, f32[8,512]{1,0:T(8,128)S(1)}, u32[]{:S(2)}, u32[]{:S(2)}) collective-permute-start(f32[8,512]{1,0:T(8,128)S(1)} %get-tuple-element.55.s0_ref), channel_id=1, source_target_pairs={{0,2},{1,3},{2,0},{3,1},{4,6},{5,7},{6,4},{7,5},{8,10},{9,11},{10,... | collective-permute-start | bytes 49160 | tf_op jit(solution)/shard_map/ppermute | solution.py:348
  31.9 8.2 %collective-permute-start.8 = (f32[8,512]{1,0:T(8,128)S(1)}, f32[8,512]{1,0:T(8,128)S(1)}, u32[]{:S(2)}, u32[]{:S(2)}) collective-permute-start(f32[8,512]{1,0:T(8,128)S(1)} %get-tuple-element.55.s0_ref), channel_id=1, source_target_pairs={{0,3},{1,0},{2,1},{3,2},{4,7},{5,4},{6,5},{7,6},{8,11},{9,8},{10,9... | collective-permute-start | bytes 49160 | tf_op jit(solution)/shard_map/ppermute | solution.py:348
  38.0 19.7 %collective-permute-start.13 = (bf16[3,8,64,256]{3,2,1,0:T(8,128)(2,1)S(1)}, bf16[3,8,64,256]{3,2,1,0:T(8,128)(2,1)S(1)}, u32[]{:S(2)}, u32[]{:S(2)}) collective-permute-start(bf16[3,8,64,256]{3,2,1,0:T(8,128)(2,1)S(1)} %get-tuple-element.54), channel_id=1, source_target_pairs={{0,64},{32,96},{64,128},{96,160},{128,192},{160,224},{192,0},{224,... | collective-permute-start | bytes 2359304 | tf_op jit(solution)/shard_map/ppermute | solution.py:362
  39.9 19.3 %collective-permute-start.14 = (bf16[3,8,64,256]{3,2,1,0:T(8,128)(2,1)S(1)}, bf16[3,8,64,256]{3,2,1,0:T(8,128)(2,1)S(1)}, u32[]{:S(2)}, u32[]{:S(2)}) collective-permute-start(bf16[3,8,64,256]{3,2,1,0:T(8,128)(2,1)S(1)} %get-tuple-element.57), channel_id=1, source_target_pairs={{0,192},{32,224},{64,0},{96,32},{128,64},{160,96},{192,128},{224,1... | collective-permute-start | bytes 2359304 | tf_op jit(solution)/shard_map/ppermute | solution.py:363
  40.5 30.6 %collective-permute-start.15 = (bf16[3,8,128,256]{3,2,1,0:T(8,128)(2,1)S(1)}, bf16[3,8,128,256]{3,2,1,0:T(8,128)(2,1)S(1)}, u32[]{:S(2)}, u32[]{:S(2)}) collective-permute-start(bf16[3,8,128,256]{3,2,1,0:T(8,128)(2,1)S(1)} %get-tuple-element.60.refs_0_), channel_id=1, source_target_pairs={{0,32},{32,0},{64,96},{96,64},{128,160},{160,128},{192,224},{224,1... | collective-permute-start | bytes 4718600 | tf_op jit(solution)/shard_map/ppermute | solution.py:387
  40.6 14.3 %collective-permute-start.9 = (bf16[512,512]{1,0:T(8,128)(2,1)S(1)}, bf16[512,512]{1,0:T(8,128)(2,1)S(1)}, u32[]{:S(2)}, u32[]{:S(2)}) collective-permute-start(bf16[512,512]{1,0:T(8,128)(2,1)S(1)} %shard_map.98.n0_ref), channel_id=1, source_target_pairs={{0,8},{1,9},{2,10},{3,11},{4,12},{5,13},{6,14},{7,15},{8,16},{9,17... | collective-permute-start | bytes 1572872 | tf_op jit(solution)/shard_map/ppermute | solution.py:372
  42.7 19.1 %collective-permute-start.11 = (bf16[512,512]{1,0:T(8,128)(2,1)S(1)}, bf16[512,512]{1,0:T(8,128)(2,1)S(1)}, u32[]{:S(2)}, u32[]{:S(2)}) collective-permute-start(bf16[512,512]{1,0:T(8,128)(2,1)S(1)} %shard_map.98.n0_ref), channel_id=1, source_target_pairs={{0,24},{1,25},{2,26},{3,27},{4,28},{5,29},{6,30},{7,31},{8,0},{9,1... | collective-permute-start | bytes 1572872 | tf_op jit(solution)/shard_map/ppermute | solution.py:372
  59.2 11.9 %collective-permute-start.16 = (bf16[3,8,64,256]{3,2,1,0:T(8,128)(2,1)S(1)}, bf16[3,8,64,256]{3,2,1,0:T(8,128)(2,1)S(1)}, u32[]{:S(2)}, u32[]{:S(2)}) collective-permute-start(bf16[3,8,64,256]{3,2,1,0:T(8,128)(2,1)S(1)} %collective-permute-done.13.refs_2_), channel_id=1, source_target_pairs={{0,32},{32,0},{64,96},{96,64},{128,160},{160,128},{192,224},{224,1... | collective-permute-start | bytes 2359304 | tf_op jit(solution)/shard_map/ppermute | solution.py:387
  59.2 11.9 %collective-permute-start.17 = (bf16[3,8,64,256]{3,2,1,0:T(8,128)(2,1)S(1)}, bf16[3,8,64,256]{3,2,1,0:T(8,128)(2,1)S(1)}, u32[]{:S(2)}, u32[]{:S(2)}) collective-permute-start(bf16[3,8,64,256]{3,2,1,0:T(8,128)(2,1)S(1)} %collective-permute-done.14.refs_3_), channel_id=1, source_target_pairs={{0,32},{32,0},{64,96},{96,64},{128,160},{160,128},{192,224},{224,1... | collective-permute-start | bytes 2359304 | tf_op jit(solution)/shard_map/ppermute | solution.py:387
  59.7 8.3 %collective-permute-start.10 = (bf16[256,512]{1,0:T(8,128)(2,1)S(1)}, bf16[256,512]{1,0:T(8,128)(2,1)S(1)}, u32[]{:S(2)}, u32[]{:S(2)}) collective-permute-start(bf16[256,512]{1,0:T(8,128)(2,1)S(1)} %slice.44), channel_id=1, source_target_pairs={{0,8},{1,9},{2,10},{3,11},{4,12},{5,13},{6,14},{7,15},{8,16},{9,17... | collective-permute-start | bytes 786440 | tf_op jit(solution)/shard_map/ppermute | solution.py:373
  61.9 9.2 %collective-permute-start.12 = (bf16[256,512]{1,0:T(8,128)(2,1)S(1)}, bf16[256,512]{1,0:T(8,128)(2,1)S(1)}, u32[]{:S(2)}, u32[]{:S(2)}) collective-permute-start(bf16[256,512]{1,0:T(8,128)(2,1)S(1)} %slice.45), channel_id=1, source_target_pairs={{0,24},{1,25},{2,26},{3,27},{4,28},{5,29},{6,30},{7,31},{8,0},{9,1... | collective-permute-start | bytes 786440 | tf_op jit(solution)/shard_map/ppermute | solution.py:374
  72.4 5.0 %collective-permute-start.18 = (bf16[256,256]{1,0:T(8,128)(2,1)S(1)}, bf16[256,256]{1,0:T(8,128)(2,1)S(1)}, u32[]{:S(2)}, u32[]{:S(2)}) collective-permute-start(bf16[256,256]{1,0:T(8,128)(2,1)S(1)} %get-tuple-element.63), channel_id=1, source_target_pairs={{0,1},{1,2},{2,3},{3,4},{4,5},{5,6},{6,7},{7,0},{8,9},{9,10},{10,1... | collective-permute-start | bytes 393224 | tf_op jit(solution)/shard_map/ppermute | solution.py:417
  74.4 6.1 %collective-permute-start.19 = (bf16[256,256]{1,0:T(8,128)(2,1)S(1)}, bf16[256,256]{1,0:T(8,128)(2,1)S(1)}, u32[]{:S(2)}, u32[]{:S(2)}) collective-permute-start(bf16[256,256]{1,0:T(8,128)(2,1)S(1)} %get-tuple-element.64), channel_id=1, source_target_pairs={{0,7},{1,0},{2,1},{3,2},{4,3},{5,4},{6,5},{7,6},{8,15},{9,8},{10,9... | collective-permute-start | bytes 393224 | tf_op jit(solution)/shard_map/ppermute | solution.py:417
  80.5 7.7 %collective-permute-start.22 = (bf16[512,256]{1,0:T(8,128)(2,1)S(1)}, bf16[512,256]{1,0:T(8,128)(2,1)S(1)}, u32[]{:S(2)}, u32[]{:S(2)}) collective-permute-start(bf16[512,256]{1,0:T(8,128)(2,1)S(1)} %pad_maximum_fusion.1), channel_id=1, source_target_pairs={{0,7},{1,0},{2,1},{3,2},{4,3},{5,4},{6,5},{7,6},{8,15},{9,8},{10,9... | collective-permute-start | bytes 786440 | tf_op jit(solution)/shard_map/ppermute | solution.py:417
  80.6 7.5 %collective-permute-start.20 = (bf16[512,256]{1,0:T(8,128)(2,1)S(1)}, bf16[512,256]{1,0:T(8,128)(2,1)S(1)}, u32[]{:S(2)}, u32[]{:S(2)}) collective-permute-start(bf16[512,256]{1,0:T(8,128)(2,1)S(1)} %pad_maximum_fusion), channel_id=1, source_target_pairs={{0,1},{1,2},{2,3},{3,4},{4,5},{5,6},{6,7},{7,0},{8,9},{9,10},{10,1... | collective-permute-start | bytes 786440 | tf_op jit(solution)/shard_map/ppermute | solution.py:417
  88.3 7.2 %collective-permute-start.21 = (bf16[512,256]{1,0:T(8,128)(2,1)S(1)}, bf16[512,256]{1,0:T(8,128)(2,1)S(1)}, u32[]{:S(2)}, u32[]{:S(2)}) collective-permute-start(bf16[512,256]{1,0:T(8,128)(2,1)S(1)} %get-tuple-element.73), channel_id=1, source_target_pairs={{0,1},{1,2},{2,3},{3,4},{4,5},{5,6},{6,7},{7,0},{8,9},{9,10},{10,1... | collective-permute-start | bytes 786440 | tf_op jit(solution)/shard_map/ppermute | solution.py:417
  91.6 7.7 %collective-permute-start.23 = (bf16[512,256]{1,0:T(8,128)(2,1)S(1)}, bf16[512,256]{1,0:T(8,128)(2,1)S(1)}, u32[]{:S(2)}, u32[]{:S(2)}) collective-permute-start(bf16[512,256]{1,0:T(8,128)(2,1)S(1)} %get-tuple-element.74), channel_id=1, source_target_pairs={{0,7},{1,0},{2,1},{3,2},{4,3},{5,4},{6,5},{7,6},{8,15},{9,8},{10,9... | collective-permute-start | bytes 786440 | tf_op jit(solution)/shard_map/ppermute | solution.py:417
  99.4 8.5 %collective-permute-start.24 = (bf16[512,256]{1,0:T(8,128)(2,1)S(1)}, bf16[512,256]{1,0:T(8,128)(2,1)S(1)}, u32[]{:S(2)}, u32[]{:S(2)}) collective-permute-start(bf16[512,256]{1,0:T(8,128)(2,1)S(1)} %get-tuple-element.71), channel_id=1, source_target_pairs={{0,1},{1,2},{2,3},{3,4},{4,5},{5,6},{6,7},{7,0},{8,9},{9,10},{10,1... | collective-permute-start | bytes 786440 | tf_op jit(solution)/shard_map/ppermute | solution.py:417
  104.0 6.4 %collective-permute-start.25 = (bf16[512,256]{1,0:T(8,128)(2,1)S(1)}, bf16[512,256]{1,0:T(8,128)(2,1)S(1)}, u32[]{:S(2)}, u32[]{:S(2)}) collective-permute-start(bf16[512,256]{1,0:T(8,128)(2,1)S(1)} %get-tuple-element.72), channel_id=1, source_target_pairs={{0,7},{1,0},{2,1},{3,2},{4,3},{5,4},{6,5},{7,6},{8,15},{9,8},{10,9... | collective-permute-start | bytes 786440 | tf_op jit(solution)/shard_map/ppermute | solution.py:417
  (3 other events, 11.1 us)

commit v4 on v3

--- a/solution.py
+++ b/solution.py
@@ -420,12 +420,18 @@
     up, down = send(far_up, 1), send(far_down, -1)
     [third] = project((3, 5), far_up)
     [second] = project((2, 6), (up, down))
-    up = send(jnp.concatenate([add(third[0, :mid], up), third[0, mid:]], 0), 1)
-    down = send(jnp.concatenate([third[1, :mid], add(third[1, mid:], down)], 0), -1)
+    after = lambda v, other: lax.optimization_barrier((v, other))[0]
+    up_sum = jnp.concatenate([add(third[0, :mid], up), third[0, mid:]], 0)
+    down_sum = jnp.concatenate([third[1, :mid], add(third[1, mid:], after(down, up_sum))], 0)
+    up, down = send(up_sum, 1), send(down_sum, -1)
     [first] = project((1, 7), (up, down))
-    up, down = send(add(second[0], up), 1), send(add(second[1], down), -1)
+    up_sum = add(second[0], up)
+    down_sum = add(second[1], after(down, up_sum))
+    up, down = send(up_sum, 1), send(down_sum, -1)
     own_halves = project((0,), (up, down))
-    up, down = send(add(first[0], up), 1), send(add(first[1], down), -1)
+    up_sum = add(first[0], up)
+    down_sum = add(first[1], after(down, up_sum))
+    up, down = send(up_sum, 1), send(down_sum, -1)
     own = jnp.concatenate(own_halves, 0)
     return (own.astype(F32) + up.astype(F32) + down.astype(F32)).astype(BF16).T
 

time: 112 us -> 110 us (0.982)
  the two profiles are of different devices: /device:TPU:90 before, /device:TPU:4 now
where the time goes in v4:
time: 110 us; the launch traced here: 108 us
  starting transfers between devices  42.7 us (39%)
  waiting for transfers between devices  38.2 us (35%)
  Pallas kernels  22.3 us (20%)
  local copies, waits for them, and re-layouts  3.81 us (3%)
    pallas_call x11, Pallas kernels, call(): pl.pallas_call(body, grid_spec=pltpu.PrefetchScalarGridSpec(num_scalar_pr...  21.1 us
    ppermute x8, starting transfers between devices, on_device(): send = lambda v, d: lax.ppermute(v, 'head', z_route(d))  14 us
    ppermute x8, waiting for transfers between devices, on_device(): send = lambda v, d: lax.ppermute(v, 'head', z_route(d))  10.7 us
    ppermute x2, waiting for transfers between devices, on_device(): lax.ppermute(normed, 'head', y_route(d))  9.94 us
    ppermute x3, starting transfers between devices, on_device(): more = [lax.ppermute(ss, 'head', quad_route(d)) for d in range(1, QUAD)]  6.21 us
    ppermute x1, waiting for transfers between devices, on_device(): far_low = lax.ppermute(near_up[:mid], 'head', y_route(1))  6.11 us
    ppermute x3, waiting for transfers between devices, on_device(): befores = [lax.ppermute(chip, 'seq', x_route(d)) for d in (1, 2, 3)]  6.1 us
    all_to_all x1, starting transfers between devices, on_device(): lax.all_to_all(ahead, 'head', 0, 0, tiled=True, axis_index_groups=columns)  4.61 us
  transfers between devices with their start and end apart: 27, of which 14 were waited for; matrix products, arithmetic and copies ran while one was open for 0% of the time, Pallas kernels for 19%

profile of v4, /device:TPU:4, one launch (start us, length us, event | category | flops | bytes accessed | tf_op | source)
XLA Modules:
  0.0 107.9 jit_solution(8290857004081005636)
XLA Ops:
  1.4 1.9 %collective-permute-start = (bf16[16,1024]{1,0:T(8,128)(2,1)S(1)}, bf16[16,1024]{1,0:T(8,128)(2,1)S(1)}, u32[]{:S(2)}, u32[]{:S(2)}) collective-permute-start(bf16[16,1024]{1,0:T(8,128)(2,1)S(1)} %pad_maximum_fusion.2), channel_id=1, source_target_pairs={{0,32},{32,64},{64,96},{96,128},{128,160},{160,192},{192,224},{1,3... | collective-permute-start | bytes 98312 | tf_op jit(solution)/shard_map/ppermute | solution.py:291
  3.5 2.2 %shard_map.91 = bf16[4,8,128,256]{3,2,1,0:T(8,128)(2,1)S(1)} custom-call(s32[5]{0:T(128)S(1)} %stack.23.at_ref, bf16[512,8192]{1,0:T(8,128)(2,1)} %w_ref.1, bf16[512,8192]{1,0:T(8,128)(2,1)} %w_ref.1, bf16[512,8192]{1,0:T(8,128)(2,1)} %w_ref.1, bf16[512,8192]{1,0:T(8,128)(2,1)} %w_ref.1), custom_call_target="tpu_custom_call" | custom-call | bytes 35651584 | tf_op jit(solution)/shard_map/pallas_call | solution.py:267
  5.7 1.4 %copy-done = bf16[4,8,128,256]{3,2,1,0:T(8,128)(2,1)} copy-done((bf16[4,8,128,256]{3,2,1,0:T(8,128)(2,1)}, bf16[4,8,128,256]{3,2,1,0:T(8,128)(2,1)S(1)}, u32[]{:S(2)}) %copy-start) | copy-done | bytes 2097176
  7.1 4.6 %all-to-all-start = ((bf16[4,8,128,256]{3,2,1,0:T(8,128)(2,1)}), bf16[4,8,128,256]{3,2,1,0:T(8,128)(2,1)S(1)}, u32[]{:S(2)}, u32[]{:S(2)}) async-start(bf16[4,8,128,256]{3,2,1,0:T(8,128)(2,1)} %copy-done), calls=%async_computation | async-start | bytes 4194304 | tf_op jit(solution)/shard_map/all_to_all | solution.py:309
  11.8 4.5 %shard_map.92 = (bf16[272,512]{1,0:T(8,128)(2,1)S(1)}, bf16[512,512]{1,0:T(8,128)(2,1)S(1)}, bf16[512,512]{1,0:T(8,128)(2,1)S(1)}, bf16[256,512]{1,0:T(8,128)(2,...) custom-call(s32[5]{0:T(128)S(1)} %stack.23.at_ref, bf16[512,512]{1,0:T(8,128)(2,1)S(1)} %copy-done.1, ...), custom_call_target="tpu_custom_call" | custom-call | bytes 6426656 | tf_op jit(solution)/shard_map/pallas_call | solution.py:267
  19.1 2.5 %collective-permute-start.2 = (bf16[272,256]{1,0:T(8,128)(2,1)S(1)}, bf16[272,256]{1,0:T(8,128)(2,1)S(1)}, u32[]{:S(2)}, u32[]{:S(2)}) collective-permute-start(bf16[272,256]{1,0:T(8,128)(2,1)S(1)} %shard_map.93), channel_id=1, source_target_pairs={{0,64},{32,96},{64,128},{96,160},{128,192},{160,224},{1,65},{33,97... | collective-permute-start | bytes 417800 | tf_op jit(solution)/shard_map/ppermute | solution.py:330
  21.6 1.3 %collective-permute-start.3 = (bf16[272,256]{1,0:T(8,128)(2,1)S(1)}, bf16[272,256]{1,0:T(8,128)(2,1)S(1)}, u32[]{:S(2)}, u32[]{:S(2)}) collective-permute-start(bf16[272,256]{1,0:T(8,128)(2,1)S(1)} %shard_map.93), channel_id=1, source_target_pairs={{0,128},{32,160},{64,192},{96,224},{1,129},{33,161},{65,193},{97,2... | collective-permute-start | bytes 417800 | tf_op jit(solution)/shard_map/ppermute | solution.py:330
  24.3 2.6 %collective-permute-done.2.one_ref = bf16[272,256]{1,0:T(8,128)(2,1)S(1)} collective-permute-done((bf16[272,256]{1,0:T(8,128)(2,1)S(1)}, bf16[272,256]{1,0:T(8,128)(2,1)S(1)}, u32[]{:S(2)}, u32[]{:S(2)}) %collective-permute-start.2) | collective-permute-done | bytes 139296 | tf_op jit(solution)/shard_map/ppermute | solution.py:330
  27.0 3.5 %collective-permute-done.3.two_ref = bf16[272,256]{1,0:T(8,128)(2,1)S(1)} collective-permute-done((bf16[272,256]{1,0:T(8,128)(2,1)S(1)}, bf16[272,256]{1,0:T(8,128)(2,1)S(1)}, u32[]{:S(2)}, u32[]{:S(2)}) %collective-permute-start.3) | collective-permute-done | bytes 139296 | tf_op jit(solution)/shard_map/ppermute | solution.py:330
  30.6 1.3 %collective-permute-done.5.theirs_ref = bf16[256,256]{1,0:T(8,128)(2,1)S(1)} collective-permute-done((bf16[256,256]{1,0:T(8,128)(2,1)S(1)}, bf16[256,256]{1,0:T(8,128)(2,1)S(1)}, u32[]{:S(2)}, u32[]{:S(2)}) %collective-permute-start.5) | collective-permute-done | bytes 131104 | tf_op jit(solution)/shard_map/ppermute | solution.py:340
  33.2 1.9 %collective-permute-start.6 = (f32[8,512]{1,0:T(8,128)S(1)}, f32[8,512]{1,0:T(8,128)S(1)}, u32[]{:S(2)}, u32[]{:S(2)}) collective-permute-start(f32[8,512]{1,0:T(8,128)S(1)} %get-tuple-element.58.s0_ref), channel_id=1, source_target_pairs={{0,1},{1,2},{2,3},{3,0},{4,5},{5,6},{6,7},{7,4},{8,9},{9,10},{10,1... | collective-permute-start | bytes 49160 | tf_op jit(solution)/shard_map/ppermute | solution.py:348
  35.1 3.3 %collective-permute-start.7 = (f32[8,512]{1,0:T(8,128)S(1)}, f32[8,512]{1,0:T(8,128)S(1)}, u32[]{:S(2)}, u32[]{:S(2)}) collective-permute-start(f32[8,512]{1,0:T(8,128)S(1)} %get-tuple-element.58.s0_ref), channel_id=1, source_target_pairs={{0,2},{1,3},{2,0},{3,1},{4,6},{5,7},{6,4},{7,5},{8,10},{9,11},{10,... | collective-permute-start | bytes 49160 | tf_op jit(solution)/shard_map/ppermute | solution.py:348
  40.2 3.0 %collective-permute-start.13 = (bf16[3,8,64,256]{3,2,1,0:T(8,128)(2,1)S(1)}, bf16[3,8,64,256]{3,2,1,0:T(8,128)(2,1)S(1)}, u32[]{:S(2)}, u32[]{:S(2)}) collective-permute-start(bf16[3,8,64,256]{3,2,1,0:T(8,128)(2,1)S(1)} %get-tuple-element.57), channel_id=1, source_target_pairs={{0,64},{32,96},{64,128},{96,160},{128,192},{160,224},{192,0},{224,... | collective-permute-start | bytes 2359304 | tf_op jit(solution)/shard_map/ppermute | solution.py:362
  43.6 1.8 %collective-permute-start.9 = (bf16[512,512]{1,0:T(8,128)(2,1)S(1)}, bf16[512,512]{1,0:T(8,128)(2,1)S(1)}, u32[]{:S(2)}, u32[]{:S(2)}) collective-permute-start(bf16[512,512]{1,0:T(8,128)(2,1)S(1)} %shard_map.98.n0_ref), channel_id=1, source_target_pairs={{0,8},{1,9},{2,10},{3,11},{4,12},{5,13},{6,14},{7,15},{8,16},{9,17... | collective-permute-start | bytes 1572872 | tf_op jit(solution)/shard_map/ppermute | solution.py:372
  45.4 1.5 %collective-permute-start.11 = (bf16[512,512]{1,0:T(8,128)(2,1)S(1)}, bf16[512,512]{1,0:T(8,128)(2,1)S(1)}, u32[]{:S(2)}, u32[]{:S(2)}) collective-permute-start(bf16[512,512]{1,0:T(8,128)(2,1)S(1)} %shard_map.98.n0_ref), channel_id=1, source_target_pairs={{0,24},{1,25},{2,26},{3,27},{4,28},{5,29},{6,30},{7,31},{8,0},{9,1... | collective-permute-start | bytes 1572872 | tf_op jit(solution)/shard_map/ppermute | solution.py:372
  46.9 2.3 %shard_map.99.w0_ref = bf16[8,512,256]{2,1,0:T(8,128)(2,1)S(1)} custom-call(s32[5]{0:T(128)S(1)} %stack.23.at_ref, bf16[512,8192]{1,0:T(8,128)(2,1)} %w_ref.1), custom_call_target="tpu_custom_call" | custom-call | bytes 10485760 | tf_op jit(solution)/shard_map/pallas_call | solution.py:267
  49.2 9.9 %collective-permute-done.9.n1_ref = bf16[512,512]{1,0:T(8,128)(2,1)S(1)} collective-permute-done((bf16[512,512]{1,0:T(8,128)(2,1)S(1)}, bf16[512,512]{1,0:T(8,128)(2,1)S(1)}, u32[]{:S(2)}, u32[]{:S(2)}) %collective-permute-start.9) | collective-permute-done | bytes 524320 | tf_op jit(solution)/shard_map/ppermute | solution.py:372
  59.8 1.8 %collective-permute-done.14.refs_3_ = bf16[3,8,64,256]{3,2,1,0:T(8,128)(2,1)S(1)} collective-permute-done((bf16[3,8,64,256]{3,2,1,0:T(8,128)(2,1)S(1)}, bf16[3,8,64,256]{3,2,1,0:T(8,128)(2,1)S(1)}, u32[]{:S(2)}, u32[]{:S(2)}) %collective-permute-start.14) | collective-permute-done | bytes 786464 | tf_op jit(solution)/shard_map/ppermute | solution.py:363
  62.1 1.8 %collective-permute-start.10 = (bf16[256,512]{1,0:T(8,128)(2,1)S(1)}, bf16[256,512]{1,0:T(8,128)(2,1)S(1)}, u32[]{:S(2)}, u32[]{:S(2)}) collective-permute-start(bf16[256,512]{1,0:T(8,128)(2,1)S(1)} %slice.44), channel_id=1, source_target_pairs={{0,8},{1,9},{2,10},{3,11},{4,12},{5,13},{6,14},{7,15},{8,16},{9,17... | collective-permute-start | bytes 786440 | tf_op jit(solution)/shard_map/ppermute | solution.py:373
  64.0 1.5 %collective-permute-start.12 = (bf16[256,512]{1,0:T(8,128)(2,1)S(1)}, bf16[256,512]{1,0:T(8,128)(2,1)S(1)}, u32[]{:S(2)}, u32[]{:S(2)}) collective-permute-start(bf16[256,512]{1,0:T(8,128)(2,1)S(1)} %slice.45), channel_id=1, source_target_pairs={{0,24},{1,25},{2,26},{3,27},{4,28},{5,29},{6,30},{7,31},{8,0},{9,1... | collective-permute-start | bytes 786440 | tf_op jit(solution)/shard_map/ppermute | solution.py:374
  65.6 6.1 %collective-permute-done.10.low_ref = bf16[256,512]{1,0:T(8,128)(2,1)S(1)} collective-permute-done((bf16[256,512]{1,0:T(8,128)(2,1)S(1)}, bf16[256,512]{1,0:T(8,128)(2,1)S(1)}, u32[]{:S(2)}, u32[]{:S(2)}) %collective-permute-start.10) | collective-permute-done | bytes 262176 | tf_op jit(solution)/shard_map/ppermute | solution.py:373
  74.4 2.8 %collective-permute-start.19 = (bf16[256,256]{1,0:T(8,128)(2,1)S(1)}, bf16[256,256]{1,0:T(8,128)(2,1)S(1)}, u32[]{:S(2)}, u32[]{:S(2)}) collective-permute-start(bf16[256,256]{1,0:T(8,128)(2,1)S(1)} %get-tuple-element.67), channel_id=1, source_target_pairs={{0,7},{1,0},{2,1},{3,2},{4,3},{5,4},{6,5},{7,6},{8,15},{9,8},{10,9... | collective-permute-start | bytes 393224 | tf_op jit(solution)/shard_map/ppermute | solution.py:417
  77.3 2.4 %shard_map.102 = bf16[2,512,256]{2,1,0:T(8,128)(2,1)S(1)} custom-call(s32[5]{0:T(128)S(1)} %stack.23.at_ref, bf16[512,512]{1,0:T(8,128)(2,1)S(1)} %shard_map.98.n0_ref, bf16[512,512]{1,0:T(8,128)(2,1)S(1)} %collective-permute-done.9.n1_ref, bf16[256,512]{1,0:T(8,128)(2,1)S(1)} %collective-permute-done.10.low_ref, ...), custom_call_target="tpu_custom_call" | custom-call | flops 1073741824 | bytes 11010048 | tf_op jit(solution)/shard_map/pallas_call | solution.py:267
  80.3 3.3 %collective-permute-start.22 = (bf16[512,256]{1,0:T(8,128)(2,1)S(1)}, bf16[512,256]{1,0:T(8,128)(2,1)S(1)}, u32[]{:S(2)}, u32[]{:S(2)}) collective-permute-start(bf16[512,256]{1,0:T(8,128)(2,1)S(1)} %pad_maximum_fusion.1), channel_id=1, source_target_pairs={{0,7},{1,0},{2,1},{3,2},{4,3},{5,4},{6,5},{7,6},{8,15},{9,8},{10,9... | collective-permute-start | bytes 786440 | tf_op jit(solution)/shard_map/ppermute | solution.py:417
  83.6 2.4 %shard_map.101 = bf16[2,512,256]{2,1,0:T(8,128)(2,1)S(1)} custom-call(s32[5]{0:T(128)S(1)} %stack.23.at_ref, bf16[512,512]{1,0:T(8,128)(2,1)S(1)} %shard_map.98.n0_ref, bf16[512,512]{1,0:T(8,128)(2,1)S(1)} %collective-permute-done.9.n1_ref, bf16[256,512]{1,0:T(8,128)(2,1)S(1)} %collective-permute-done.10.low_ref, ...), custom_call_target="tpu_custom_call" | custom-call | flops 1073741824 | bytes 11010048 | tf_op jit(solution)/shard_map/pallas_call | solution.py:267
  86.0 2.1 %collective-permute-done.20 = bf16[512,256]{1,0:T(8,128)(2,1)S(1)} collective-permute-done((bf16[512,256]{1,0:T(8,128)(2,1)S(1)}, bf16[512,256]{1,0:T(8,128)(2,1)S(1)}, u32[]{:S(2)}, u32[]{:S(2)}) %collective-permute-start.20) | collective-permute-done | bytes 262176 | tf_op jit(solution)/shard_map/ppermute | solution.py:417
  88.3 3.3 %collective-permute-start.23 = (bf16[512,256]{1,0:T(8,128)(2,1)S(1)}, bf16[512,256]{1,0:T(8,128)(2,1)S(1)}, u32[]{:S(2)}, u32[]{:S(2)}) collective-permute-start(bf16[512,256]{1,0:T(8,128)(2,1)S(1)} %fusion.2), channel_id=1, source_target_pairs={{0,7},{1,0},{2,1},{3,2},{4,3},{5,4},{6,5},{7,6},{8,15},{9,8},{10,9... | collective-permute-start | bytes 786440 | tf_op jit(solution)/shard_map/ppermute | solution.py:417
  91.6 2.4 %shard_map.104 = bf16[2,512,256]{2,1,0:T(8,128)(2,1)S(1)} custom-call(s32[5]{0:T(128)S(1)} %stack.23.at_ref, bf16[512,512]{1,0:T(8,128)(2,1)S(1)} %shard_map.98.n0_ref, bf16[512,512]{1,0:T(8,128)(2,1)S(1)} %collective-permute-done.9.n1_ref, bf16[256,512]{1,0:T(8,128)(2,1)S(1)} %collective-permute-done.10.low_ref, ...), custom_call_target="tpu_custom_call" | custom-call | flops 1073741824 | bytes 11010048 | tf_op jit(solution)/shard_map/pallas_call | solution.py:267
  94.0 1.8 %collective-permute-done.21 = bf16[512,256]{1,0:T(8,128)(2,1)S(1)} collective-permute-done((bf16[512,256]{1,0:T(8,128)(2,1)S(1)}, bf16[512,256]{1,0:T(8,128)(2,1)S(1)}, u32[]{:S(2)}, u32[]{:S(2)}) %collective-permute-start.21) | collective-permute-done | bytes 262176 | tf_op jit(solution)/shard_map/ppermute | solution.py:417
  96.0 3.4 %collective-permute-start.25 = (bf16[512,256]{1,0:T(8,128)(2,1)S(1)}, bf16[512,256]{1,0:T(8,128)(2,1)S(1)}, u32[]{:S(2)}, u32[]{:S(2)}) collective-permute-start(bf16[512,256]{1,0:T(8,128)(2,1)S(1)} %fusion), channel_id=1, source_target_pairs={{0,7},{1,0},{2,1},{3,2},{4,3},{5,4},{6,5},{7,6},{8,15},{9,8},{10,9... | collective-permute-start | bytes 786440 | tf_op jit(solution)/shard_map/ppermute | solution.py:417
  100.6 2.6 %collective-permute-done.25 = bf16[512,256]{1,0:T(8,128)(2,1)S(1)} collective-permute-done((bf16[512,256]{1,0:T(8,128)(2,1)S(1)}, bf16[512,256]{1,0:T(8,128)(2,1)S(1)}, u32[]{:S(2)}, u32[]{:S(2)}) %collective-permute-start.25) | collective-permute-done | bytes 262176 | tf_op jit(solution)/shard_map/ppermute | solution.py:417
  103.2 3.7 %collective-permute-done.24 = bf16[512,256]{1,0:T(8,128)(2,1)S(1)} collective-permute-done((bf16[512,256]{1,0:T(8,128)(2,1)S(1)}, bf16[512,256]{1,0:T(8,128)(2,1)S(1)}, u32[]{:S(2)}, u32[]{:S(2)}) %collective-permute-start.24) | collective-permute-done | bytes 262176 | tf_op jit(solution)/shard_map/ppermute | solution.py:417
  (69 shorter events, 16.6 us)
Async XLA Ops:
  1.4 5.7 %collective-permute-start = (bf16[16,1024]{1,0:T(8,128)(2,1)S(1)}, bf16[16,1024]{1,0:T(8,128)(2,1)S(1)}, u32[]{:S(2)}, u32[]{:S(2)}) collective-permute-start(bf16[16,1024]{1,0:T(8,128)(2,1)S(1)} %pad_maximum_fusion.2), channel_id=1, source_target_pairs={{0,32},{32,64},{64,96},{96,128},{128,160},{160,192},{192,224},{1,3... | collective-permute-start | bytes 98312 | tf_op jit(solution)/shard_map/ppermute | solution.py:291
  7.1 4.6 %copy-start.4 = (f32[8,512]{1,0:T(8,128)S(1)}, f32[8,512]{1,0:T(8,128)}, u32[]{:S(2)}) copy-start(f32[8,512]{1,0:T(8,128)} %dt_ref.1) | copy-start | bytes 49156
  7.1 4.6 %copy-start.5 = (bf16[4,512]{1,0:T(4,128)(2,1)S(1)}, bf16[4,512]{1,0:T(4,128)(2,1)}, u32[]{:S(2)}) copy-start(bf16[4,512]{1,0:T(4,128)(2,1)} %wx_ref.1) | copy-start | bytes 12292
  7.1 4.7 %copy-start.7 = (f32[8]{0:T(128)S(1)}, f32[8]{0:T(128)}, u32[]{:S(2)}) copy-start(f32[8]{0:T(128)} %param.13) | copy-start | bytes 100
  7.1 32.3 %all-to-all-start = ((bf16[4,8,128,256]{3,2,1,0:T(8,128)(2,1)}), bf16[4,8,128,256]{3,2,1,0:T(8,128)(2,1)S(1)}, u32[]{:S(2)}, u32[]{:S(2)}) async-start(bf16[4,8,128,256]{3,2,1,0:T(8,128)(2,1)} %copy-done), calls=%async_computation | async-start | bytes 4194304 | tf_op jit(solution)/shard_map/all_to_all | solution.py:309
  11.7 11.8 %copy-start.2 = (bf16[512,512]{1,0:T(8,128)(2,1)S(1)}, bf16[512,512]{1,0:T(8,128)(2,1)}, u32[]{:S(2)}) copy-start(bf16[512,512]{1,0:T(8,128)(2,1)} %z_ref.1) | copy-start | bytes 1572868
  16.2 2.3 %collective-permute-start.1 = (bf16[272,512]{1,0:T(8,128)(2,1)S(1)}, bf16[272,512]{1,0:T(8,128)(2,1)S(1)}, u32[]{:S(2)}, u32[]{:S(2)}) collective-permute-start(bf16[272,512]{1,0:T(8,128)(2,1)S(1)} %get-tuple-element.43.own_ref), channel_id=1, source_target_pairs={{0,32},{32,0},{64,96},{96,64},{128,160},{160,128},{192,224},{224,1... | collective-permute-start | bytes 835592 | tf_op jit(solution)/shard_map/ppermute | solution.py:328
  19.1 7.8 %collective-permute-start.2 = (bf16[272,256]{1,0:T(8,128)(2,1)S(1)}, bf16[272,256]{1,0:T(8,128)(2,1)S(1)}, u32[]{:S(2)}, u32[]{:S(2)}) collective-permute-start(bf16[272,256]{1,0:T(8,128)(2,1)S(1)} %shard_map.93), channel_id=1, source_target_pairs={{0,64},{32,96},{64,128},{96,160},{128,192},{160,224},{1,65},{33,97... | collective-permute-start | bytes 417800 | tf_op jit(solution)/shard_map/ppermute | solution.py:330
  21.6 8.8 %collective-permute-start.3 = (bf16[272,256]{1,0:T(8,128)(2,1)S(1)}, bf16[272,256]{1,0:T(8,128)(2,1)S(1)}, u32[]{:S(2)}, u32[]{:S(2)}) collective-permute-start(bf16[272,256]{1,0:T(8,128)(2,1)S(1)} %shard_map.93), channel_id=1, source_target_pairs={{0,128},{32,160},{64,192},{96,224},{1,129},{33,161},{65,193},{97,2... | collective-permute-start | bytes 417800 | tf_op jit(solution)/shard_map/ppermute | solution.py:330
  22.9 7.5 %collective-permute-start.4 = (bf16[272,256]{1,0:T(8,128)(2,1)S(1)}, bf16[272,256]{1,0:T(8,128)(2,1)S(1)}, u32[]{:S(2)}, u32[]{:S(2)}) collective-permute-start(bf16[272,256]{1,0:T(8,128)(2,1)S(1)} %shard_map.93), channel_id=1, source_target_pairs={{0,192},{32,224},{1,193},{33,225},{2,194},{34,226},{3,195},{35,227... | collective-permute-start | bytes 417800 | tf_op jit(solution)/shard_map/ppermute | solution.py:330
  30.5 1.4 %collective-permute-start.5 = (bf16[256,256]{1,0:T(8,128)(2,1)S(1)}, bf16[256,256]{1,0:T(8,128)(2,1)S(1)}, u32[]{:S(2)}, u32[]{:S(2)}) collective-permute-start(bf16[256,256]{1,0:T(8,128)(2,1)S(1)} %shard_map.95.mine_ref), channel_id=1, source_target_pairs={{0,32},{32,0},{64,96},{96,64},{128,160},{160,128},{192,224},{224,1... | collective-permute-start | bytes 393224 | tf_op jit(solution)/shard_map/ppermute | solution.py:340
  33.2 10.0 %copy-start.6 = (f32[512]{0:T(512)S(1)}, f32[512]{0:T(512)}, u32[]{:S(2)}) copy-start(f32[512]{0:T(512)} %param.16) | copy-start | bytes 6148
  33.2 10.0 %collective-permute-start.6 = (f32[8,512]{1,0:T(8,128)S(1)}, f32[8,512]{1,0:T(8,128)S(1)}, u32[]{:S(2)}, u32[]{:S(2)}) collective-permute-start(f32[8,512]{1,0:T(8,128)S(1)} %get-tuple-element.58.s0_ref), channel_id=1, source_target_pairs={{0,1},{1,2},{2,3},{3,0},{4,5},{5,6},{6,7},{7,4},{8,9},{9,10},{10,1... | collective-permute-start | bytes 49160 | tf_op jit(solution)/shard_map/ppermute | solution.py:348
  35.1 8.0 %collective-permute-start.7 = (f32[8,512]{1,0:T(8,128)S(1)}, f32[8,512]{1,0:T(8,128)S(1)}, u32[]{:S(2)}, u32[]{:S(2)}) collective-permute-start(f32[8,512]{1,0:T(8,128)S(1)} %get-tuple-element.58.s0_ref), channel_id=1, source_target_pairs={{0,2},{1,3},{2,0},{3,1},{4,6},{5,7},{6,4},{7,5},{8,10},{9,11},{10,... | collective-permute-start | bytes 49160 | tf_op jit(solution)/shard_map/ppermute | solution.py:348
  38.4 4.8 %collective-permute-start.8 = (f32[8,512]{1,0:T(8,128)S(1)}, f32[8,512]{1,0:T(8,128)S(1)}, u32[]{:S(2)}, u32[]{:S(2)}) collective-permute-start(f32[8,512]{1,0:T(8,128)S(1)} %get-tuple-element.58.s0_ref), channel_id=1, source_target_pairs={{0,3},{1,0},{2,1},{3,2},{4,7},{5,4},{6,5},{7,6},{8,11},{9,8},{10,9... | collective-permute-start | bytes 49160 | tf_op jit(solution)/shard_map/ppermute | solution.py:348
  40.2 19.6 %collective-permute-start.13 = (bf16[3,8,64,256]{3,2,1,0:T(8,128)(2,1)S(1)}, bf16[3,8,64,256]{3,2,1,0:T(8,128)(2,1)S(1)}, u32[]{:S(2)}, u32[]{:S(2)}) collective-permute-start(bf16[3,8,64,256]{3,2,1,0:T(8,128)(2,1)S(1)} %get-tuple-element.57), channel_id=1, source_target_pairs={{0,64},{32,96},{64,128},{96,160},{128,192},{160,224},{192,0},{224,... | collective-permute-start | bytes 2359304 | tf_op jit(solution)/shard_map/ppermute | solution.py:362
  43.1 18.5 %collective-permute-start.14 = (bf16[3,8,64,256]{3,2,1,0:T(8,128)(2,1)S(1)}, bf16[3,8,64,256]{3,2,1,0:T(8,128)(2,1)S(1)}, u32[]{:S(2)}, u32[]{:S(2)}) collective-permute-start(bf16[3,8,64,256]{3,2,1,0:T(8,128)(2,1)S(1)} %get-tuple-element.60), channel_id=1, source_target_pairs={{0,192},{32,224},{64,0},{96,32},{128,64},{160,96},{192,128},{224,1... | collective-permute-start | bytes 2359304 | tf_op jit(solution)/shard_map/ppermute | solution.py:363
  43.5 28.5 %collective-permute-start.15 = (bf16[3,8,128,256]{3,2,1,0:T(8,128)(2,1)S(1)}, bf16[3,8,128,256]{3,2,1,0:T(8,128)(2,1)S(1)}, u32[]{:S(2)}, u32[]{:S(2)}) collective-permute-start(bf16[3,8,128,256]{3,2,1,0:T(8,128)(2,1)S(1)} %get-tuple-element.63.refs_0_), channel_id=1, source_target_pairs={{0,32},{32,0},{64,96},{96,64},{128,160},{160,128},{192,224},{224,1... | collective-permute-start | bytes 4718600 | tf_op jit(solution)/shard_map/ppermute | solution.py:387
  43.6 15.6 %collective-permute-start.9 = (bf16[512,512]{1,0:T(8,128)(2,1)S(1)}, bf16[512,512]{1,0:T(8,128)(2,1)S(1)}, u32[]{:S(2)}, u32[]{:S(2)}) collective-permute-start(bf16[512,512]{1,0:T(8,128)(2,1)S(1)} %shard_map.98.n0_ref), channel_id=1, source_target_pairs={{0,8},{1,9},{2,10},{3,11},{4,12},{5,13},{6,14},{7,15},{8,16},{9,17... | collective-permute-start | bytes 1572872 | tf_op jit(solution)/shard_map/ppermute | solution.py:372
  45.4 18.6 %collective-permute-start.11 = (bf16[512,512]{1,0:T(8,128)(2,1)S(1)}, bf16[512,512]{1,0:T(8,128)(2,1)S(1)}, u32[]{:S(2)}, u32[]{:S(2)}) collective-permute-start(bf16[512,512]{1,0:T(8,128)(2,1)S(1)} %shard_map.98.n0_ref), channel_id=1, source_target_pairs={{0,24},{1,25},{2,26},{3,27},{4,28},{5,29},{6,30},{7,31},{8,0},{9,1... | collective-permute-start | bytes 1572872 | tf_op jit(solution)/shard_map/ppermute | solution.py:372
  61.6 10.4 %collective-permute-start.16 = (bf16[3,8,64,256]{3,2,1,0:T(8,128)(2,1)S(1)}, bf16[3,8,64,256]{3,2,1,0:T(8,128)(2,1)S(1)}, u32[]{:S(2)}, u32[]{:S(2)}) collective-permute-start(bf16[3,8,64,256]{3,2,1,0:T(8,128)(2,1)S(1)} %collective-permute-done.13.refs_2_), channel_id=1, source_target_pairs={{0,32},{32,0},{64,96},{96,64},{128,160},{160,128},{192,224},{224,1... | collective-permute-start | bytes 2359304 | tf_op jit(solution)/shard_map/ppermute | solution.py:387
  61.6 10.4 %collective-permute-start.17 = (bf16[3,8,64,256]{3,2,1,0:T(8,128)(2,1)S(1)}, bf16[3,8,64,256]{3,2,1,0:T(8,128)(2,1)S(1)}, u32[]{:S(2)}, u32[]{:S(2)}) collective-permute-start(bf16[3,8,64,256]{3,2,1,0:T(8,128)(2,1)S(1)} %collective-permute-done.14.refs_3_), channel_id=1, source_target_pairs={{0,32},{32,0},{64,96},{96,64},{128,160},{160,128},{192,224},{224,1... | collective-permute-start | bytes 2359304 | tf_op jit(solution)/shard_map/ppermute | solution.py:387
  62.1 9.5 %collective-permute-start.10 = (bf16[256,512]{1,0:T(8,128)(2,1)S(1)}, bf16[256,512]{1,0:T(8,128)(2,1)S(1)}, u32[]{:S(2)}, u32[]{:S(2)}) collective-permute-start(bf16[256,512]{1,0:T(8,128)(2,1)S(1)} %slice.44), channel_id=1, source_target_pairs={{0,8},{1,9},{2,10},{3,11},{4,12},{5,13},{6,14},{7,15},{8,16},{9,17... | collective-permute-start | bytes 786440 | tf_op jit(solution)/shard_map/ppermute | solution.py:373
  64.0 8.0 %collective-permute-start.12 = (bf16[256,512]{1,0:T(8,128)(2,1)S(1)}, bf16[256,512]{1,0:T(8,128)(2,1)S(1)}, u32[]{:S(2)}, u32[]{:S(2)}) collective-permute-start(bf16[256,512]{1,0:T(8,128)(2,1)S(1)} %slice.45), channel_id=1, source_target_pairs={{0,24},{1,25},{2,26},{3,27},{4,28},{5,29},{6,30},{7,31},{8,0},{9,1... | collective-permute-start | bytes 786440 | tf_op jit(solution)/shard_map/ppermute | solution.py:374
  73.3 6.8 %collective-permute-start.18 = (bf16[256,256]{1,0:T(8,128)(2,1)S(1)}, bf16[256,256]{1,0:T(8,128)(2,1)S(1)}, u32[]{:S(2)}, u32[]{:S(2)}) collective-permute-start(bf16[256,256]{1,0:T(8,128)(2,1)S(1)} %get-tuple-element.66), channel_id=1, source_target_pairs={{0,1},{1,2},{2,3},{3,4},{4,5},{5,6},{6,7},{7,0},{8,9},{9,10},{10,1... | collective-permute-start | bytes 393224 | tf_op jit(solution)/shard_map/ppermute | solution.py:417
  74.4 5.8 %collective-permute-start.19 = (bf16[256,256]{1,0:T(8,128)(2,1)S(1)}, bf16[256,256]{1,0:T(8,128)(2,1)S(1)}, u32[]{:S(2)}, u32[]{:S(2)}) collective-permute-start(bf16[256,256]{1,0:T(8,128)(2,1)S(1)} %get-tuple-element.67), channel_id=1, source_target_pairs={{0,7},{1,0},{2,1},{3,2},{4,3},{5,4},{6,5},{7,6},{8,15},{9,8},{10,9... | collective-permute-start | bytes 393224 | tf_op jit(solution)/shard_map/ppermute | solution.py:417
  80.2 7.9 %collective-permute-start.20 = (bf16[512,256]{1,0:T(8,128)(2,1)S(1)}, bf16[512,256]{1,0:T(8,128)(2,1)S(1)}, u32[]{:S(2)}, u32[]{:S(2)}) collective-permute-start(bf16[512,256]{1,0:T(8,128)(2,1)S(1)} %pad_maximum_fusion), channel_id=1, source_target_pairs={{0,1},{1,2},{2,3},{3,4},{4,5},{5,6},{6,7},{7,0},{8,9},{9,10},{10,1... | collective-permute-start | bytes 786440 | tf_op jit(solution)/shard_map/ppermute | solution.py:417
  80.3 7.9 %collective-permute-start.22 = (bf16[512,256]{1,0:T(8,128)(2,1)S(1)}, bf16[512,256]{1,0:T(8,128)(2,1)S(1)}, u32[]{:S(2)}, u32[]{:S(2)}) collective-permute-start(bf16[512,256]{1,0:T(8,128)(2,1)S(1)} %pad_maximum_fusion.1), channel_id=1, source_target_pairs={{0,7},{1,0},{2,1},{3,2},{4,3},{5,4},{6,5},{7,6},{8,15},{9,8},{10,9... | collective-permute-start | bytes 786440 | tf_op jit(solution)/shard_map/ppermute | solution.py:417
  88.2 7.7 %collective-permute-start.21 = (bf16[512,256]{1,0:T(8,128)(2,1)S(1)}, bf16[512,256]{1,0:T(8,128)(2,1)S(1)}, u32[]{:S(2)}, u32[]{:S(2)}) collective-permute-start(bf16[512,256]{1,0:T(8,128)(2,1)S(1)} %fusion.3), channel_id=1, source_target_pairs={{0,1},{1,2},{2,3},{3,4},{4,5},{5,6},{6,7},{7,0},{8,9},{9,10},{10,1... | collective-permute-start | bytes 786440 | tf_op jit(solution)/shard_map/ppermute | solution.py:417
  88.3 7.6 %collective-permute-start.23 = (bf16[512,256]{1,0:T(8,128)(2,1)S(1)}, bf16[512,256]{1,0:T(8,128)(2,1)S(1)}, u32[]{:S(2)}, u32[]{:S(2)}) collective-permute-start(bf16[512,256]{1,0:T(8,128)(2,1)S(1)} %fusion.2), channel_id=1, source_target_pairs={{0,7},{1,0},{2,1},{3,2},{4,3},{5,4},{6,5},{7,6},{8,15},{9,8},{10,9... | collective-permute-start | bytes 786440 | tf_op jit(solution)/shard_map/ppermute | solution.py:417
  96.0 7.3 %collective-permute-start.25 = (bf16[512,256]{1,0:T(8,128)(2,1)S(1)}, bf16[512,256]{1,0:T(8,128)(2,1)S(1)}, u32[]{:S(2)}, u32[]{:S(2)}) collective-permute-start(bf16[512,256]{1,0:T(8,128)(2,1)S(1)} %fusion), channel_id=1, source_target_pairs={{0,7},{1,0},{2,1},{3,2},{4,3},{5,4},{6,5},{7,6},{8,15},{9,8},{10,9... | collective-permute-start | bytes 786440 | tf_op jit(solution)/shard_map/ppermute | solution.py:417
  99.3 7.6 %collective-permute-start.24 = (bf16[512,256]{1,0:T(8,128)(2,1)S(1)}, bf16[512,256]{1,0:T(8,128)(2,1)S(1)}, u32[]{:S(2)}, u32[]{:S(2)}) collective-permute-start(bf16[512,256]{1,0:T(8,128)(2,1)S(1)} %fusion.1), channel_id=1, source_target_pairs={{0,1},{1,2},{2,3},{3,4},{4,5},{5,6},{6,7},{7,0},{8,9},{9,10},{10,1... | collective-permute-start | bytes 786440 | tf_op jit(solution)/shard_map/ppermute | solution.py:417
  (3 other events, 10.7 us)
